TPU v7x, 512 devices: a whole 4x4x16 slice. The times are simulated.
512 devices in a mesh: depth: 8 (over z_lo), plan: 64 (over x, y, z_hi, core).
Axes of the slice: x: 4, y: 4, z: 16 (z_hi: 2, z_lo: 8; z = z_hi * 8 + z_lo), core: 2. Of those that a mesh axis runs over, the one named last changes fastest.
Arguments:
- level_set: float32 [16, 1024, 1024], P('depth', 'plan'), may hold values from -4.6 to 4.6
- contrast: float32 [16], P('depth'), may hold values from -2 to 2
Outputs:
- gravity: float32 [1024, 1024], P('plan', 'depth')
All inputs are finite; a program needn't handle non-finite values.
Results may differ from a plain program's by a relative error of at most 0.00012.
Values sent between devices are 32-bit elements; how exact they have to be, the bound alone decides.
A program may use at most 64 MiB of HBM per device.

v0:
```python
import functools
import math

import jax
import jax.numpy as jnp
import ml_dtypes
import numpy as np
from jax import lax
from jax.experimental import pallas as pl
from jax.experimental.pallas import tpu as pltpu
from jax.sharding import PartitionSpec as P

MESH = pl.DeviceIdType.MESH
F32 = jnp.float32
BF16 = jnp.bfloat16

NX = 1024
HALF = NX // 2
LAYERS = 16
DEPTH = 8
PLAN = 64
ROWS = NX // PLAN
GROUP = 32
RING = 16
COEF = 2 * NX // GROUP

bend_weight = 0.5
grav_scale = 0.05
top_depth = 0.0
thickness = 1.0


def basis():
    j = np.arange(HALF, dtype=np.float64)[:, None] + 0.5
    v = np.arange(NX, dtype=np.float64)[None, :]
    v_sin = np.where(v == 0, float(NX), v)
    both = np.stack([np.cos(np.pi * v * j / NX), np.sin(np.pi * v_sin * j / NX)])
    high = both.astype(ml_dtypes.bfloat16)
    low = (both - high.astype(np.float64)).astype(ml_dtypes.bfloat16)
    wide = np.stack([high, low], axis=1)
    return wide, np.ascontiguousarray(np.swapaxes(wide, 2, 3))


def flux(step):
    return step * lax.rsqrt(1.0 + step * step)


def flip(value, axis, size):
    index = lax.broadcasted_iota(jnp.int32, value.shape, axis)
    step = size // 2
    value = pltpu.roll(value, step, axis)
    while step > 1:
        step //= 2
        up = pltpu.roll(value, step, axis)
        down = pltpu.roll(value, size - step, axis)
        value = jnp.where((index & step) != 0, up, down)
    return value


def flip_lanes(value):
    blocks = value.shape[1] // 128
    parts = [flip(value[:, 128 * k : 128 * (k + 1)], 1, 128) for k in reversed(range(blocks))]
    return jnp.concatenate(parts, axis=1) if blocks > 1 else parts[0]


def split(value):
    high = value.astype(BF16)
    low = (value - high.astype(F32)).astype(BF16)
    return high, low


def matmul(a, b):
    return jnp.dot(a, b, preferred_element_type=F32)


def table_right(value, high_table, low_table):
    n = value.shape[0]
    high, low = split(value)
    both = matmul(jnp.concatenate([high, low], axis=0), high_table)
    return both[:n] + both[n:] + matmul(high, low_table)


def kernel(
    ls_hbm, con_hbm, wide_hbm, tall_hbm, out_ref,
    ls_ref, con_ref, wide, tall, zhalo, rsend, rhalo, csend, sbuf, sst, rsp, rsp_first, pst, phi, xsend, cbuf, gsend, gbuf,
    ls_sem, con_sem, wide_sem, tall_sem, hs, hr, cs, cr, xs, xr, gs, gr,
):
    d = lax.axis_index("depth")
    p = lax.axis_index("plan")
    core = p % 2
    zh = (p // 2) % 2
    q = (p // 4) * 2 + core
    z = zh * DEPTH + d
    lower = p < PLAN // 2

    def at_q(other):
        return (d, (other // 2) * 4 + zh * 2 + other % 2)

    def at_z(other):
        return (other % DEPTH, (q // 2) * 4 + (other // DEPTH) * 2 + core)

    ls_copy = pltpu.make_async_copy(ls_hbm, ls_ref, ls_sem)
    con_copy = pltpu.make_async_copy(con_hbm, con_ref, con_sem)
    ls_copy.start()
    con_copy.start()
    wide_copy = pltpu.make_async_copy(wide_hbm, wide, wide_sem)
    tall_copy = pltpu.make_async_copy(tall_hbm, tall, tall_sem)
    wide_copy.start()
    tall_copy.start()

    barrier = pltpu.get_barrier_semaphore()

    def greet(target):
        pl.semaphore_signal(barrier, inc=1, device_id=target, device_id_type=MESH)

    @pl.loop(1, GROUP)
    def _(k):
        greet(at_q((q + k) % GROUP))

    @pl.loop(1, RING)
    def _(k):
        greet(at_z((z + k) % RING))

    outer = jnp.where(core == 0, p - 1, p + 1)

    has_outer = (outer >= 0) & (outer < PLAN)

    @pl.when(has_outer)
    def _():
        greet((d, outer))

    ls_copy.wait()
    con_copy.wait()

    for layer in range(2):
        for k in range(8):
            spot = layer * 8 + k
            rsend[0, spot : spot + 1, :] = ls_ref[layer, 0:1, 128 * k : 128 * (k + 1)]
            rsend[1, spot : spot + 1, :] = ls_ref[layer, ROWS - 1 : ROWS, 128 * k : 128 * (k + 1)]

    pl.semaphore_wait(barrier, GROUP + RING - 2 + has_outer.astype(jnp.int32))

    def halo(source, target, number, device):
        return pltpu.make_async_remote_copy(
            src_ref=source, dst_ref=target, send_sem=hs.at[number], recv_sem=hr.at[number],
            device_id=device, device_id_type=MESH,
        )

    z_up = halo(ls_ref.at[1], zhalo.at[0], 0, (d + 1, p))
    z_down = halo(ls_ref.at[0], zhalo.at[1], 1, (d - 1, p))
    r_up = halo(rsend.at[1], rhalo.at[0], 2, (d, p + 1))
    r_down = halo(rsend.at[0], rhalo.at[1], 3, (d, p - 1))
    has = (d < DEPTH - 1, d > 0, p < PLAN - 1, p > 0)
    gets = (d > 0, d < DEPTH - 1, p > 0, p < PLAN - 1)
    lands = (zhalo.at[0], zhalo.at[1], rhalo.at[0], rhalo.at[1])
    copies = (z_up, z_down, r_up, r_down)
    for copy, there in zip(copies, has):
        pl.when(there)(copy.start)
    for land, comes in zip(lands, gets):

        @pl.when(jnp.logical_not(comes))
        def _(land=land):
            land[...] = jnp.zeros(land.shape, F32)

    for copy, comes in zip(copies, gets):
        pl.when(comes)(copy.wait_recv)
    row_id = lax.broadcasted_iota(jnp.int32, (ROWS, NX), 0)
    col_id = lax.broadcasted_iota(jnp.int32, (ROWS, NX), 1)
    field = [ls_ref[0], ls_ref[1]]
    z_flux = [flux(field[0] - zhalo[0]), flux(field[1] - field[0]), flux(zhalo[1] - field[1])]
    even, odd = [], []
    for layer in range(2):
        centre = field[layer]

        def row_of(side):
            parts = [
                jnp.broadcast_to(rhalo[side, layer * 8 + k : layer * 8 + k + 1, :], (ROWS, 128)) for k in range(8)
            ]
            return jnp.concatenate(parts, axis=1)

        bend = z_flux[layer + 1] - z_flux[layer]
        above = jnp.where(row_id == 0, row_of(0), pltpu.roll(centre, 1, 0))
        row_flux = flux(centre - above)
        last = flux(row_of(1) - centre)
        bend = bend + jnp.where(row_id == ROWS - 1, last, pltpu.roll(row_flux, ROWS - 1, 0)) - row_flux
        before = jnp.where(col_id == 0, 0.0, pltpu.roll(centre, 1, 1))
        col_flux = flux(centre - before)
        bend = bend + jnp.where(col_id == NX - 1, flux(-centre), pltpu.roll(col_flux, NX - 1, 1)) - col_flux
        density = con_ref[layer] * (0.5 * (1.0 + jnp.tanh(centre))) + bend_weight * bend
        density = jnp.where(lower, flip(density, 0, ROWS), density)
        left = flip_lanes(density[:, :HALF])
        right = density[:, HALF:]
        even.append(right + left)
        odd.append(right - left)

    block = jnp.where(lower, PLAN // 2 - 1 - p, p - PLAN // 2)
    half_lane = lax.broadcasted_iota(jnp.int32, (ROWS, 128), 1) < COEF
    wide_copy.wait()

    def send_coef(other):
        return pltpu.make_async_remote_copy(
            src_ref=csend.at[other], dst_ref=sbuf.at[block], send_sem=cs, recv_sem=cr,
            device_id=at_q(other), device_id_type=MESH,
        )

    for kind, pair in enumerate((even, odd)):
        coef = table_right(jnp.concatenate(pair, axis=0), wide[kind, 0], wide[kind, 1])
        for m in range(8):
            first = coef[:ROWS, 128 * m : 128 * (m + 1)]
            second = coef[ROWS:, 128 * m : 128 * (m + 1)]
            spot = kind * 16 + 2 * m
            csend[spot] = jnp.where(half_lane, first, pltpu.roll(second, COEF, 1))
            csend[spot + 1] = jnp.where(half_lane, pltpu.roll(first, COEF, 1), second)

        @pl.loop(0, 16)
        def _(k, kind=kind):
            other = kind * 16 + (q + k) % 16

            @pl.when(other != q)
            def _():
                send_coef(other).start()

    def respond(first, count, is_sin):
        lane = lax.broadcasted_iota(jnp.int32, (count, 128), 1)
        row = lax.broadcasted_iota(jnp.int32, (count, 128), 0) + first
        place = (q % (GROUP // 2)) * COEF + lane % COEF
        v = jnp.where((place == 0) & (q >= GROUP // 2), NX, place).astype(F32)
        scale = 2.0 * math.pi * grav_scale * thickness / (4.0 * NX * NX)
        weight = jnp.where(place == 0, scale, 2.0 * scale) * jnp.where(row == 0, 1.0, 2.0)
        layer = (2 * d + lane // COEF).astype(F32)
        rate = (top_depth + (layer + 0.5) * thickness) * (-2.0 * math.pi / (2 * NX))
        u = (jnp.where(row == 0, NX, row) if is_sin else row).astype(F32)
        return jnp.exp(jnp.sqrt(u * u + v * v) * rate) * weight

    @pl.loop(0, NX // 256)
    def _(k):
        rsp[pl.ds(pl.multiple_of(256 * k, 256), 256), :] = respond(256 * k, 256, False)

    rsp_first[...] = respond(0, 8, True)

    sbuf[block] = csend[q]
    pltpu.make_async_copy(sbuf.at[pl.ds(0, GROUP - 1)], sbuf.at[pl.ds(0, GROUP - 1)], cr).wait()

    for b in range(GROUP):
        value = sbuf[b]
        high, low = split(value)
        sst[0, ROWS * b : ROWS * (b + 1), :128] = high
        sst[0, ROWS * b : ROWS * (b + 1), 128:] = low
        sign = jnp.where((b // 2) % 2 == zh, 1.0, -1.0)
        high, low = split(value * sign)
        sst[1, ROWS * b : ROWS * (b + 1), :128] = high
        sst[1, ROWS * b : ROWS * (b + 1), 128:] = low
    tall_copy.wait()
    step = 256
    wide_half = lax.broadcasted_iota(jnp.int32, (step, 128), 1) < COEF
    for kind in range(2):

        @pl.loop(0, NX // step)
        def _(k, kind=kind):
            here = pl.ds(pl.multiple_of(k * step, step), step)
            both = matmul(tall[kind, 0, here, :], sst[kind])
            value = both[:, :128] + both[:, 128:] + matmul(tall[kind, 1, here, :], sst[kind, :, :128])
            factor = rsp[here, :]
            if kind == 1:
                fixed = jnp.concatenate([rsp_first[...], factor[8:]], axis=0)
                factor = jnp.where(k == 0, fixed, factor)
            value = value * factor
            value = value + pltpu.roll(value, COEF, 1)
            high = value.astype(BF16).astype(F32)
            pst[kind, here, :] = jnp.where(wide_half, high, value - high).astype(BF16)
            phi[kind, here, :] = jnp.where(wide_half, high, 0.0).astype(BF16)

    def send_rows(other):
        return pltpu.make_async_remote_copy(
            src_ref=xsend.at[other], dst_ref=cbuf.at[q], send_sem=xs, recv_sem=xr,
            device_id=at_q(other), device_id_type=MESH,
        )

    for part in range(2):
        cut = slice(256 * part, 256 * (part + 1))
        parity = []
        for kind in range(2):
            value = matmul(wide[kind, 0, cut, :], pst[kind]) + matmul(wide[kind, 1, cut, :], phi[kind])
            parity.append(value + pltpu.roll(value, COEF, 1))
        plus = parity[0] + parity[1]
        minus = parity[0] - parity[1]
        for g in range(4):
            up = [plus[ROWS * (4 * g + n) : ROWS * (4 * g + n + 1)] for n in range(4)]
            down = [minus[ROWS * (4 * g + n) : ROWS * (4 * g + n + 1)] for n in range(4)]
            chunk = 4 * part + g
            xsend[2 * (8 + chunk)] = jnp.where(half_lane, up[0], up[2])
            xsend[2 * (8 + chunk) + 1] = jnp.where(half_lane, up[1], up[3])
            xsend[2 * (7 - chunk)] = jnp.where(half_lane, down[3], down[1])
            xsend[2 * (7 - chunk) + 1] = jnp.where(half_lane, down[2], down[0])

        @pl.loop(0, 16)
        def _(k, part=part):
            if part == 0:
                other = 8 + (q + k) % 16
            else:
                other = (24 + (q + k) % 16) % GROUP

            @pl.when(other != q)
            def _():
                send_rows(other).start()

    cbuf[q] = xsend[q]
    pltpu.make_async_copy(cbuf.at[pl.ds(0, GROUP - 1)], cbuf.at[pl.ds(0, GROUP - 1)], xr).wait()

    parity = []
    for kind in range(2):
        tops, bottoms = [], []
        for m in range(8):
            first, second = cbuf[kind * 16 + 2 * m], cbuf[kind * 16 + 2 * m + 1]
            tops.append(jnp.where(half_lane, first, pltpu.roll(second, COEF, 1)))
            bottoms.append(jnp.where(half_lane, pltpu.roll(first, COEF, 1), second))
        value = jnp.concatenate([jnp.concatenate(tops, axis=1), jnp.concatenate(bottoms, axis=1)], axis=0)
        parity.append(table_right(value, tall[kind, 0], tall[kind, 1]))
    plus = parity[0] + parity[1]
    minus = parity[0] - parity[1]
    for other in range(RING):
        rows = slice(ROWS * (other // DEPTH), ROWS * (other // DEPTH + 1))
        col = other % DEPTH
        if col >= 4:
            gsend[other] = plus[rows, 128 * (col - 4) : 128 * (col - 3)]
        else:
            gsend[other] = minus[rows, 128 * (3 - col) : 128 * (4 - col)]

    def send_field(other):
        return pltpu.make_async_remote_copy(
            src_ref=gsend.at[other], dst_ref=gbuf.at[z], send_sem=gs, recv_sem=gr,
            device_id=at_z(other), device_id_type=MESH,
        )

    @pl.loop(0, RING - 1)
    def _(k):
        send_field((z + 8 + ((k + 1) // 2) * (1 - 2 * (k % 2)) + RING) % RING).start()

    gbuf[z] = gsend[z]
    pltpu.make_async_copy(gbuf.at[pl.ds(0, RING - 1)], gbuf.at[pl.ds(0, RING - 1)], gr).wait()
    total = gbuf[0]
    for other in range(1, RING):
        total = total + gbuf[other]
    total = jnp.where(d < DEPTH // 2, flip(total, 1, 128), total)
    out_ref[...] = jnp.where(lower, flip(total, 0, ROWS), total)

    for copy, there in zip(copies, has):
        pl.when(there)(copy.wait_send)
    pltpu.make_async_copy(csend.at[pl.ds(0, GROUP - 1)], csend.at[pl.ds(0, GROUP - 1)], cs).wait()
    pltpu.make_async_copy(xsend.at[pl.ds(0, GROUP - 1)], xsend.at[pl.ds(0, GROUP - 1)], xs).wait()
    pltpu.make_async_copy(gsend.at[pl.ds(0, RING - 1)], gsend.at[pl.ds(0, RING - 1)], gs).wait()


def solution(mesh):
    wide, tall = basis()

    def step(level_set, contrast):
        vmem = pl.BlockSpec(memory_space=pltpu.VMEM)
        anywhere = pl.BlockSpec(memory_space=pl.ANY)
        dma = pltpu.SemaphoreType.DMA
        return pl.pallas_call(
            kernel,
            out_shape=jax.ShapeDtypeStruct((ROWS, 128), F32),
            in_specs=[anywhere] * 4,
            out_specs=vmem,
            scratch_shapes=[
                pltpu.VMEM((2, ROWS, NX), F32),
                pltpu.SMEM((2,), F32),
                pltpu.VMEM((2, 2, HALF, NX), BF16),
                pltpu.VMEM((2, 2, NX, HALF), BF16),
                pltpu.VMEM((2, ROWS, NX), F32),
                pltpu.VMEM((2, 16, 128), F32),
                pltpu.VMEM((2, 16, 128), F32),
                pltpu.VMEM((GROUP, ROWS, 128), F32),
                pltpu.VMEM((GROUP, ROWS, 128), F32),
                pltpu.VMEM((2, HALF, 256), BF16),
                pltpu.VMEM((NX, 128), F32),
                pltpu.VMEM((8, 128), F32),
                pltpu.VMEM((2, NX, 128), BF16),
                pltpu.VMEM((2, NX, 128), BF16),
                pltpu.VMEM((GROUP, ROWS, 128), F32),
                pltpu.VMEM((GROUP, ROWS, 128), F32),
                pltpu.VMEM((RING, ROWS, 128), F32),
                pltpu.VMEM((RING, ROWS, 128), F32),
                dma(()), dma(()), dma(()), dma(()), dma((4,)), dma((4,)),
                dma(()), dma(()), dma(()), dma(()), dma(()), dma(()),
            ],
            compiler_params=pltpu.CompilerParams(
                collective_id=0, has_side_effects=True, vmem_limit_bytes=63 * 1024 * 1024
            ),
        )(level_set, contrast, jnp.asarray(wide), jnp.asarray(tall))

    return jax.shard_map(
        step,
        mesh=mesh,
        in_specs=(P("depth", "plan", None), P("depth")),
        out_specs=P("plan", "depth"),
        check_vma=False,
    )
```

profile of v0, /device:TPU:1, one launch (start us, length us, event | category | flops | bytes accessed | tf_op | source)
XLA Modules:
  0.0 57.4 jit_solution(17276243841180965524)
XLA Ops:
  0.0 56.0 %shard_map.46 = f32[16,128]{1,0:T(8,128)} custom-call(f32[2,16,1024]{2,1,0:T(8,128)} %ls_hbm.1, f32[2]{0:T(128)} %con_hbm.1, bf16[2,2,512,1024]{3,2,1,0:T(8,128)(2,1)} %constant.4.clone.wide_hbm, bf16[2,2,1024,512]{3,2,1,0:T(8,128)(2,1)} %constant.5.clone.tall_hbm), custom_call_target="tpu_custom_call" | custom-call | tf_op jit(solution)/shard_map/pallas_call | solution.py:361
  56.1 1.3 %copy.6 = f32[16,128]{1,0:T(8,128)} copy(f32[16,128]{1,0:T(8,128)} %shard_map.46) | data formatting | bytes 16384
where the time goes:
time: 57.6 us; the launch traced here: 57.4 us
  Pallas kernels  56 us (97%)
  local copies, waits for them, and re-layouts  1.3 us (2%)
    pallas_call x1, Pallas kernels, step(): pl.pallas_call(kernel, out_shape=jax.ShapeDtypeStruct((ROWS, 128), F32),...  56 us
    unnamed x1, local copies, waits for them, and re-layouts  1.3 us

commit v1 on v0

--- a/solution.py
+++ b/solution.py
@@ -87,17 +87,17 @@
 ):
     d = lax.axis_index("depth")
     p = lax.axis_index("plan")
-    core = p % 2
-    zh = (p // 2) % 2
-    q = (p // 4) * 2 + core
+    core = lax.rem(p, 2)
+    zh = lax.rem(lax.div(p, 2), 2)
+    q = lax.div(p, 4) * 2 + core
     z = zh * DEPTH + d
     lower = p < PLAN // 2
 
     def at_q(other):
-        return (d, (other // 2) * 4 + zh * 2 + other % 2)
+        return (d, lax.div(other, 2) * 4 + zh * 2 + lax.rem(other, 2))
 
     def at_z(other):
-        return (other % DEPTH, (q // 2) * 4 + (other // DEPTH) * 2 + core)
+        return (lax.rem(other, DEPTH), p + 2 * (lax.div(other, DEPTH) - zh))
 
     ls_copy = pltpu.make_async_copy(ls_hbm, ls_ref, ls_sem)
     con_copy = pltpu.make_async_copy(con_hbm, con_ref, con_sem)
@@ -113,21 +113,22 @@
     def greet(target):
         pl.semaphore_signal(barrier, inc=1, device_id=target, device_id_type=MESH)
 
-    @pl.loop(1, GROUP)
-    def _(k):
-        greet(at_q((q + k) % GROUP))
-
-    @pl.loop(1, RING)
-    def _(k):
-        greet(at_z((z + k) % RING))
-
+    has = (d < DEPTH - 1, d > 0, p < PLAN - 1, p > 0)
+    gets = (d > 0, d < DEPTH - 1, p > 0, p < PLAN - 1)
+    pl.when(has[0])(lambda: greet((d + 1, p)))
+    pl.when(has[1])(lambda: greet((d - 1, p)))
+    pl.when(has[2])(lambda: greet((d, p + 1)))
+    pl.when(has[3])(lambda: greet((d, p - 1)))
     outer = jnp.where(core == 0, p - 1, p + 1)
-
     has_outer = (outer >= 0) & (outer < PLAN)
-
-    @pl.when(has_outer)
-    def _():
-        greet((d, outer))
+    buddy = p + 1 - 2 * core
+    for other in range(GROUP):
+        target = (other // 2) * 4 + other % 2 + zh * 2
+        pl.when((target != p) & (target != buddy))(lambda target=target: greet((d, target)))
+    for other in range(RING):
+        row = other // DEPTH
+        far = (row != zh) | (other % DEPTH > d + 1) | (other % DEPTH < d - 1)
+        pl.when(far)(lambda other=other, row=row: greet((other % DEPTH, p + 2 * (row - zh))))
 
     ls_copy.wait()
     con_copy.wait()
@@ -150,8 +151,6 @@
     z_down = halo(ls_ref.at[0], zhalo.at[1], 1, (d - 1, p))
     r_up = halo(rsend.at[1], rhalo.at[0], 2, (d, p + 1))
     r_down = halo(rsend.at[0], rhalo.at[1], 3, (d, p - 1))
-    has = (d < DEPTH - 1, d > 0, p < PLAN - 1, p > 0)
-    gets = (d > 0, d < DEPTH - 1, p > 0, p < PLAN - 1)
     lands = (zhalo.at[0], zhalo.at[1], rhalo.at[0], rhalo.at[1])
     copies = (z_up, z_down, r_up, r_down)
     for copy, there in zip(copies, has):
@@ -214,7 +213,7 @@
 
         @pl.loop(0, 16)
         def _(k, kind=kind):
-            other = kind * 16 + (q + k) % 16
+            other = kind * 16 + lax.rem(q + k, 16)
 
             @pl.when(other != q)
             def _():
@@ -296,9 +295,9 @@
         @pl.loop(0, 16)
         def _(k, part=part):
             if part == 0:
-                other = 8 + (q + k) % 16
+                other = 8 + lax.rem(q + k, 16)
             else:
-                other = (24 + (q + k) % 16) % GROUP
+                other = lax.rem(24 + lax.rem(q + k, 16), GROUP)
 
             @pl.when(other != q)
             def _():
@@ -334,7 +333,7 @@
 
     @pl.loop(0, RING - 1)
     def _(k):
-        send_field((z + 8 + ((k + 1) // 2) * (1 - 2 * (k % 2)) + RING) % RING).start()
+        send_field(lax.rem(z + 8 + lax.div(k + 1, 2) * (1 - 2 * lax.rem(k, 2)) + RING, RING)).start()
 
     gbuf[z] = gsend[z]
     pltpu.make_async_copy(gbuf.at[pl.ds(0, RING - 1)], gbuf.at[pl.ds(0, RING - 1)], gr).wait()

time: 57.6 us -> 56.3 us (0.977)
  Pallas kernels: 56 us -> 54.8 us
    pallas_call x1, Pallas kernels: 56 us -> 54.8 us  [step(): pl.pallas_call(kernel, out_shape=jax.ShapeDtypeStruct((ROWS, 128), F32),...]
where the time goes in v1:
time: 56.3 us; the launch traced here: 56.2 us
  Pallas kernels  54.8 us (97%)
  local copies, waits for them, and re-layouts  1.3 us (2%)
    pallas_call x1, Pallas kernels, step(): pl.pallas_call(kernel, out_shape=jax.ShapeDtypeStruct((ROWS, 128), F32),...  54.8 us
    unnamed x1, local copies, waits for them, and re-layouts  1.3 us

profile of v1, /device:TPU:1, one launch (start us, length us, event | category | flops | bytes accessed | tf_op | source)
XLA Modules:
  0.0 56.2 jit_solution(3261476175070913514)
XLA Ops:
  0.0 54.8 %shard_map.46 = f32[16,128]{1,0:T(8,128)} custom-call(f32[2,16,1024]{2,1,0:T(8,128)} %ls_hbm.1, f32[2]{0:T(128)} %con_hbm.1, bf16[2,2,512,1024]{3,2,1,0:T(8,128)(2,1)} %constant.4.clone.wide_hbm, bf16[2,2,1024,512]{3,2,1,0:T(8,128)(2,1)} %constant.5.clone.tall_hbm), custom_call_target="tpu_custom_call" | custom-call | tf_op jit(solution)/shard_map/pallas_call | solution.py:360
  54.9 1.3 %copy.6 = f32[16,128]{1,0:T(8,128)} copy(f32[16,128]{1,0:T(8,128)} %shard_map.46) | data formatting | bytes 16384

commit v2 on v1

--- a/solution.py
+++ b/solution.py
@@ -38,7 +38,9 @@
     high = both.astype(ml_dtypes.bfloat16)
     low = (both - high.astype(np.float64)).astype(ml_dtypes.bfloat16)
     wide = np.stack([high, low], axis=1)
-    return wide, np.ascontiguousarray(np.swapaxes(wide, 2, 3))
+    tall = np.swapaxes(wide, 2, 3)
+    order = np.arange(HALF).reshape(GROUP, 2, ROWS // 2).transpose(1, 0, 2).reshape(-1)
+    return wide, np.ascontiguousarray(tall[..., order]), np.ascontiguousarray(tall)
 
 
 def flux(step):
@@ -81,9 +83,9 @@
 
 
 def kernel(
-    ls_hbm, con_hbm, wide_hbm, tall_hbm, out_ref,
-    ls_ref, con_ref, wide, tall, zhalo, rsend, rhalo, csend, sbuf, sst, rsp, rsp_first, pst, phi, xsend, cbuf, gsend, gbuf,
-    ls_sem, con_sem, wide_sem, tall_sem, hs, hr, cs, cr, xs, xr, gs, gr,
+    ls_hbm, con_hbm, wide_hbm, mixed_hbm, tall_hbm, out_ref,
+    ls_ref, con_ref, wide, mixed, tall, zhalo, rsend, rhalo, csend, sbuf, sst, acc, rsp, rsp_first, pst, phi, xsend, cbuf, gsend, gbuf,
+    ls_sem, con_sem, wide_sem, mixed_sem, tall_sem, hs, hr, cs, cr, xs, xr, gs, gr,
 ):
     d = lax.axis_index("depth")
     p = lax.axis_index("plan")
@@ -104,9 +106,9 @@
     ls_copy.start()
     con_copy.start()
     wide_copy = pltpu.make_async_copy(wide_hbm, wide, wide_sem)
+    mixed_copy = pltpu.make_async_copy(mixed_hbm, mixed, mixed_sem)
     tall_copy = pltpu.make_async_copy(tall_hbm, tall, tall_sem)
     wide_copy.start()
-    tall_copy.start()
 
     barrier = pltpu.get_barrier_semaphore()
 
@@ -163,6 +165,8 @@
 
     for copy, comes in zip(copies, gets):
         pl.when(comes)(copy.wait_recv)
+    mixed_copy.start()
+    tall_copy.start()
     row_id = lax.broadcasted_iota(jnp.int32, (ROWS, NX), 0)
     col_id = lax.broadcasted_iota(jnp.int32, (ROWS, NX), 1)
     field = [ls_ref[0], ls_ref[1]]
@@ -196,11 +200,20 @@
     half_lane = lax.broadcasted_iota(jnp.int32, (ROWS, 128), 1) < COEF
     wide_copy.wait()
 
-    def send_coef(other):
+    def send_coef(part, other):
         return pltpu.make_async_remote_copy(
-            src_ref=csend.at[other], dst_ref=sbuf.at[block], send_sem=cs, recv_sem=cr,
+            src_ref=csend.at[part, other], dst_ref=sbuf.at[part, block], send_sem=cs.at[part], recv_sem=cr.at[part],
             device_id=at_q(other), device_id_type=MESH,
         )
+
+    def send_coefs(part, kind):
+        @pl.loop(0, 16)
+        def _(k):
+            other = kind * 16 + lax.rem(q + k, 16)
+
+            @pl.when(other != q)
+            def _():
+                send_coef(part, other).start()
 
     for kind, pair in enumerate((even, odd)):
         coef = table_right(jnp.concatenate(pair, axis=0), wide[kind, 0], wide[kind, 1])
@@ -208,16 +221,14 @@
             first = coef[:ROWS, 128 * m : 128 * (m + 1)]
             second = coef[ROWS:, 128 * m : 128 * (m + 1)]
             spot = kind * 16 + 2 * m
-            csend[spot] = jnp.where(half_lane, first, pltpu.roll(second, COEF, 1))
-            csend[spot + 1] = jnp.where(half_lane, pltpu.roll(first, COEF, 1), second)
-
-        @pl.loop(0, 16)
-        def _(k, kind=kind):
-            other = kind * 16 + lax.rem(q + k, 16)
-
-            @pl.when(other != q)
-            def _():
-                send_coef(other).start()
+            one = jnp.where(half_lane, first, pltpu.roll(second, COEF, 1))
+            two = jnp.where(half_lane, pltpu.roll(first, COEF, 1), second)
+            for part in range(2):
+                csend[part, spot] = one[8 * part : 8 * part + 8]
+                csend[part, spot + 1] = two[8 * part : 8 * part + 8]
+        send_coefs(0, kind)
+    send_coefs(1, 0)
+    send_coefs(1, 1)
 
     def respond(first, count, is_sin):
         lane = lax.broadcasted_iota(jnp.int32, (count, 128), 1)
@@ -237,46 +248,58 @@
 
     rsp_first[...] = respond(0, 8, True)
 
-    sbuf[block] = csend[q]
-    pltpu.make_async_copy(sbuf.at[pl.ds(0, GROUP - 1)], sbuf.at[pl.ds(0, GROUP - 1)], cr).wait()
-
-    for b in range(GROUP):
-        value = sbuf[b]
-        high, low = split(value)
-        sst[0, ROWS * b : ROWS * (b + 1), :128] = high
-        sst[0, ROWS * b : ROWS * (b + 1), 128:] = low
-        sign = jnp.where((b // 2) % 2 == zh, 1.0, -1.0)
-        high, low = split(value * sign)
-        sst[1, ROWS * b : ROWS * (b + 1), :128] = high
-        sst[1, ROWS * b : ROWS * (b + 1), 128:] = low
-    tall_copy.wait()
     step = 256
     wide_half = lax.broadcasted_iota(jnp.int32, (step, 128), 1) < COEF
-    for kind in range(2):
-
-        @pl.loop(0, NX // step)
-        def _(k, kind=kind):
-            here = pl.ds(pl.multiple_of(k * step, step), step)
-            both = matmul(tall[kind, 0, here, :], sst[kind])
-            value = both[:, :128] + both[:, 128:] + matmul(tall[kind, 1, here, :], sst[kind, :, :128])
-            factor = rsp[here, :]
-            if kind == 1:
-                fixed = jnp.concatenate([rsp_first[...], factor[8:]], axis=0)
-                factor = jnp.where(k == 0, fixed, factor)
-            value = value * factor
-            value = value + pltpu.roll(value, COEF, 1)
-            high = value.astype(BF16).astype(F32)
-            pst[kind, here, :] = jnp.where(wide_half, high, value - high).astype(BF16)
-            phi[kind, here, :] = jnp.where(wide_half, high, 0.0).astype(BF16)
-
-    def send_rows(other):
+    block_of = lax.div(lax.broadcasted_iota(jnp.int32, (step, 128), 0), 16)
+    sign = jnp.where(lax.rem(block_of, 2) == zh, 1.0, -1.0)
+    mixed_copy.wait()
+    for part in range(2):
+        sbuf[part, block] = csend[part, q]
+        landed = sbuf.at[part, pl.ds(0, GROUP - 1)]
+        pltpu.make_async_copy(landed, landed, cr.at[part]).wait()
+        value = sbuf[part].reshape(step, 128)
+        for kind in range(2):
+            high, low = split(value * sign if kind else value)
+            sst[kind, part, :, :128] = high
+            sst[kind, part, :, 128:] = low
+        for kind in range(2):
+
+            @pl.loop(0, NX // step)
+            def _(k, kind=kind, part=part):
+                here = pl.ds(pl.multiple_of(k * step, step), step)
+                cols = slice(step * part, step * (part + 1))
+                both = matmul(mixed[kind, 0, here, cols], sst[kind, part])
+                value = both[:, :128] + both[:, 128:] + matmul(mixed[kind, 1, here, cols], sst[kind, part, :, :128])
+                if part == 0:
+                    acc[kind, here, :] = value
+                    return
+                factor = rsp[here, :]
+                if kind == 1:
+                    fixed = jnp.concatenate([rsp_first[...], factor[8:]], axis=0)
+                    factor = jnp.where(k == 0, fixed, factor)
+                value = (value + acc[kind, here, :]) * factor
+                value = value + pltpu.roll(value, COEF, 1)
+                high = value.astype(BF16).astype(F32)
+                pst[kind, here, :] = jnp.where(wide_half, high, value - high).astype(BF16)
+                phi[kind, here, :] = jnp.where(wide_half, high, 0.0).astype(BF16)
+
+    def send_row(part, other):
         return pltpu.make_async_remote_copy(
-            src_ref=xsend.at[other], dst_ref=cbuf.at[q], send_sem=xs, recv_sem=xr,
+            src_ref=xsend.at[part, other], dst_ref=cbuf.at[part, q], send_sem=xs.at[part], recv_sem=xr.at[part],
             device_id=at_q(other), device_id_type=MESH,
         )
 
-    for part in range(2):
-        cut = slice(256 * part, 256 * (part + 1))
+    def send_rows(part, chunk):
+        @pl.loop(0, 16)
+        def _(k):
+            other = lax.rem(8 + 16 * chunk + lax.rem(q + k, 16), GROUP)
+
+            @pl.when(other != q)
+            def _():
+                send_row(part, other).start()
+
+    for chunk in range(2):
+        cut = slice(256 * chunk, 256 * (chunk + 1))
         parity = []
         for kind in range(2):
             value = matmul(wide[kind, 0, cut, :], pst[kind]) + matmul(wide[kind, 1, cut, :], phi[kind])
@@ -286,72 +309,80 @@
         for g in range(4):
             up = [plus[ROWS * (4 * g + n) : ROWS * (4 * g + n + 1)] for n in range(4)]
             down = [minus[ROWS * (4 * g + n) : ROWS * (4 * g + n + 1)] for n in range(4)]
-            chunk = 4 * part + g
-            xsend[2 * (8 + chunk)] = jnp.where(half_lane, up[0], up[2])
-            xsend[2 * (8 + chunk) + 1] = jnp.where(half_lane, up[1], up[3])
-            xsend[2 * (7 - chunk)] = jnp.where(half_lane, down[3], down[1])
-            xsend[2 * (7 - chunk) + 1] = jnp.where(half_lane, down[2], down[0])
-
-        @pl.loop(0, 16)
-        def _(k, part=part):
-            if part == 0:
-                other = 8 + lax.rem(q + k, 16)
-            else:
-                other = lax.rem(24 + lax.rem(q + k, 16), GROUP)
-
-            @pl.when(other != q)
-            def _():
-                send_rows(other).start()
-
-    cbuf[q] = xsend[q]
-    pltpu.make_async_copy(cbuf.at[pl.ds(0, GROUP - 1)], cbuf.at[pl.ds(0, GROUP - 1)], xr).wait()
-
-    parity = []
-    for kind in range(2):
-        tops, bottoms = [], []
-        for m in range(8):
-            first, second = cbuf[kind * 16 + 2 * m], cbuf[kind * 16 + 2 * m + 1]
-            tops.append(jnp.where(half_lane, first, pltpu.roll(second, COEF, 1)))
-            bottoms.append(jnp.where(half_lane, pltpu.roll(first, COEF, 1), second))
-        value = jnp.concatenate([jnp.concatenate(tops, axis=1), jnp.concatenate(bottoms, axis=1)], axis=0)
-        parity.append(table_right(value, tall[kind, 0], tall[kind, 1]))
-    plus = parity[0] + parity[1]
-    minus = parity[0] - parity[1]
-    for other in range(RING):
-        rows = slice(ROWS * (other // DEPTH), ROWS * (other // DEPTH + 1))
-        col = other % DEPTH
-        if col >= 4:
-            gsend[other] = plus[rows, 128 * (col - 4) : 128 * (col - 3)]
-        else:
-            gsend[other] = minus[rows, 128 * (3 - col) : 128 * (4 - col)]
-
-    def send_field(other):
+            place = 4 * chunk + g
+            for spot, one, two in (
+                (2 * (8 + place), up[0], up[2]),
+                (2 * (8 + place) + 1, up[1], up[3]),
+                (2 * (7 - place), down[3], down[1]),
+                (2 * (7 - place) + 1, down[2], down[0]),
+            ):
+                value = jnp.where(half_lane, one, two)
+                for part in range(2):
+                    xsend[part, spot] = value[8 * part : 8 * part + 8]
+        send_rows(0, chunk)
+    send_rows(1, 0)
+    send_rows(1, 1)
+
+    def send_field(part, other):
         return pltpu.make_async_remote_copy(
-            src_ref=gsend.at[other], dst_ref=gbuf.at[z], send_sem=gs, recv_sem=gr,
+            src_ref=gsend.at[part, other], dst_ref=gbuf.at[part, z], send_sem=gs.at[part], recv_sem=gr.at[part],
             device_id=at_z(other), device_id_type=MESH,
         )
 
-    @pl.loop(0, RING - 1)
-    def _(k):
-        send_field(lax.rem(z + 8 + lax.div(k + 1, 2) * (1 - 2 * lax.rem(k, 2)) + RING, RING)).start()
-
-    gbuf[z] = gsend[z]
-    pltpu.make_async_copy(gbuf.at[pl.ds(0, RING - 1)], gbuf.at[pl.ds(0, RING - 1)], gr).wait()
-    total = gbuf[0]
-    for other in range(1, RING):
-        total = total + gbuf[other]
+    tall_copy.wait()
+    half_lane = lax.broadcasted_iota(jnp.int32, (8, 128), 1) < COEF
+    for part in range(2):
+        cbuf[part, q] = xsend[part, q]
+        landed = cbuf.at[part, pl.ds(0, GROUP - 1)]
+        pltpu.make_async_copy(landed, landed, xr.at[part]).wait()
+        parity = []
+        for kind in range(2):
+            tops, bottoms = [], []
+            for m in range(8):
+                first, second = cbuf[part, kind * 16 + 2 * m], cbuf[part, kind * 16 + 2 * m + 1]
+                tops.append(jnp.where(half_lane, first, pltpu.roll(second, COEF, 1)))
+                bottoms.append(jnp.where(half_lane, pltpu.roll(first, COEF, 1), second))
+            value = jnp.concatenate([jnp.concatenate(tops, axis=1), jnp.concatenate(bottoms, axis=1)], axis=0)
+            parity.append(table_right(value, tall[kind, 0], tall[kind, 1]))
+        plus = parity[0] + parity[1]
+        minus = parity[0] - parity[1]
+        for other in range(RING):
+            rows = slice(8 * (other // DEPTH), 8 * (other // DEPTH + 1))
+            col = other % DEPTH
+            if col >= 4:
+                gsend[part, other] = plus[rows, 128 * (col - 4) : 128 * (col - 3)]
+            else:
+                gsend[part, other] = minus[rows, 128 * (3 - col) : 128 * (4 - col)]
+
+        @pl.loop(0, RING - 1)
+        def _(k, part=part):
+            other = z + 8 + lax.div(k + 1, 2) * (1 - 2 * lax.rem(k, 2)) + RING
+            send_field(part, lax.rem(other, RING)).start()
+
+        gbuf[part, z] = gsend[part, z]
+
+    halves = []
+    for part in range(2):
+        landed = gbuf.at[part, pl.ds(0, RING - 1)]
+        pltpu.make_async_copy(landed, landed, gr.at[part]).wait()
+        total = gbuf[part, 0]
+        for other in range(1, RING):
+            total = total + gbuf[part, other]
+        halves.append(total)
+    total = jnp.concatenate(halves, axis=0)
     total = jnp.where(d < DEPTH // 2, flip(total, 1, 128), total)
     out_ref[...] = jnp.where(lower, flip(total, 0, ROWS), total)
 
     for copy, there in zip(copies, has):
         pl.when(there)(copy.wait_send)
-    pltpu.make_async_copy(csend.at[pl.ds(0, GROUP - 1)], csend.at[pl.ds(0, GROUP - 1)], cs).wait()
-    pltpu.make_async_copy(xsend.at[pl.ds(0, GROUP - 1)], xsend.at[pl.ds(0, GROUP - 1)], xs).wait()
-    pltpu.make_async_copy(gsend.at[pl.ds(0, RING - 1)], gsend.at[pl.ds(0, RING - 1)], gs).wait()
+    for part in range(2):
+        for buffer, semaphore, peers in ((csend, cs, GROUP - 1), (xsend, xs, GROUP - 1), (gsend, gs, RING - 1)):
+            left = buffer.at[part, pl.ds(0, peers)]
+            pltpu.make_async_copy(left, left, semaphore.at[part]).wait()
 
 
 def solution(mesh):
-    wide, tall = basis()
+    wide, mixed, tall = basis()
 
     def step(level_set, contrast):
         vmem = pl.BlockSpec(memory_space=pltpu.VMEM)
@@ -360,34 +391,36 @@
         return pl.pallas_call(
             kernel,
             out_shape=jax.ShapeDtypeStruct((ROWS, 128), F32),
-            in_specs=[anywhere] * 4,
+            in_specs=[anywhere] * 5,
             out_specs=vmem,
             scratch_shapes=[
                 pltpu.VMEM((2, ROWS, NX), F32),
                 pltpu.SMEM((2,), F32),
                 pltpu.VMEM((2, 2, HALF, NX), BF16),
                 pltpu.VMEM((2, 2, NX, HALF), BF16),
+                pltpu.VMEM((2, 2, NX, HALF), BF16),
                 pltpu.VMEM((2, ROWS, NX), F32),
                 pltpu.VMEM((2, 16, 128), F32),
                 pltpu.VMEM((2, 16, 128), F32),
-                pltpu.VMEM((GROUP, ROWS, 128), F32),
-                pltpu.VMEM((GROUP, ROWS, 128), F32),
-                pltpu.VMEM((2, HALF, 256), BF16),
+                pltpu.VMEM((2, GROUP, 8, 128), F32),
+                pltpu.VMEM((2, GROUP, 8, 128), F32),
+                pltpu.VMEM((2, 2, HALF // 2, 256), BF16),
+                pltpu.VMEM((2, NX, 128), F32),
                 pltpu.VMEM((NX, 128), F32),
                 pltpu.VMEM((8, 128), F32),
                 pltpu.VMEM((2, NX, 128), BF16),
                 pltpu.VMEM((2, NX, 128), BF16),
-                pltpu.VMEM((GROUP, ROWS, 128), F32),
-                pltpu.VMEM((GROUP, ROWS, 128), F32),
-                pltpu.VMEM((RING, ROWS, 128), F32),
-                pltpu.VMEM((RING, ROWS, 128), F32),
-                dma(()), dma(()), dma(()), dma(()), dma((4,)), dma((4,)),
-                dma(()), dma(()), dma(()), dma(()), dma(()), dma(()),
+                pltpu.VMEM((2, GROUP, 8, 128), F32),
+                pltpu.VMEM((2, GROUP, 8, 128), F32),
+                pltpu.VMEM((2, RING, 8, 128), F32),
+                pltpu.VMEM((2, RING, 8, 128), F32),
+                dma(()), dma(()), dma(()), dma(()), dma(()), dma((4,)), dma((4,)),
+                dma((2,)), dma((2,)), dma((2,)), dma((2,)), dma((2,)), dma((2,)),
             ],
             compiler_params=pltpu.CompilerParams(
                 collective_id=0, has_side_effects=True, vmem_limit_bytes=63 * 1024 * 1024
             ),
-        )(level_set, contrast, jnp.asarray(wide), jnp.asarray(tall))
+        )(level_set, contrast, jnp.asarray(wide), jnp.asarray(mixed), jnp.asarray(tall))
 
     return jax.shard_map(
         step,

time: 56.3 us -> 58 us (1.030)
  Pallas kernels: 54.8 us -> 56.5 us
    pallas_call x1, Pallas kernels: 54.8 us -> 56.5 us  [step(): pl.pallas_call(kernel, out_shape=jax.ShapeDtypeStruct((ROWS, 128), F32),...]
where the time goes in v2:
time: 58 us; the launch traced here: 57.8 us
  Pallas kernels  56.5 us (97%)
  local copies, waits for them, and re-layouts  1.3 us (2%)
    pallas_call x1, Pallas kernels, step(): pl.pallas_call(kernel, out_shape=jax.ShapeDtypeStruct((ROWS, 128), F32),...  56.5 us
    unnamed x1, local copies, waits for them, and re-layouts  1.3 us

profile of v2, /device:TPU:1, one launch (start us, length us, event | category | flops | bytes accessed | tf_op | source)
XLA Modules:
  0.0 57.8 jit_solution(7964795612032340533)
XLA Ops:
  0.0 56.5 %shard_map.55 = f32[16,128]{1,0:T(8,128)} custom-call(f32[2,16,1024]{2,1,0:T(8,128)} %ls_hbm.1, f32[2]{0:T(128)} %con_hbm.1, bf16[2,2,512,1024]{3,2,1,0:T(8,128)(2,1)} %constant.6.clone.wide_hbm, bf16[2,2,1024,512]{3,2,1,0:T(8,128)(2,1)} %constant.7.clone.mixed_hbm, bf16[2,2,1024,512]{3,2,1,0:T(8,128)(2,1)} %constant.8.clone.tall_hbm), custom_call_target="tpu_custom_call" | custom-call | tf_op jit(solution)/shard_map/pallas_call | solution.py:391
  56.5 1.3 %copy.7 = f32[16,128]{1,0:T(8,128)} copy(f32[16,128]{1,0:T(8,128)} %shard_map.55) | data formatting | bytes 16384

commit v3 on v1

--- a/solution.py
+++ b/solution.py
@@ -211,12 +211,11 @@
             csend[spot] = jnp.where(half_lane, first, pltpu.roll(second, COEF, 1))
             csend[spot + 1] = jnp.where(half_lane, pltpu.roll(first, COEF, 1), second)
 
-        @pl.loop(0, 16)
-        def _(k, kind=kind):
+        for k in range(16):
             other = kind * 16 + lax.rem(q + k, 16)
-
-            @pl.when(other != q)
-            def _():
+            if k == 0:
+                pl.when(other != q)(send_coef(other).start)
+            else:
                 send_coef(other).start()
 
     def respond(first, count, is_sin):
@@ -253,16 +252,13 @@
     step = 256
     wide_half = lax.broadcasted_iota(jnp.int32, (step, 128), 1) < COEF
     for kind in range(2):
-
-        @pl.loop(0, NX // step)
-        def _(k, kind=kind):
-            here = pl.ds(pl.multiple_of(k * step, step), step)
+        for k in range(NX // step):
+            here = slice(k * step, (k + 1) * step)
             both = matmul(tall[kind, 0, here, :], sst[kind])
             value = both[:, :128] + both[:, 128:] + matmul(tall[kind, 1, here, :], sst[kind, :, :128])
             factor = rsp[here, :]
-            if kind == 1:
-                fixed = jnp.concatenate([rsp_first[...], factor[8:]], axis=0)
-                factor = jnp.where(k == 0, fixed, factor)
+            if kind == 1 and k == 0:
+                factor = jnp.concatenate([rsp_first[...], factor[8:]], axis=0)
             value = value * factor
             value = value + pltpu.roll(value, COEF, 1)
             high = value.astype(BF16).astype(F32)
@@ -292,15 +288,13 @@
             xsend[2 * (7 - chunk)] = jnp.where(half_lane, down[3], down[1])
             xsend[2 * (7 - chunk) + 1] = jnp.where(half_lane, down[2], down[0])
 
-        @pl.loop(0, 16)
-        def _(k, part=part):
-            if part == 0:
-                other = 8 + lax.rem(q + k, 16)
+        for k in range(16):
+            spot = lax.rem(q + k, 16)
+            upper = lax.div(spot, 8)
+            other = spot + 16 * (upper if part else 1 - upper)
+            if k == 0:
+                pl.when(other != q)(send_rows(other).start)
             else:
-                other = lax.rem(24 + lax.rem(q + k, 16), GROUP)
-
-            @pl.when(other != q)
-            def _():
                 send_rows(other).start()
 
     cbuf[q] = xsend[q]
@@ -331,9 +325,9 @@
             device_id=at_z(other), device_id_type=MESH,
         )
 
-    @pl.loop(0, RING - 1)
-    def _(k):
-        send_field(lax.rem(z + 8 + lax.div(k + 1, 2) * (1 - 2 * lax.rem(k, 2)) + RING, RING)).start()
+    for k in range(RING - 1):
+        away = 8 + (k + 1) // 2 * (1 - 2 * (k % 2))
+        send_field(lax.rem(z + away, RING)).start()
 
     gbuf[z] = gsend[z]
     pltpu.make_async_copy(gbuf.at[pl.ds(0, RING - 1)], gbuf.at[pl.ds(0, RING - 1)], gr).wait()

time: 56.3 us -> 53.7 us (0.954)
  Pallas kernels: 54.8 us -> 51.8 us
    pallas_call x1, Pallas kernels: 54.8 us -> 51.8 us  [step(): pl.pallas_call(kernel, out_shape=jax.ShapeDtypeStruct((ROWS, 128), F32),...]
where the time goes in v3:
time: 53.7 us; the launch traced here: 53.1 us
  Pallas kernels  51.8 us (96%)
  local copies, waits for them, and re-layouts  1.3 us (2%)
    pallas_call x1, Pallas kernels, step(): pl.pallas_call(kernel, out_shape=jax.ShapeDtypeStruct((ROWS, 128), F32),...  51.8 us
    unnamed x1, local copies, waits for them, and re-layouts  1.3 us

profile of v3, /device:TPU:1, one launch (start us, length us, event | category | flops | bytes accessed | tf_op | source)
XLA Modules:
  0.0 53.1 jit_solution(17667810823730421330)
XLA Ops:
  0.0 51.8 %shard_map.46 = f32[16,128]{1,0:T(8,128)} custom-call(f32[2,16,1024]{2,1,0:T(8,128)} %ls_hbm.1, f32[2]{0:T(128)} %con_hbm.1, bf16[2,2,512,1024]{3,2,1,0:T(8,128)(2,1)} %constant.4.clone.wide_hbm, bf16[2,2,1024,512]{3,2,1,0:T(8,128)(2,1)} %constant.5.clone.tall_hbm), custom_call_target="tpu_custom_call" | custom-call | tf_op jit(solution)/shard_map/pallas_call | solution.py:354
  51.8 1.3 %copy.6 = f32[16,128]{1,0:T(8,128)} copy(f32[16,128]{1,0:T(8,128)} %shard_map.46) | data formatting | bytes 16384

commit v4 on v3

--- a/solution.py
+++ b/solution.py
@@ -73,16 +73,19 @@
     return jnp.dot(a, b, preferred_element_type=F32)
 
 
-def table_right(value, high_table, low_table):
-    n = value.shape[0]
-    high, low = split(value)
-    both = matmul(jnp.concatenate([high, low], axis=0), high_table)
-    return both[:n] + both[n:] + matmul(high, low_table)
+def pair(value):
+    return jnp.concatenate(split(value), axis=0)
+
+
+def table_right(both, high_table, low_table):
+    n = both.shape[0] // 2
+    product = matmul(both, high_table)
+    return product[:n] + product[n:] + matmul(both[:n], low_table)
 
 
 def kernel(
     ls_hbm, con_hbm, wide_hbm, tall_hbm, out_ref,
-    ls_ref, con_ref, wide, tall, zhalo, rsend, rhalo, csend, sbuf, sst, rsp, rsp_first, pst, phi, xsend, cbuf, gsend, gbuf,
+    ls_ref, con_ref, own, part_density, wide, tall, zhalo, rsend, rhalo, csend, sbuf, sst, rsp, rsp_first, pst, phi, xsend, cbuf, gsend, gbuf,
     ls_sem, con_sem, wide_sem, tall_sem, hs, hr, cs, cr, xs, xr, gs, gr,
 ):
     d = lax.axis_index("depth")
@@ -115,29 +118,36 @@
 
     has = (d < DEPTH - 1, d > 0, p < PLAN - 1, p > 0)
     gets = (d > 0, d < DEPTH - 1, p > 0, p < PLAN - 1)
-    pl.when(has[0])(lambda: greet((d + 1, p)))
-    pl.when(has[1])(lambda: greet((d - 1, p)))
-    pl.when(has[2])(lambda: greet((d, p + 1)))
-    pl.when(has[3])(lambda: greet((d, p - 1)))
+    xy = lax.div(p, 4)
     outer = jnp.where(core == 0, p - 1, p + 1)
     has_outer = (outer >= 0) & (outer < PLAN)
-    buddy = p + 1 - 2 * core
-    for other in range(GROUP):
-        target = (other // 2) * 4 + other % 2 + zh * 2
-        pl.when((target != p) & (target != buddy))(lambda target=target: greet((d, target)))
-    for other in range(RING):
-        row = other // DEPTH
-        far = (row != zh) | (other % DEPTH > d + 1) | (other % DEPTH < d - 1)
-        pl.when(far)(lambda other=other, row=row: greet((other % DEPTH, p + 2 * (row - zh))))
+    for k in (1, RING - 1):
+        greet(at_z(lax.rem(z + k, RING)))
+    greet((d, p + 1 - 2 * core))
+    pl.when(has_outer)(lambda: greet((d, outer)))
+    for k in range(1, GROUP // 2):
+        first = 4 * lax.rem(xy + k, GROUP // 2) + 2 * zh
+        greet((d, first))
+        greet((d, first + 1))
+    for k in range(2, RING - 1):
+        greet(at_z(lax.rem(z + k, RING)))
 
     ls_copy.wait()
     con_copy.wait()
+
+    for layer in range(2):
+        value = ls_ref[layer]
+        value = jnp.where(lower, flip(value, 0, ROWS), value)
+        own[layer, :, :HALF] = value[:, HALF:]
+        own[layer, :, HALF:] = flip_lanes(value[:, :HALF])
 
     for layer in range(2):
         for k in range(8):
             spot = layer * 8 + k
-            rsend[0, spot : spot + 1, :] = ls_ref[layer, 0:1, 128 * k : 128 * (k + 1)]
-            rsend[1, spot : spot + 1, :] = ls_ref[layer, ROWS - 1 : ROWS, 128 * k : 128 * (k + 1)]
+            top = own[layer, 0:1, 128 * k : 128 * (k + 1)]
+            bottom = own[layer, ROWS - 1 : ROWS, 128 * k : 128 * (k + 1)]
+            rsend[0, spot : spot + 1, :] = jnp.where(lower, bottom, top)
+            rsend[1, spot : spot + 1, :] = jnp.where(lower, top, bottom)
 
     pl.semaphore_wait(barrier, GROUP + RING - 2 + has_outer.astype(jnp.int32))
 
@@ -147,8 +157,8 @@
             device_id=device, device_id_type=MESH,
         )
 
-    z_up = halo(ls_ref.at[1], zhalo.at[0], 0, (d + 1, p))
-    z_down = halo(ls_ref.at[0], zhalo.at[1], 1, (d - 1, p))
+    z_up = halo(own.at[1], zhalo.at[0], 0, (d + 1, p))
+    z_down = halo(own.at[0], zhalo.at[1], 1, (d - 1, p))
     r_up = halo(rsend.at[1], rhalo.at[0], 2, (d, p + 1))
     r_down = halo(rsend.at[0], rhalo.at[1], 3, (d, p - 1))
     lands = (zhalo.at[0], zhalo.at[1], rhalo.at[0], rhalo.at[1])
@@ -161,36 +171,43 @@
         def _(land=land):
             land[...] = jnp.zeros(land.shape, F32)
 
+    row_id = lax.broadcasted_iota(jnp.int32, (ROWS, NX), 0)
+    lane_id = lax.broadcasted_iota(jnp.int32, (ROWS, HALF), 1)
+    field = [own[0], own[1]]
+    middle = flux(field[1] - field[0])
+    for layer in range(2):
+        centre = field[layer]
+        bend = -middle if layer else middle
+        inner_flux = flux(pltpu.roll(centre, 1, 0) - centre)
+        bend = bend + jnp.where(row_id == 0, 0.0, inner_flux)
+        bend = bend - jnp.where(row_id == ROWS - 1, 0.0, pltpu.roll(inner_flux, ROWS - 1, 0))
+        sides = centre[:, :HALF], centre[:, HALF:]
+        across = []
+        for side in range(2):
+            here = sides[side]
+            inside = jnp.where(lane_id == 0, sides[1 - side], pltpu.roll(here, 1, 1))
+            inner_flux = flux(inside - here)
+            outside = jnp.where(lane_id == HALF - 1, flux(here), pltpu.roll(inner_flux, HALF - 1, 1))
+            across.append(inner_flux - outside)
+        bend = bend + jnp.concatenate(across, axis=1)
+        part_density[layer] = con_ref[layer] * (0.5 * (1.0 + jnp.tanh(centre))) + bend_weight * bend
+
     for copy, comes in zip(copies, gets):
         pl.when(comes)(copy.wait_recv)
-    row_id = lax.broadcasted_iota(jnp.int32, (ROWS, NX), 0)
-    col_id = lax.broadcasted_iota(jnp.int32, (ROWS, NX), 1)
-    field = [ls_ref[0], ls_ref[1]]
-    z_flux = [flux(field[0] - zhalo[0]), flux(field[1] - field[0]), flux(zhalo[1] - field[1])]
     even, odd = [], []
     for layer in range(2):
-        centre = field[layer]
-
-        def row_of(side):
-            parts = [
-                jnp.broadcast_to(rhalo[side, layer * 8 + k : layer * 8 + k + 1, :], (ROWS, 128)) for k in range(8)
-            ]
-            return jnp.concatenate(parts, axis=1)
-
-        bend = z_flux[layer + 1] - z_flux[layer]
-        above = jnp.where(row_id == 0, row_of(0), pltpu.roll(centre, 1, 0))
-        row_flux = flux(centre - above)
-        last = flux(row_of(1) - centre)
-        bend = bend + jnp.where(row_id == ROWS - 1, last, pltpu.roll(row_flux, ROWS - 1, 0)) - row_flux
-        before = jnp.where(col_id == 0, 0.0, pltpu.roll(centre, 1, 1))
-        col_flux = flux(centre - before)
-        bend = bend + jnp.where(col_id == NX - 1, flux(-centre), pltpu.roll(col_flux, NX - 1, 1)) - col_flux
-        density = con_ref[layer] * (0.5 * (1.0 + jnp.tanh(centre))) + bend_weight * bend
-        density = jnp.where(lower, flip(density, 0, ROWS), density)
-        left = flip_lanes(density[:, :HALF])
-        right = density[:, HALF:]
-        even.append(right + left)
-        odd.append(right - left)
+        centre = own[layer]
+        here = slice(layer * 8, layer * 8 + 8)
+        top = jnp.where(lower, rhalo[1, here, :], rhalo[0, here, :])
+        bottom = jnp.where(lower, rhalo[0, here, :], rhalo[1, here, :])
+        tops = [jnp.broadcast_to(top[k : k + 1], (ROWS, 128)) for k in range(8)]
+        bottoms = [jnp.broadcast_to(bottom[k : k + 1], (ROWS, 128)) for k in range(8)]
+        beside = jnp.where(row_id == 0, jnp.concatenate(tops, axis=1), jnp.concatenate(bottoms, axis=1))
+        outer_rows = (row_id == 0) | (row_id == ROWS - 1)
+        bend = flux(zhalo[layer] - centre) + jnp.where(outer_rows, flux(beside - centre), 0.0)
+        density = part_density[layer] + bend_weight * bend
+        even.append(density[:, :HALF] + density[:, HALF:])
+        odd.append(density[:, :HALF] - density[:, HALF:])
 
     block = jnp.where(lower, PLAN // 2 - 1 - p, p - PLAN // 2)
     half_lane = lax.broadcasted_iota(jnp.int32, (ROWS, 128), 1) < COEF
@@ -202,21 +219,23 @@
             device_id=at_q(other), device_id_type=MESH,
         )
 
-    for kind, pair in enumerate((even, odd)):
-        coef = table_right(jnp.concatenate(pair, axis=0), wide[kind, 0], wide[kind, 1])
-        for m in range(8):
-            first = coef[:ROWS, 128 * m : 128 * (m + 1)]
-            second = coef[ROWS:, 128 * m : 128 * (m + 1)]
-            spot = kind * 16 + 2 * m
-            csend[spot] = jnp.where(half_lane, first, pltpu.roll(second, COEF, 1))
-            csend[spot + 1] = jnp.where(half_lane, pltpu.roll(first, COEF, 1), second)
-
-        for k in range(16):
-            other = kind * 16 + lax.rem(q + k, 16)
-            if k == 0:
-                pl.when(other != q)(send_coef(other).start)
-            else:
-                send_coef(other).start()
+    for kind, folded in enumerate((even, odd)):
+        both = pair(jnp.concatenate(folded, axis=0))
+        for cut in range(2):
+            cols = slice(HALF * cut, HALF * (cut + 1))
+            coef = table_right(both, wide[kind, 0, :, cols], wide[kind, 1, :, cols])
+            start = kind * 16 + 8 * cut
+            for m in range(4):
+                first = coef[:ROWS, 128 * m : 128 * (m + 1)]
+                second = coef[ROWS:, 128 * m : 128 * (m + 1)]
+                csend[start + 2 * m] = jnp.where(half_lane, first, pltpu.roll(second, COEF, 1))
+                csend[start + 2 * m + 1] = jnp.where(half_lane, pltpu.roll(first, COEF, 1), second)
+            for k in range(8):
+                other = start + lax.rem(q + k, 8)
+                if k == 0:
+                    pl.when(other != q)(send_coef(other).start)
+                else:
+                    send_coef(other).start()
 
     def respond(first, count, is_sin):
         lane = lax.broadcasted_iota(jnp.int32, (count, 128), 1)
@@ -300,7 +319,13 @@
     cbuf[q] = xsend[q]
     pltpu.make_async_copy(cbuf.at[pl.ds(0, GROUP - 1)], cbuf.at[pl.ds(0, GROUP - 1)], xr).wait()
 
-    parity = []
+    def send_field(other):
+        return pltpu.make_async_remote_copy(
+            src_ref=gsend.at[other], dst_ref=gbuf.at[z], send_sem=gs, recv_sem=gr,
+            device_id=at_z(other), device_id_type=MESH,
+        )
+
+    pairs = []
     for kind in range(2):
         tops, bottoms = [], []
         for m in range(8):
@@ -308,34 +333,44 @@
             tops.append(jnp.where(half_lane, first, pltpu.roll(second, COEF, 1)))
             bottoms.append(jnp.where(half_lane, pltpu.roll(first, COEF, 1), second))
         value = jnp.concatenate([jnp.concatenate(tops, axis=1), jnp.concatenate(bottoms, axis=1)], axis=0)
-        parity.append(table_right(value, tall[kind, 0], tall[kind, 1]))
-    plus = parity[0] + parity[1]
-    minus = parity[0] - parity[1]
-    for other in range(RING):
-        rows = slice(ROWS * (other // DEPTH), ROWS * (other // DEPTH + 1))
-        col = other % DEPTH
-        if col >= 4:
-            gsend[other] = plus[rows, 128 * (col - 4) : 128 * (col - 3)]
-        else:
-            gsend[other] = minus[rows, 128 * (3 - col) : 128 * (4 - col)]
-
-    def send_field(other):
-        return pltpu.make_async_remote_copy(
-            src_ref=gsend.at[other], dst_ref=gbuf.at[z], send_sem=gs, recv_sem=gr,
-            device_id=at_z(other), device_id_type=MESH,
-        )
-
-    for k in range(RING - 1):
-        away = 8 + (k + 1) // 2 * (1 - 2 * (k % 2))
-        send_field(lax.rem(z + away, RING)).start()
+        pairs.append(pair(value))
+    for cut in range(2):
+        cols = slice(256 * cut, 256 * (cut + 1))
+        parity = [table_right(pairs[kind], tall[kind, 0, :, cols], tall[kind, 1, :, cols]) for kind in range(2)]
+        plus = parity[0] + parity[1]
+        minus = parity[0] - parity[1]
+        for half in range(2):
+            rows = slice(ROWS * half, ROWS * (half + 1))
+            for n in range(2):
+                lanes = slice(128 * n, 128 * (n + 1))
+                gsend[DEPTH * half + 4 + 2 * cut + n] = plus[rows, lanes]
+                gsend[DEPTH * half + 3 - 2 * cut - n] = minus[rows, lanes]
+        for k in range(8):
+            turn = lax.rem(z + k, 8)
+            other = DEPTH * lax.div(turn, 4) + lax.rem(2 + 4 * cut + lax.rem(turn, 4), DEPTH)
+            pl.when(other != z)(send_field(other).start)
 
     gbuf[z] = gsend[z]
     pltpu.make_async_copy(gbuf.at[pl.ds(0, RING - 1)], gbuf.at[pl.ds(0, RING - 1)], gr).wait()
     total = gbuf[0]
     for other in range(1, RING):
         total = total + gbuf[other]
-    total = jnp.where(d < DEPTH // 2, flip(total, 1, 128), total)
-    out_ref[...] = jnp.where(lower, flip(total, 0, ROWS), total)
+    across = lax.broadcasted_iota(jnp.int32, (128, 128), 0) + lax.broadcasted_iota(jnp.int32, (128, 128), 1)
+    reverse = jnp.where(across == 127, 1.0, 0.0).astype(BF16)
+    high, rest = split(total)
+    low = (total - high.astype(F32) - rest.astype(F32)).astype(BF16)
+    turned = matmul(jnp.concatenate([high, rest, low], axis=0), reverse)
+    turned = turned[:ROWS] + turned[ROWS : 2 * ROWS] + turned[2 * ROWS :]
+    total = jnp.where(d < DEPTH // 2, turned, total)
+
+    @pl.when(lower)
+    def _():
+        for row in range(ROWS):
+            out_ref[ROWS - 1 - row : ROWS - row, :] = total[row : row + 1]
+
+    @pl.when(jnp.logical_not(lower))
+    def _():
+        out_ref[...] = total
 
     for copy, there in zip(copies, has):
         pl.when(there)(copy.wait_send)
@@ -359,6 +394,8 @@
             scratch_shapes=[
                 pltpu.VMEM((2, ROWS, NX), F32),
                 pltpu.SMEM((2,), F32),
+                pltpu.VMEM((2, ROWS, NX), F32),
+                pltpu.VMEM((2, ROWS, NX), F32),
                 pltpu.VMEM((2, 2, HALF, NX), BF16),
                 pltpu.VMEM((2, 2, NX, HALF), BF16),
                 pltpu.VMEM((2, ROWS, NX), F32),

time: 53.7 us -> 55 us (1.024)
  Pallas kernels: 51.8 us -> 53.6 us
    pallas_call x1, Pallas kernels: 51.8 us -> 53.6 us  [step(): pl.pallas_call(kernel, out_shape=jax.ShapeDtypeStruct((ROWS, 128), F32),...]
where the time goes in v4:
time: 55 us; the launch traced here: 54.9 us
  Pallas kernels  53.6 us (97%)
  local copies, waits for them, and re-layouts  1.3 us (2%)
    pallas_call x1, Pallas kernels, step(): pl.pallas_call(kernel, out_shape=jax.ShapeDtypeStruct((ROWS, 128), F32),...  53.6 us
    unnamed x1, local copies, waits for them, and re-layouts  1.3 us

profile of v4, /device:TPU:1, one launch (start us, length us, event | category | flops | bytes accessed | tf_op | source)
XLA Modules:
  0.0 54.9 jit_solution(1774007085694618122)
XLA Ops:
  0.0 53.6 %shard_map.46 = f32[16,128]{1,0:T(8,128)} custom-call(f32[2,16,1024]{2,1,0:T(8,128)} %ls_hbm.1, f32[2]{0:T(128)} %con_hbm.1, bf16[2,2,512,1024]{3,2,1,0:T(8,128)(2,1)} %constant.4.clone.wide_hbm, bf16[2,2,1024,512]{3,2,1,0:T(8,128)(2,1)} %constant.5.clone.tall_hbm), custom_call_target="tpu_custom_call" | custom-call | tf_op jit(solution)/shard_map/pallas_call | solution.py:389
  53.6 1.3 %copy.6 = f32[16,128]{1,0:T(8,128)} copy(f32[16,128]{1,0:T(8,128)} %shard_map.46) | data formatting | bytes 16384

commit v5 on v4

--- a/solution.py
+++ b/solution.py
@@ -85,7 +85,7 @@
 
 def kernel(
     ls_hbm, con_hbm, wide_hbm, tall_hbm, out_ref,
-    ls_ref, con_ref, own, part_density, wide, tall, zhalo, rsend, rhalo, csend, sbuf, sst, rsp, rsp_first, pst, phi, xsend, cbuf, gsend, gbuf,
+    ls_ref, con_ref, own, part_density, wide, tall, zhalo, rsend, rhalo, csend, sbuf, rsp, rsp_first, pst, xsend, cbuf, gsend, gbuf,
     ls_sem, con_sem, wide_sem, tall_sem, hs, hr, cs, cr, xs, xr, gs, gr,
 ):
     d = lax.axis_index("depth")
@@ -237,52 +237,39 @@
                 else:
                     send_coef(other).start()
 
-    def respond(first, count, is_sin):
-        lane = lax.broadcasted_iota(jnp.int32, (count, 128), 1)
-        row = lax.broadcasted_iota(jnp.int32, (count, 128), 0) + first
-        place = (q % (GROUP // 2)) * COEF + lane % COEF
+    def respond(start, is_sin):
+        row = lax.broadcasted_iota(jnp.int32, (128, 128), 0)
+        col = lax.broadcasted_iota(jnp.int32, (128, 128), 1) + start
+        place = lax.rem(q, GROUP // 2) * COEF + lax.rem(row, COEF)
         v = jnp.where((place == 0) & (q >= GROUP // 2), NX, place).astype(F32)
         scale = 2.0 * math.pi * grav_scale * thickness / (4.0 * NX * NX)
-        weight = jnp.where(place == 0, scale, 2.0 * scale) * jnp.where(row == 0, 1.0, 2.0)
-        layer = (2 * d + lane // COEF).astype(F32)
+        weight = jnp.where(place == 0, scale, 2.0 * scale) * jnp.where(col == 0, 1.0, 2.0)
+        layer = (2 * d + lax.div(row, COEF)).astype(F32)
         rate = (top_depth + (layer + 0.5) * thickness) * (-2.0 * math.pi / (2 * NX))
-        u = (jnp.where(row == 0, NX, row) if is_sin else row).astype(F32)
+        u = (jnp.where(col == 0, NX, col) if is_sin else col).astype(F32)
         return jnp.exp(jnp.sqrt(u * u + v * v) * rate) * weight
 
-    @pl.loop(0, NX // 256)
-    def _(k):
-        rsp[pl.ds(pl.multiple_of(256 * k, 256), 256), :] = respond(256 * k, 256, False)
-
-    rsp_first[...] = respond(0, 8, True)
+    rsp_first[...] = respond(0, True)
+    for k in range(NX // 128):
+        rsp[:, 128 * k : 128 * (k + 1)] = respond(128 * k, False)
 
     sbuf[block] = csend[q]
     pltpu.make_async_copy(sbuf.at[pl.ds(0, GROUP - 1)], sbuf.at[pl.ds(0, GROUP - 1)], cr).wait()
 
-    for b in range(GROUP):
-        value = sbuf[b]
-        high, low = split(value)
-        sst[0, ROWS * b : ROWS * (b + 1), :128] = high
-        sst[0, ROWS * b : ROWS * (b + 1), 128:] = low
-        sign = jnp.where((b // 2) % 2 == zh, 1.0, -1.0)
-        high, low = split(value * sign)
-        sst[1, ROWS * b : ROWS * (b + 1), :128] = high
-        sst[1, ROWS * b : ROWS * (b + 1), 128:] = low
     tall_copy.wait()
+    value = sbuf[...].reshape(HALF, 128).T
+    side = lax.rem(lax.div(lax.broadcasted_iota(jnp.int32, (128, HALF), 1), 2 * ROWS), 2)
     step = 256
-    wide_half = lax.broadcasted_iota(jnp.int32, (step, 128), 1) < COEF
     for kind in range(2):
+        both = pair(jnp.where(side == zh, value, -value) if kind else value)
         for k in range(NX // step):
             here = slice(k * step, (k + 1) * step)
-            both = matmul(tall[kind, 0, here, :], sst[kind])
-            value = both[:, :128] + both[:, 128:] + matmul(tall[kind, 1, here, :], sst[kind, :, :128])
-            factor = rsp[here, :]
+            coef = table_right(both, wide[kind, 0, :, here], wide[kind, 1, :, here])
+            factor = rsp[:, here]
             if kind == 1 and k == 0:
-                factor = jnp.concatenate([rsp_first[...], factor[8:]], axis=0)
-            value = value * factor
-            value = value + pltpu.roll(value, COEF, 1)
-            high = value.astype(BF16).astype(F32)
-            pst[kind, here, :] = jnp.where(wide_half, high, value - high).astype(BF16)
-            phi[kind, here, :] = jnp.where(wide_half, high, 0.0).astype(BF16)
+                factor = jnp.concatenate([rsp_first[...], factor[:, 128:]], axis=1)
+            coef = coef * factor
+            pst[kind, :, here] = pair(coef[:COEF] + coef[COEF:])
 
     def send_rows(other):
         return pltpu.make_async_remote_copy(
@@ -291,21 +278,17 @@
         )
 
     for part in range(2):
-        cut = slice(256 * part, 256 * (part + 1))
-        parity = []
-        for kind in range(2):
-            value = matmul(wide[kind, 0, cut, :], pst[kind]) + matmul(wide[kind, 1, cut, :], phi[kind])
-            parity.append(value + pltpu.roll(value, COEF, 1))
-        plus = parity[0] + parity[1]
-        minus = parity[0] - parity[1]
+        cols = slice(256 * part, 256 * (part + 1))
+        parity = [table_right(pst[kind], tall[kind, 0, :, cols], tall[kind, 1, :, cols]) for kind in range(2)]
+        value = jnp.concatenate([parity[0] + parity[1], parity[0] - parity[1]], axis=0).T
         for g in range(4):
-            up = [plus[ROWS * (4 * g + n) : ROWS * (4 * g + n + 1)] for n in range(4)]
-            down = [minus[ROWS * (4 * g + n) : ROWS * (4 * g + n + 1)] for n in range(4)]
+            plain = [value[ROWS * (4 * g + n) : ROWS * (4 * g + n + 1)] for n in range(4)]
+            turned = [pltpu.roll(block_now, COEF, 1) for block_now in plain]
             chunk = 4 * part + g
-            xsend[2 * (8 + chunk)] = jnp.where(half_lane, up[0], up[2])
-            xsend[2 * (8 + chunk) + 1] = jnp.where(half_lane, up[1], up[3])
-            xsend[2 * (7 - chunk)] = jnp.where(half_lane, down[3], down[1])
-            xsend[2 * (7 - chunk) + 1] = jnp.where(half_lane, down[2], down[0])
+            xsend[2 * (8 + chunk)] = jnp.where(half_lane, plain[0], turned[2])
+            xsend[2 * (8 + chunk) + 1] = jnp.where(half_lane, plain[1], turned[3])
+            xsend[2 * (7 - chunk)] = jnp.where(half_lane, turned[3], plain[1])
+            xsend[2 * (7 - chunk) + 1] = jnp.where(half_lane, turned[2], plain[0])
 
         for k in range(16):
             spot = lax.rem(q + k, 16)
@@ -346,9 +329,12 @@
                 gsend[DEPTH * half + 4 + 2 * cut + n] = plus[rows, lanes]
                 gsend[DEPTH * half + 3 - 2 * cut - n] = minus[rows, lanes]
         for k in range(8):
-            turn = lax.rem(z + k, 8)
+            turn = lax.rem(4 * zh + lax.rem(d + 2, 4) + k, 8)
             other = DEPTH * lax.div(turn, 4) + lax.rem(2 + 4 * cut + lax.rem(turn, 4), DEPTH)
-            pl.when(other != z)(send_field(other).start)
+            if k == 0:
+                pl.when(other != z)(send_field(other).start)
+            else:
+                send_field(other).start()
 
     gbuf[z] = gsend[z]
     pltpu.make_async_copy(gbuf.at[pl.ds(0, RING - 1)], gbuf.at[pl.ds(0, RING - 1)], gr).wait()
@@ -403,11 +389,9 @@
                 pltpu.VMEM((2, 16, 128), F32),
                 pltpu.VMEM((GROUP, ROWS, 128), F32),
                 pltpu.VMEM((GROUP, ROWS, 128), F32),
-                pltpu.VMEM((2, HALF, 256), BF16),
-                pltpu.VMEM((NX, 128), F32),
-                pltpu.VMEM((8, 128), F32),
-                pltpu.VMEM((2, NX, 128), BF16),
-                pltpu.VMEM((2, NX, 128), BF16),
+                pltpu.VMEM((128, NX), F32),
+                pltpu.VMEM((128, 128), F32),
+                pltpu.VMEM((2, 128, NX), BF16),
                 pltpu.VMEM((GROUP, ROWS, 128), F32),
                 pltpu.VMEM((GROUP, ROWS, 128), F32),
                 pltpu.VMEM((RING, ROWS, 128), F32),

time: 55 us -> 55.2 us (level)
  no operation moved by 1% of the time
where the time goes in v5:
time: 55.2 us; the launch traced here: 55 us
  Pallas kernels  53.7 us (97%)
  local copies, waits for them, and re-layouts  1.3 us (2%)
    pallas_call x1, Pallas kernels, step(): pl.pallas_call(kernel, out_shape=jax.ShapeDtypeStruct((ROWS, 128), F32),...  53.7 us
    unnamed x1, local copies, waits for them, and re-layouts  1.3 us

profile of v5, /device:TPU:1, one launch (start us, length us, event | category | flops | bytes accessed | tf_op | source)
XLA Modules:
  0.0 55.0 jit_solution(12985106793083122734)
XLA Ops:
  0.0 53.7 %shard_map.46 = f32[16,128]{1,0:T(8,128)} custom-call(f32[2,16,1024]{2,1,0:T(8,128)} %ls_hbm.1, f32[2]{0:T(128)} %con_hbm.1, bf16[2,2,512,1024]{3,2,1,0:T(8,128)(2,1)} %constant.4.clone.wide_hbm, bf16[2,2,1024,512]{3,2,1,0:T(8,128)(2,1)} %constant.5.clone.tall_hbm), custom_call_target="tpu_custom_call" | custom-call | tf_op jit(solution)/shard_map/pallas_call | solution.py:375
  53.7 1.3 %copy.6 = f32[16,128]{1,0:T(8,128)} copy(f32[16,128]{1,0:T(8,128)} %shard_map.46) | data formatting | bytes 16384

commit v6 on v5

--- a/solution.py
+++ b/solution.py
@@ -33,12 +33,15 @@
 def basis():
     j = np.arange(HALF, dtype=np.float64)[:, None] + 0.5
     v = np.arange(NX, dtype=np.float64)[None, :]
-    v_sin = np.where(v == 0, float(NX), v)
-    both = np.stack([np.cos(np.pi * v * j / NX), np.sin(np.pi * v_sin * j / NX)])
-    high = both.astype(ml_dtypes.bfloat16)
-    low = (both - high.astype(np.float64)).astype(ml_dtypes.bfloat16)
-    wide = np.stack([high, low], axis=1)
-    return wide, np.ascontiguousarray(np.swapaxes(wide, 2, 3))
+    table = np.cos(np.pi * v * j / NX)
+    high = table.astype(ml_dtypes.bfloat16)
+    low = (table - high.astype(np.float64)).astype(ml_dtypes.bfloat16)
+    wide = np.stack([high, low])
+    return wide, np.ascontiguousarray(np.swapaxes(wide, 1, 2))
+
+
+def alternating(shape):
+    return 1.0 - 2.0 * lax.rem(lax.broadcasted_iota(jnp.int32, shape, 1), 2).astype(F32)
 
 
 def flux(step):
@@ -85,7 +88,7 @@
 
 def kernel(
     ls_hbm, con_hbm, wide_hbm, tall_hbm, out_ref,
-    ls_ref, con_ref, own, part_density, wide, tall, zhalo, rsend, rhalo, csend, sbuf, rsp, rsp_first, pst, xsend, cbuf, gsend, gbuf,
+    ls_ref, con_ref, own, part_density, wide, tall, zhalo, rsend, rhalo, csend, sbuf, rsp, pst, xsend, cbuf, gsend, gbuf,
     ls_sem, con_sem, wide_sem, tall_sem, hs, hr, cs, cr, xs, xr, gs, gr,
 ):
     d = lax.axis_index("depth")
@@ -106,10 +109,10 @@
     con_copy = pltpu.make_async_copy(con_hbm, con_ref, con_sem)
     ls_copy.start()
     con_copy.start()
-    wide_copy = pltpu.make_async_copy(wide_hbm, wide, wide_sem)
-    tall_copy = pltpu.make_async_copy(tall_hbm, tall, tall_sem)
-    wide_copy.start()
-    tall_copy.start()
+    wide_copies = [pltpu.make_async_copy(wide_hbm.at[n], wide.at[n], wide_sem.at[n]) for n in range(2)]
+    tall_copies = [pltpu.make_async_copy(tall_hbm.at[n], tall.at[n], tall_sem.at[n]) for n in range(2)]
+    for copy in wide_copies:
+        copy.start()
 
     barrier = pltpu.get_barrier_semaphore()
 
@@ -165,6 +168,8 @@
     copies = (z_up, z_down, r_up, r_down)
     for copy, there in zip(copies, has):
         pl.when(there)(copy.start)
+    for copy in tall_copies:
+        copy.start()
     for land, comes in zip(lands, gets):
 
         @pl.when(jnp.logical_not(comes))
@@ -207,11 +212,12 @@
         bend = flux(zhalo[layer] - centre) + jnp.where(outer_rows, flux(beside - centre), 0.0)
         density = part_density[layer] + bend_weight * bend
         even.append(density[:, :HALF] + density[:, HALF:])
-        odd.append(density[:, :HALF] - density[:, HALF:])
+        odd.append((density[:, :HALF] - density[:, HALF:]) * alternating((ROWS, HALF)))
 
     block = jnp.where(lower, PLAN // 2 - 1 - p, p - PLAN // 2)
     half_lane = lax.broadcasted_iota(jnp.int32, (ROWS, 128), 1) < COEF
-    wide_copy.wait()
+    for copy in wide_copies:
+        copy.wait()
 
     def send_coef(other):
         return pltpu.make_async_remote_copy(
@@ -219,15 +225,15 @@
             device_id=at_q(other), device_id_type=MESH,
         )
 
-    for kind, folded in enumerate((even, odd)):
-        both = pair(jnp.concatenate(folded, axis=0))
-        for cut in range(2):
-            cols = slice(HALF * cut, HALF * (cut + 1))
-            coef = table_right(both, wide[kind, 0, :, cols], wide[kind, 1, :, cols])
+    both = pair(jnp.concatenate(even + odd, axis=0))
+    for cut in range(2):
+        cols = slice(HALF * cut, HALF * (cut + 1))
+        coef = table_right(both, wide[0, :, cols], wide[1, :, cols])
+        for kind in range(2):
             start = kind * 16 + 8 * cut
             for m in range(4):
-                first = coef[:ROWS, 128 * m : 128 * (m + 1)]
-                second = coef[ROWS:, 128 * m : 128 * (m + 1)]
+                first = coef[2 * ROWS * kind : 2 * ROWS * kind + ROWS, 128 * m : 128 * (m + 1)]
+                second = coef[2 * ROWS * kind + ROWS : 2 * ROWS * (kind + 1), 128 * m : 128 * (m + 1)]
                 csend[start + 2 * m] = jnp.where(half_lane, first, pltpu.roll(second, COEF, 1))
                 csend[start + 2 * m + 1] = jnp.where(half_lane, pltpu.roll(first, COEF, 1), second)
             for k in range(8):
@@ -241,35 +247,34 @@
         row = lax.broadcasted_iota(jnp.int32, (128, 128), 0)
         col = lax.broadcasted_iota(jnp.int32, (128, 128), 1) + start
         place = lax.rem(q, GROUP // 2) * COEF + lax.rem(row, COEF)
-        v = jnp.where((place == 0) & (q >= GROUP // 2), NX, place).astype(F32)
+        v = jnp.where(q >= GROUP // 2, NX - place, place).astype(F32)
         scale = 2.0 * math.pi * grav_scale * thickness / (4.0 * NX * NX)
         weight = jnp.where(place == 0, scale, 2.0 * scale) * jnp.where(col == 0, 1.0, 2.0)
         layer = (2 * d + lax.div(row, COEF)).astype(F32)
         rate = (top_depth + (layer + 0.5) * thickness) * (-2.0 * math.pi / (2 * NX))
-        u = (jnp.where(col == 0, NX, col) if is_sin else col).astype(F32)
+        u = (NX - col if is_sin else col).astype(F32)
         return jnp.exp(jnp.sqrt(u * u + v * v) * rate) * weight
 
-    rsp_first[...] = respond(0, True)
-    for k in range(NX // 128):
-        rsp[:, 128 * k : 128 * (k + 1)] = respond(128 * k, False)
+    for kind in range(2):
+        for k in range(NX // 128):
+            rsp[128 * kind : 128 * (kind + 1), 128 * k : 128 * (k + 1)] = respond(128 * k, kind == 1)
 
     sbuf[block] = csend[q]
     pltpu.make_async_copy(sbuf.at[pl.ds(0, GROUP - 1)], sbuf.at[pl.ds(0, GROUP - 1)], cr).wait()
 
-    tall_copy.wait()
+    for copy in tall_copies:
+        copy.wait()
     value = sbuf[...].reshape(HALF, 128).T
     side = lax.rem(lax.div(lax.broadcasted_iota(jnp.int32, (128, HALF), 1), 2 * ROWS), 2)
+    value = jnp.concatenate([value, jnp.where(side == zh, value, -value) * alternating((128, HALF))], axis=0)
+    both = pair(value)
     step = 256
-    for kind in range(2):
-        both = pair(jnp.where(side == zh, value, -value) if kind else value)
-        for k in range(NX // step):
-            here = slice(k * step, (k + 1) * step)
-            coef = table_right(both, wide[kind, 0, :, here], wide[kind, 1, :, here])
-            factor = rsp[:, here]
-            if kind == 1 and k == 0:
-                factor = jnp.concatenate([rsp_first[...], factor[:, 128:]], axis=1)
-            coef = coef * factor
-            pst[kind, :, here] = pair(coef[:COEF] + coef[COEF:])
+    for k in range(NX // step):
+        here = slice(k * step, (k + 1) * step)
+        coef = table_right(both, wide[0, :, here], wide[1, :, here]) * rsp[:, here]
+        cosine = coef[:COEF] + coef[COEF : 2 * COEF]
+        sine = coef[2 * COEF : 3 * COEF] + coef[3 * COEF :]
+        pst[:, here] = pair(jnp.concatenate([cosine, sine], axis=0))
 
     def send_rows(other):
         return pltpu.make_async_remote_copy(
@@ -279,8 +284,9 @@
 
     for part in range(2):
         cols = slice(256 * part, 256 * (part + 1))
-        parity = [table_right(pst[kind], tall[kind, 0, :, cols], tall[kind, 1, :, cols]) for kind in range(2)]
-        value = jnp.concatenate([parity[0] + parity[1], parity[0] - parity[1]], axis=0).T
+        value = table_right(pst[...], tall[0, :, cols], tall[1, :, cols])
+        evens, odds = value[:COEF], value[COEF:] * alternating((COEF, 256))
+        value = jnp.concatenate([evens + odds, evens - odds], axis=0).T
         for g in range(4):
             plain = [value[ROWS * (4 * g + n) : ROWS * (4 * g + n + 1)] for n in range(4)]
             turned = [pltpu.roll(block_now, COEF, 1) for block_now in plain]
@@ -308,20 +314,21 @@
             device_id=at_z(other), device_id_type=MESH,
         )
 
-    pairs = []
+    values = []
     for kind in range(2):
         tops, bottoms = [], []
         for m in range(8):
             first, second = cbuf[kind * 16 + 2 * m], cbuf[kind * 16 + 2 * m + 1]
             tops.append(jnp.where(half_lane, first, pltpu.roll(second, COEF, 1)))
             bottoms.append(jnp.where(half_lane, pltpu.roll(first, COEF, 1), second))
-        value = jnp.concatenate([jnp.concatenate(tops, axis=1), jnp.concatenate(bottoms, axis=1)], axis=0)
-        pairs.append(pair(value))
+        values += [jnp.concatenate(tops, axis=1), jnp.concatenate(bottoms, axis=1)]
+    both = pair(jnp.concatenate(values, axis=0))
     for cut in range(2):
         cols = slice(256 * cut, 256 * (cut + 1))
-        parity = [table_right(pairs[kind], tall[kind, 0, :, cols], tall[kind, 1, :, cols]) for kind in range(2)]
-        plus = parity[0] + parity[1]
-        minus = parity[0] - parity[1]
+        value = table_right(both, tall[0, :, cols], tall[1, :, cols])
+        evens, odds = value[: 2 * ROWS], value[2 * ROWS :] * alternating((2 * ROWS, 256))
+        plus = evens + odds
+        minus = evens - odds
         for half in range(2):
             rows = slice(ROWS * half, ROWS * (half + 1))
             for n in range(2):
@@ -382,21 +389,20 @@
                 pltpu.SMEM((2,), F32),
                 pltpu.VMEM((2, ROWS, NX), F32),
                 pltpu.VMEM((2, ROWS, NX), F32),
-                pltpu.VMEM((2, 2, HALF, NX), BF16),
-                pltpu.VMEM((2, 2, NX, HALF), BF16),
+                pltpu.VMEM((2, HALF, NX), BF16),
+                pltpu.VMEM((2, NX, HALF), BF16),
                 pltpu.VMEM((2, ROWS, NX), F32),
                 pltpu.VMEM((2, 16, 128), F32),
                 pltpu.VMEM((2, 16, 128), F32),
                 pltpu.VMEM((GROUP, ROWS, 128), F32),
                 pltpu.VMEM((GROUP, ROWS, 128), F32),
-                pltpu.VMEM((128, NX), F32),
-                pltpu.VMEM((128, 128), F32),
-                pltpu.VMEM((2, 128, NX), BF16),
+                pltpu.VMEM((256, NX), F32),
+                pltpu.VMEM((256, NX), BF16),
                 pltpu.VMEM((GROUP, ROWS, 128), F32),
                 pltpu.VMEM((GROUP, ROWS, 128), F32),
                 pltpu.VMEM((RING, ROWS, 128), F32),
                 pltpu.VMEM((RING, ROWS, 128), F32),
-                dma(()), dma(()), dma(()), dma(()), dma((4,)), dma((4,)),
+                dma(()), dma(()), dma((2,)), dma((2,)), dma((4,)), dma((4,)),
                 dma(()), dma(()), dma(()), dma(()), dma(()), dma(()),
             ],
             compiler_params=pltpu.CompilerParams(

time: 55.2 us -> 54.8 us (level)
  no operation moved by 1% of the time
where the time goes in v6:
time: 54.8 us; the launch traced here: 54.6 us
  Pallas kernels  53.3 us (97%)
  local copies, waits for them, and re-layouts  1.3 us (2%)
    pallas_call x1, Pallas kernels, step(): pl.pallas_call(kernel, out_shape=jax.ShapeDtypeStruct((ROWS, 128), F32),...  53.3 us
    unnamed x1, local copies, waits for them, and re-layouts  1.3 us

profile of v6, /device:TPU:1, one launch (start us, length us, event | category | flops | bytes accessed | tf_op | source)
XLA Modules:
  0.0 54.6 jit_solution(18145250982023545126)
XLA Ops:
  0.0 53.3 %shard_map.46 = f32[16,128]{1,0:T(8,128)} custom-call(f32[2,16,1024]{2,1,0:T(8,128)} %ls_hbm.1, f32[2]{0:T(128)} %con_hbm.1, bf16[2,512,1024]{2,1,0:T(8,128)(2,1)} %constant.4.clone.wide_hbm, bf16[2,1024,512]{2,1,0:T(8,128)(2,1)} %constant.5.clone.tall_hbm), custom_call_target="tpu_custom_call" | custom-call | tf_op jit(solution)/shard_map/pallas_call | solution.py:382
  53.3 1.3 %copy.6 = f32[16,128]{1,0:T(8,128)} copy(f32[16,128]{1,0:T(8,128)} %shard_map.46) | data formatting | bytes 16384

commit v7 on v6

--- a/solution.py
+++ b/solution.py
@@ -276,10 +276,13 @@
         sine = coef[2 * COEF : 3 * COEF] + coef[3 * COEF :]
         pst[:, here] = pair(jnp.concatenate([cosine, sine], axis=0))
 
-    def send_rows(other):
+    parity = lax.rem(d, 2)
+    mate = d + 1 - 2 * parity
+
+    def send_rows(member, depth, other):
         return pltpu.make_async_remote_copy(
-            src_ref=xsend.at[other], dst_ref=cbuf.at[q], send_sem=xs, recv_sem=xr,
-            device_id=at_q(other), device_id_type=MESH,
+            src_ref=xsend.at[GROUP * member + other], dst_ref=cbuf.at[GROUP * parity + q], send_sem=xs, recv_sem=xr,
+            device_id=(depth, at_q(other)[1]), device_id_type=MESH,
         )
 
     for part in range(2):
@@ -291,22 +294,27 @@
             plain = [value[ROWS * (4 * g + n) : ROWS * (4 * g + n + 1)] for n in range(4)]
             turned = [pltpu.roll(block_now, COEF, 1) for block_now in plain]
             chunk = 4 * part + g
-            xsend[2 * (8 + chunk)] = jnp.where(half_lane, plain[0], turned[2])
-            xsend[2 * (8 + chunk) + 1] = jnp.where(half_lane, plain[1], turned[3])
-            xsend[2 * (7 - chunk)] = jnp.where(half_lane, turned[3], plain[1])
-            xsend[2 * (7 - chunk) + 1] = jnp.where(half_lane, turned[2], plain[0])
+            for spot, block_now in (
+                (2 * (8 + chunk), jnp.where(half_lane, plain[0], turned[2])),
+                (2 * (8 + chunk) + 1, jnp.where(half_lane, plain[1], turned[3])),
+                (2 * (7 - chunk), jnp.where(half_lane, turned[3], plain[1])),
+                (2 * (7 - chunk) + 1, jnp.where(half_lane, turned[2], plain[0])),
+            ):
+                xsend[spot] = block_now[:8]
+                xsend[GROUP + spot] = block_now[8:]
 
         for k in range(16):
             spot = lax.rem(q + k, 16)
             upper = lax.div(spot, 8)
             other = spot + 16 * (upper if part else 1 - upper)
+            send_rows(1 - parity, mate, other).start()
             if k == 0:
-                pl.when(other != q)(send_rows(other).start)
+                pl.when(other != q)(send_rows(parity, d, other).start)
             else:
-                send_rows(other).start()
-
-    cbuf[q] = xsend[q]
-    pltpu.make_async_copy(cbuf.at[pl.ds(0, GROUP - 1)], cbuf.at[pl.ds(0, GROUP - 1)], xr).wait()
+                send_rows(parity, d, other).start()
+
+    cbuf[GROUP * parity + q] = xsend[GROUP * parity + q]
+    pltpu.make_async_copy(cbuf.at[pl.ds(0, 2 * GROUP - 1)], cbuf.at[pl.ds(0, 2 * GROUP - 1)], xr).wait()
 
     def send_field(other):
         return pltpu.make_async_remote_copy(
@@ -318,19 +326,21 @@
     for kind in range(2):
         tops, bottoms = [], []
         for m in range(8):
-            first, second = cbuf[kind * 16 + 2 * m], cbuf[kind * 16 + 2 * m + 1]
-            tops.append(jnp.where(half_lane, first, pltpu.roll(second, COEF, 1)))
-            bottoms.append(jnp.where(half_lane, pltpu.roll(first, COEF, 1), second))
+            spot = kind * 16 + 2 * m
+            first = cbuf[spot] + cbuf[GROUP + spot]
+            second = cbuf[spot + 1] + cbuf[GROUP + spot + 1]
+            tops.append(jnp.where(half_lane[:8], first, pltpu.roll(second, COEF, 1)))
+            bottoms.append(jnp.where(half_lane[:8], pltpu.roll(first, COEF, 1), second))
         values += [jnp.concatenate(tops, axis=1), jnp.concatenate(bottoms, axis=1)]
     both = pair(jnp.concatenate(values, axis=0))
     for cut in range(2):
         cols = slice(256 * cut, 256 * (cut + 1))
         value = table_right(both, tall[0, :, cols], tall[1, :, cols])
-        evens, odds = value[: 2 * ROWS], value[2 * ROWS :] * alternating((2 * ROWS, 256))
+        evens, odds = value[:ROWS], value[ROWS:] * alternating((ROWS, 256))
         plus = evens + odds
         minus = evens - odds
         for half in range(2):
-            rows = slice(ROWS * half, ROWS * (half + 1))
+            rows = slice(8 * half, 8 * (half + 1))
             for n in range(2):
                 lanes = slice(128 * n, 128 * (n + 1))
                 gsend[DEPTH * half + 4 + 2 * cut + n] = plus[rows, lanes]
@@ -345,9 +355,10 @@
 
     gbuf[z] = gsend[z]
     pltpu.make_async_copy(gbuf.at[pl.ds(0, RING - 1)], gbuf.at[pl.ds(0, RING - 1)], gr).wait()
-    total = gbuf[0]
-    for other in range(1, RING):
-        total = total + gbuf[other]
+    totals = [gbuf[0], gbuf[1]]
+    for other in range(2, RING):
+        totals[other % 2] = totals[other % 2] + gbuf[other]
+    total = jnp.concatenate(totals, axis=0)
     across = lax.broadcasted_iota(jnp.int32, (128, 128), 0) + lax.broadcasted_iota(jnp.int32, (128, 128), 1)
     reverse = jnp.where(across == 127, 1.0, 0.0).astype(BF16)
     high, rest = split(total)
@@ -368,7 +379,7 @@
     for copy, there in zip(copies, has):
         pl.when(there)(copy.wait_send)
     pltpu.make_async_copy(csend.at[pl.ds(0, GROUP - 1)], csend.at[pl.ds(0, GROUP - 1)], cs).wait()
-    pltpu.make_async_copy(xsend.at[pl.ds(0, GROUP - 1)], xsend.at[pl.ds(0, GROUP - 1)], xs).wait()
+    pltpu.make_async_copy(xsend.at[pl.ds(0, 2 * GROUP - 1)], xsend.at[pl.ds(0, 2 * GROUP - 1)], xs).wait()
     pltpu.make_async_copy(gsend.at[pl.ds(0, RING - 1)], gsend.at[pl.ds(0, RING - 1)], gs).wait()
 
 
@@ -398,10 +409,10 @@
                 pltpu.VMEM((GROUP, ROWS, 128), F32),
                 pltpu.VMEM((256, NX), F32),
                 pltpu.VMEM((256, NX), BF16),
-                pltpu.VMEM((GROUP, ROWS, 128), F32),
-                pltpu.VMEM((GROUP, ROWS, 128), F32),
-                pltpu.VMEM((RING, ROWS, 128), F32),
-                pltpu.VMEM((RING, ROWS, 128), F32),
+                pltpu.VMEM((2 * GROUP, 8, 128), F32),
+                pltpu.VMEM((2 * GROUP, 8, 128), F32),
+                pltpu.VMEM((RING, 8, 128), F32),
+                pltpu.VMEM((RING, 8, 128), F32),
                 dma(()), dma(()), dma((2,)), dma((2,)), dma((4,)), dma((4,)),
                 dma(()), dma(()), dma(()), dma(()), dma(()), dma(()),
             ],

time: 54.8 us -> 52.4 us (0.956)
  Pallas kernels: 53.3 us -> 50.9 us
    pallas_call x1, Pallas kernels: 53.3 us -> 50.9 us  [step(): pl.pallas_call(kernel, out_shape=jax.ShapeDtypeStruct((ROWS, 128), F32),...]
where the time goes in v7:
time: 52.4 us; the launch traced here: 52.2 us
  Pallas kernels  50.9 us (97%)
  local copies, waits for them, and re-layouts  1.3 us (2%)
    pallas_call x1, Pallas kernels, step(): pl.pallas_call(kernel, out_shape=jax.ShapeDtypeStruct((ROWS, 128), F32),...  50.9 us
    unnamed x1, local copies, waits for them, and re-layouts  1.3 us

profile of v7, /device:TPU:1, one launch (start us, length us, event | category | flops | bytes accessed | tf_op | source)
XLA Modules:
  0.0 52.2 jit_solution(6426532161321156722)
XLA Ops:
  0.0 50.9 %shard_map.46 = f32[16,128]{1,0:T(8,128)} custom-call(f32[2,16,1024]{2,1,0:T(8,128)} %ls_hbm.1, f32[2]{0:T(128)} %con_hbm.1, bf16[2,512,1024]{2,1,0:T(8,128)(2,1)} %constant.4.clone.wide_hbm, bf16[2,1024,512]{2,1,0:T(8,128)(2,1)} %constant.5.clone.tall_hbm), custom_call_target="tpu_custom_call" | custom-call | tf_op jit(solution)/shard_map/pallas_call | solution.py:393
  50.9 1.3 %copy.6 = f32[16,128]{1,0:T(8,128)} copy(f32[16,128]{1,0:T(8,128)} %shard_map.46) | data formatting | bytes 16384

commit v8 on v7

--- a/solution.py
+++ b/solution.py
@@ -23,6 +23,7 @@
 GROUP = 32
 RING = 16
 COEF = 2 * NX // GROUP
+SHARE = COEF // 2
 
 bend_weight = 0.5
 grav_scale = 0.05
@@ -37,7 +38,8 @@
     high = table.astype(ml_dtypes.bfloat16)
     low = (table - high.astype(np.float64)).astype(ml_dtypes.bfloat16)
     wide = np.stack([high, low])
-    return wide, np.ascontiguousarray(np.swapaxes(wide, 1, 2))
+    order = np.arange(HALF).reshape(GROUP, 2, ROWS // 2).transpose(1, 0, 2).reshape(-1)
+    return wide, np.ascontiguousarray(wide[:, order]), np.ascontiguousarray(np.swapaxes(wide, 1, 2))
 
 
 def alternating(shape):
@@ -86,10 +88,22 @@
     return product[:n] + product[n:] + matmul(both[:n], low_table)
 
 
+def regroup(parts):
+    lane = lax.broadcasted_iota(jnp.int32, parts[0].shape, 1)
+    early, even = lane < 64, lax.rem(lane, 64) < 32
+    wide = [jnp.where(early, parts[g], pltpu.roll(parts[g + 2], 64, 1)) for g in range(2)]
+    wide += [jnp.where(early, pltpu.roll(parts[g], 64, 1), parts[g + 2]) for g in range(2)]
+    out = []
+    for first, second in (wide[:2], wide[2:]):
+        out.append(jnp.where(even, first, pltpu.roll(second, 32, 1)))
+        out.append(jnp.where(even, pltpu.roll(first, 96, 1), second))
+    return out
+
+
 def kernel(
-    ls_hbm, con_hbm, wide_hbm, tall_hbm, out_ref,
-    ls_ref, con_ref, own, part_density, wide, tall, zhalo, rsend, rhalo, csend, sbuf, rsp, pst, xsend, cbuf, gsend, gbuf,
-    ls_sem, con_sem, wide_sem, tall_sem, hs, hr, cs, cr, xs, xr, gs, gr,
+    ls_hbm, con_hbm, wide_hbm, mixed_hbm, tall_hbm, out_ref,
+    ls_ref, con_ref, own, part_density, wide, mixed, tall, zhalo, rsend, rhalo, csend, sbuf, rsp, pst, xsend, cbuf, coefs, gsend, gbuf,
+    ls_sem, con_sem, wide_sem, mixed_sem, tall_sem, hs, hr, cs, cr, xs, xr, gs, gr,
 ):
     d = lax.axis_index("depth")
     p = lax.axis_index("plan")
@@ -110,6 +124,7 @@
     ls_copy.start()
     con_copy.start()
     wide_copies = [pltpu.make_async_copy(wide_hbm.at[n], wide.at[n], wide_sem.at[n]) for n in range(2)]
+    mixed_copies = [pltpu.make_async_copy(mixed_hbm.at[n], mixed.at[n], mixed_sem.at[n]) for n in range(2)]
     tall_copies = [pltpu.make_async_copy(tall_hbm.at[n], tall.at[n], tall_sem.at[n]) for n in range(2)]
     for copy in wide_copies:
         copy.start()
@@ -168,7 +183,7 @@
     copies = (z_up, z_down, r_up, r_down)
     for copy, there in zip(copies, has):
         pl.when(there)(copy.start)
-    for copy in tall_copies:
+    for copy in mixed_copies + tall_copies:
         copy.start()
     for land, comes in zip(lands, gets):
 
@@ -215,14 +230,15 @@
         odd.append((density[:, :HALF] - density[:, HALF:]) * alternating((ROWS, HALF)))
 
     block = jnp.where(lower, PLAN // 2 - 1 - p, p - PLAN // 2)
-    half_lane = lax.broadcasted_iota(jnp.int32, (ROWS, 128), 1) < COEF
+    parity = lax.rem(d, 2)
+    mate = d + 1 - 2 * parity
     for copy in wide_copies:
         copy.wait()
 
-    def send_coef(other):
+    def send_coef(member, depth, other):
         return pltpu.make_async_remote_copy(
-            src_ref=csend.at[other], dst_ref=sbuf.at[block], send_sem=cs, recv_sem=cr,
-            device_id=at_q(other), device_id_type=MESH,
+            src_ref=csend.at[2 * other + member], dst_ref=sbuf.at[GROUP * parity + block], send_sem=cs, recv_sem=cr,
+            device_id=(depth, at_q(other)[1]), device_id_type=MESH,
         )
 
     both = pair(jnp.concatenate(even + odd, axis=0))
@@ -232,25 +248,26 @@
         for kind in range(2):
             start = kind * 16 + 8 * cut
             for m in range(4):
-                first = coef[2 * ROWS * kind : 2 * ROWS * kind + ROWS, 128 * m : 128 * (m + 1)]
-                second = coef[2 * ROWS * kind + ROWS : 2 * ROWS * (kind + 1), 128 * m : 128 * (m + 1)]
-                csend[start + 2 * m] = jnp.where(half_lane, first, pltpu.roll(second, COEF, 1))
-                csend[start + 2 * m + 1] = jnp.where(half_lane, pltpu.roll(first, COEF, 1), second)
+                lanes = slice(128 * m, 128 * (m + 1))
+                starts = [2 * ROWS * kind + ROWS * layer + 8 * half for half in range(2) for layer in range(2)]
+                for t, value in enumerate(regroup([coef[n : n + 8, lanes] for n in starts])):
+                    csend[2 * start + 4 * m + t] = value
             for k in range(8):
                 other = start + lax.rem(q + k, 8)
+                send_coef(1 - parity, mate, other).start()
                 if k == 0:
-                    pl.when(other != q)(send_coef(other).start)
+                    pl.when(other != q)(send_coef(parity, d, other).start)
                 else:
-                    send_coef(other).start()
+                    send_coef(parity, d, other).start()
 
     def respond(start, is_sin):
         row = lax.broadcasted_iota(jnp.int32, (128, 128), 0)
         col = lax.broadcasted_iota(jnp.int32, (128, 128), 1) + start
-        place = lax.rem(q, GROUP // 2) * COEF + lax.rem(row, COEF)
+        place = lax.rem(q, GROUP // 2) * COEF + parity * SHARE + lax.rem(row, SHARE)
         v = jnp.where(q >= GROUP // 2, NX - place, place).astype(F32)
         scale = 2.0 * math.pi * grav_scale * thickness / (4.0 * NX * NX)
         weight = jnp.where(place == 0, scale, 2.0 * scale) * jnp.where(col == 0, 1.0, 2.0)
-        layer = (2 * d + lax.div(row, COEF)).astype(F32)
+        layer = (2 * (d - parity) + lax.div(row, SHARE)).astype(F32)
         rate = (top_depth + (layer + 0.5) * thickness) * (-2.0 * math.pi / (2 * NX))
         u = (NX - col if is_sin else col).astype(F32)
         return jnp.exp(jnp.sqrt(u * u + v * v) * rate) * weight
@@ -259,49 +276,60 @@
         for k in range(NX // 128):
             rsp[128 * kind : 128 * (kind + 1), 128 * k : 128 * (k + 1)] = respond(128 * k, kind == 1)
 
-    sbuf[block] = csend[q]
-    pltpu.make_async_copy(sbuf.at[pl.ds(0, GROUP - 1)], sbuf.at[pl.ds(0, GROUP - 1)], cr).wait()
-
-    for copy in tall_copies:
+    sbuf[GROUP * parity + block] = csend[2 * q + parity]
+    landed = sbuf.at[pl.ds(0, 2 * GROUP - 1)]
+    pltpu.make_async_copy(landed, landed, cr).wait()
+
+    for copy in mixed_copies + tall_copies:
         copy.wait()
-    value = sbuf[...].reshape(HALF, 128).T
-    side = lax.rem(lax.div(lax.broadcasted_iota(jnp.int32, (128, HALF), 1), 2 * ROWS), 2)
+    layers = []
+    for member in range(2):
+        value = sbuf[GROUP * member : GROUP * (member + 1)].reshape(HALF // 2, 128).T
+        layers.append(jnp.concatenate([value[:64], value[64:]], axis=1))
+    value = jnp.concatenate(layers, axis=0)
+    side = lax.rem(lax.div(lax.broadcasted_iota(jnp.int32, (128, HALF), 1), 16), 2)
     value = jnp.concatenate([value, jnp.where(side == zh, value, -value) * alternating((128, HALF))], axis=0)
     both = pair(value)
     step = 256
     for k in range(NX // step):
         here = slice(k * step, (k + 1) * step)
-        coef = table_right(both, wide[0, :, here], wide[1, :, here]) * rsp[:, here]
-        cosine = coef[:COEF] + coef[COEF : 2 * COEF]
-        sine = coef[2 * COEF : 3 * COEF] + coef[3 * COEF :]
+        coef = table_right(both, mixed[0, :, here], mixed[1, :, here]) * rsp[:, here]
+        parts = [coef[SHARE * n : SHARE * (n + 1)] for n in range(8)]
+        cosine = (parts[0] + parts[1]) + (parts[2] + parts[3])
+        sine = (parts[4] + parts[5]) + (parts[6] + parts[7])
         pst[:, here] = pair(jnp.concatenate([cosine, sine], axis=0))
-
-    parity = lax.rem(d, 2)
-    mate = d + 1 - 2 * parity
 
     def send_rows(member, depth, other):
         return pltpu.make_async_remote_copy(
-            src_ref=xsend.at[GROUP * member + other], dst_ref=cbuf.at[GROUP * parity + q], send_sem=xs, recv_sem=xr,
+            src_ref=xsend.at[2 * other + member], dst_ref=cbuf.at[2 * q + parity], send_sem=xs, recv_sem=xr,
             device_id=(depth, at_q(other)[1]), device_id_type=MESH,
         )
 
+    lane = lax.broadcasted_iota(jnp.int32, (8, 128), 1)
+    early, even_lane = lane < 64, lax.rem(lane, 64) < 32
     for part in range(2):
         cols = slice(256 * part, 256 * (part + 1))
         value = table_right(pst[...], tall[0, :, cols], tall[1, :, cols])
-        evens, odds = value[:COEF], value[COEF:] * alternating((COEF, 256))
-        value = jnp.concatenate([evens + odds, evens - odds], axis=0).T
+        evens, odds = value[:SHARE], value[SHARE:] * alternating((SHARE, 256))
+        plus, minus = evens + odds, evens - odds
+        value = jnp.concatenate([plus, minus, plus, minus], axis=0).T
         for g in range(4):
-            plain = [value[ROWS * (4 * g + n) : ROWS * (4 * g + n + 1)] for n in range(4)]
-            turned = [pltpu.roll(block_now, COEF, 1) for block_now in plain]
             chunk = 4 * part + g
-            for spot, block_now in (
-                (2 * (8 + chunk), jnp.where(half_lane, plain[0], turned[2])),
-                (2 * (8 + chunk) + 1, jnp.where(half_lane, plain[1], turned[3])),
-                (2 * (7 - chunk), jnp.where(half_lane, turned[3], plain[1])),
-                (2 * (7 - chunk) + 1, jnp.where(half_lane, turned[2], plain[0])),
-            ):
-                xsend[spot] = block_now[:8]
-                xsend[GROUP + spot] = block_now[8:]
+            for member in range(2):
+                ups, downs = [], []
+                for n in range(4):
+                    start = ROWS * (4 * g + n) + 8 * member
+                    rows = value[start : start + 8]
+                    later = pltpu.roll(rows, 4, 0)
+                    ups.append(jnp.where(even_lane, rows, pltpu.roll(later, 32, 1)))
+                    downs.append(jnp.where(even_lane, pltpu.roll(rows, 32, 1), later))
+                for spot, one, two in (
+                    (2 * (8 + chunk), ups[0], ups[2]),
+                    (2 * (8 + chunk) + 1, ups[1], ups[3]),
+                    (2 * (7 - chunk), downs[3], downs[1]),
+                    (2 * (7 - chunk) + 1, downs[2], downs[0]),
+                ):
+                    xsend[2 * spot + member] = jnp.where(early, one, two)[:4]
 
         for k in range(16):
             spot = lax.rem(q + k, 16)
@@ -313,8 +341,9 @@
             else:
                 send_rows(parity, d, other).start()
 
-    cbuf[GROUP * parity + q] = xsend[GROUP * parity + q]
-    pltpu.make_async_copy(cbuf.at[pl.ds(0, 2 * GROUP - 1)], cbuf.at[pl.ds(0, 2 * GROUP - 1)], xr).wait()
+    cbuf[2 * q + parity] = xsend[2 * q + parity]
+    landed = cbuf.at[pl.ds(0, 2 * GROUP - 1)]
+    pltpu.make_async_copy(landed, landed, xr).wait()
 
     def send_field(other):
         return pltpu.make_async_remote_copy(
@@ -322,17 +351,13 @@
             device_id=at_z(other), device_id_type=MESH,
         )
 
-    values = []
-    for kind in range(2):
-        tops, bottoms = [], []
-        for m in range(8):
-            spot = kind * 16 + 2 * m
-            first = cbuf[spot] + cbuf[GROUP + spot]
-            second = cbuf[spot + 1] + cbuf[GROUP + spot + 1]
-            tops.append(jnp.where(half_lane[:8], first, pltpu.roll(second, COEF, 1)))
-            bottoms.append(jnp.where(half_lane[:8], pltpu.roll(first, COEF, 1), second))
-        values += [jnp.concatenate(tops, axis=1), jnp.concatenate(bottoms, axis=1)]
-    both = pair(jnp.concatenate(values, axis=0))
+    for m in range(2 * NX // 128):
+        parts = regroup([cbuf[4 * m + t] for t in range(4)])
+        lanes = slice(128 * (m % 8), 128 * (m % 8 + 1))
+        for g in range(4):
+            start = ROWS * (m // 8) + 4 * g
+            coefs[start : start + 4, lanes] = parts[g]
+    both = pair(coefs[...])
     for cut in range(2):
         cols = slice(256 * cut, 256 * (cut + 1))
         value = table_right(both, tall[0, :, cols], tall[1, :, cols])
@@ -378,13 +403,13 @@
 
     for copy, there in zip(copies, has):
         pl.when(there)(copy.wait_send)
-    pltpu.make_async_copy(csend.at[pl.ds(0, GROUP - 1)], csend.at[pl.ds(0, GROUP - 1)], cs).wait()
+    pltpu.make_async_copy(csend.at[pl.ds(0, 2 * GROUP - 1)], csend.at[pl.ds(0, 2 * GROUP - 1)], cs).wait()
     pltpu.make_async_copy(xsend.at[pl.ds(0, 2 * GROUP - 1)], xsend.at[pl.ds(0, 2 * GROUP - 1)], xs).wait()
     pltpu.make_async_copy(gsend.at[pl.ds(0, RING - 1)], gsend.at[pl.ds(0, RING - 1)], gs).wait()
 
 
 def solution(mesh):
-    wide, tall = basis()
+    wide, mixed, tall = basis()
 
     def step(level_set, contrast):
         vmem = pl.BlockSpec(memory_space=pltpu.VMEM)
@@ -393,7 +418,7 @@
         return pl.pallas_call(
             kernel,
             out_shape=jax.ShapeDtypeStruct((ROWS, 128), F32),
-            in_specs=[anywhere] * 4,
+            in_specs=[anywhere] * 5,
             out_specs=vmem,
             scratch_shapes=[
                 pltpu.VMEM((2, ROWS, NX), F32),
@@ -401,25 +426,27 @@
                 pltpu.VMEM((2, ROWS, NX), F32),
                 pltpu.VMEM((2, ROWS, NX), F32),
                 pltpu.VMEM((2, HALF, NX), BF16),
+                pltpu.VMEM((2, HALF, NX), BF16),
                 pltpu.VMEM((2, NX, HALF), BF16),
                 pltpu.VMEM((2, ROWS, NX), F32),
                 pltpu.VMEM((2, 16, 128), F32),
                 pltpu.VMEM((2, 16, 128), F32),
-                pltpu.VMEM((GROUP, ROWS, 128), F32),
-                pltpu.VMEM((GROUP, ROWS, 128), F32),
-                pltpu.VMEM((256, NX), F32),
-                pltpu.VMEM((256, NX), BF16),
                 pltpu.VMEM((2 * GROUP, 8, 128), F32),
                 pltpu.VMEM((2 * GROUP, 8, 128), F32),
+                pltpu.VMEM((256, NX), F32),
+                pltpu.VMEM((128, NX), BF16),
+                pltpu.VMEM((2 * GROUP, 4, 128), F32),
+                pltpu.VMEM((2 * GROUP, 4, 128), F32),
+                pltpu.VMEM((2 * ROWS, NX), F32),
                 pltpu.VMEM((RING, 8, 128), F32),
                 pltpu.VMEM((RING, 8, 128), F32),
-                dma(()), dma(()), dma((2,)), dma((2,)), dma((4,)), dma((4,)),
+                dma(()), dma(()), dma((2,)), dma((2,)), dma((2,)), dma((4,)), dma((4,)),
                 dma(()), dma(()), dma(()), dma(()), dma(()), dma(()),
             ],
             compiler_params=pltpu.CompilerParams(
                 collective_id=0, has_side_effects=True, vmem_limit_bytes=63 * 1024 * 1024
             ),
-        )(level_set, contrast, jnp.asarray(wide), jnp.asarray(tall))
+        )(level_set, contrast, jnp.asarray(wide), jnp.asarray(mixed), jnp.asarray(tall))
 
     return jax.shard_map(
         step,

time: 52.4 us -> 51.9 us (level)
  no operation moved by 1% of the time
where the time goes in v8:
time: 51.9 us; the launch traced here: 51.7 us
  Pallas kernels  50.4 us (97%)
  local copies, waits for them, and re-layouts  1.3 us (3%)
    pallas_call x1, Pallas kernels, step(): pl.pallas_call(kernel, out_shape=jax.ShapeDtypeStruct((ROWS, 128), F32),...  50.4 us
    unnamed x1, local copies, waits for them, and re-layouts  1.3 us

profile of v8, /device:TPU:1, one launch (start us, length us, event | category | flops | bytes accessed | tf_op | source)
XLA Modules:
  0.0 51.7 jit_solution(194002564523191846)
XLA Ops:
  0.0 50.4 %shard_map.55 = f32[16,128]{1,0:T(8,128)} custom-call(f32[2,16,1024]{2,1,0:T(8,128)} %ls_hbm.1, f32[2]{0:T(128)} %con_hbm.1, bf16[2,512,1024]{2,1,0:T(8,128)(2,1)} %constant.6.clone.wide_hbm, bf16[2,512,1024]{2,1,0:T(8,128)(2,1)} %constant.7.clone.mixed_hbm, bf16[2,1024,512]{2,1,0:T(8,128)(2,1)} %constant.8.clone.tall_hbm), custom_call_target="tpu_custom_call" | custom-call | tf_op jit(solution)/shard_map/pallas_call | solution.py:418
  50.4 1.3 %copy.7 = f32[16,128]{1,0:T(8,128)} copy(f32[16,128]{1,0:T(8,128)} %shard_map.55) | data formatting | bytes 16384

commit v9 on v8

--- a/solution.py
+++ b/solution.py
@@ -102,7 +102,7 @@
 
 def kernel(
     ls_hbm, con_hbm, wide_hbm, mixed_hbm, tall_hbm, out_ref,
-    ls_ref, con_ref, own, part_density, wide, mixed, tall, zhalo, rsend, rhalo, csend, sbuf, rsp, pst, xsend, cbuf, coefs, gsend, gbuf,
+    ls_ref, con_ref, own, part_density, wide, mixed, tall, zhalo, rsend, rhalo, csend, sbuf, rsp, acc, pst, xsend, cbuf, coefs, gsend, gbuf,
     ls_sem, con_sem, wide_sem, mixed_sem, tall_sem, hs, hr, cs, cr, xs, xr, gs, gr,
 ):
     d = lax.axis_index("depth")
@@ -113,8 +113,9 @@
     z = zh * DEPTH + d
     lower = p < PLAN // 2
 
-    def at_q(other):
-        return (d, lax.div(other, 2) * 4 + zh * 2 + lax.rem(other, 2))
+    turns = [lax.rem(q + k, 8) for k in range(8)]
+    places = [lax.div(turn, 2) * 4 + lax.rem(turn, 2) + 2 * zh for turn in turns]
+    q_set = lax.div(q, 8)
 
     def at_z(other):
         return (lax.rem(other, DEPTH), p + 2 * (lax.div(other, DEPTH) - zh))
@@ -235,10 +236,12 @@
     for copy in wide_copies:
         copy.wait()
 
-    def send_coef(member, depth, other):
+    def send_coef(group, k, cross):
+        member = 1 - parity if cross else parity
         return pltpu.make_async_remote_copy(
-            src_ref=csend.at[2 * other + member], dst_ref=sbuf.at[GROUP * parity + block], send_sem=cs, recv_sem=cr,
-            device_id=(depth, at_q(other)[1]), device_id_type=MESH,
+            src_ref=csend.at[2 * (8 * group + turns[k]) + member], dst_ref=sbuf.at[GROUP * cross + block],
+            send_sem=cs, recv_sem=cr.at[cross],
+            device_id=(mate if cross else d, 16 * group + places[k]), device_id_type=MESH,
         )
 
     both = pair(jnp.concatenate(even + odd, axis=0))
@@ -252,57 +255,58 @@
                 starts = [2 * ROWS * kind + ROWS * layer + 8 * half for half in range(2) for layer in range(2)]
                 for t, value in enumerate(regroup([coef[n : n + 8, lanes] for n in starts])):
                     csend[2 * start + 4 * m + t] = value
-            for k in range(8):
-                other = start + lax.rem(q + k, 8)
-                send_coef(1 - parity, mate, other).start()
-                if k == 0:
-                    pl.when(other != q)(send_coef(parity, d, other).start)
-                else:
-                    send_coef(parity, d, other).start()
-
-    def respond(start, is_sin):
+            for k in range(1, 8):
+                send_coef(start // 8, k, 0).start()
+    for group in range(4):
+        pl.when(group != q_set)(send_coef(group, 0, 0).start)
+    for k in range(8):
+        for group in range(4):
+            send_coef(group, k, 1).start()
+
+    def respond(start, cross):
         row = lax.broadcasted_iota(jnp.int32, (128, 128), 0)
         col = lax.broadcasted_iota(jnp.int32, (128, 128), 1) + start
         place = lax.rem(q, GROUP // 2) * COEF + parity * SHARE + lax.rem(row, SHARE)
         v = jnp.where(q >= GROUP // 2, NX - place, place).astype(F32)
         scale = 2.0 * math.pi * grav_scale * thickness / (4.0 * NX * NX)
         weight = jnp.where(place == 0, scale, 2.0 * scale) * jnp.where(col == 0, 1.0, 2.0)
-        layer = (2 * (d - parity) + lax.div(row, SHARE)).astype(F32)
+        layer = (2 * (mate if cross else d) + lax.rem(lax.div(row, SHARE), 2)).astype(F32)
         rate = (top_depth + (layer + 0.5) * thickness) * (-2.0 * math.pi / (2 * NX))
-        u = (NX - col if is_sin else col).astype(F32)
+        u = jnp.where(row >= 64, NX - col, col).astype(F32)
         return jnp.exp(jnp.sqrt(u * u + v * v) * rate) * weight
 
-    for kind in range(2):
+    for cross in range(2):
         for k in range(NX // 128):
-            rsp[128 * kind : 128 * (kind + 1), 128 * k : 128 * (k + 1)] = respond(128 * k, kind == 1)
-
-    sbuf[GROUP * parity + block] = csend[2 * q + parity]
-    landed = sbuf.at[pl.ds(0, 2 * GROUP - 1)]
-    pltpu.make_async_copy(landed, landed, cr).wait()
-
+            rsp[cross, :, 128 * k : 128 * (k + 1)] = respond(128 * k, cross)
+
+    sbuf[block] = csend[2 * q + parity]
     for copy in mixed_copies + tall_copies:
         copy.wait()
-    layers = []
-    for member in range(2):
-        value = sbuf[GROUP * member : GROUP * (member + 1)].reshape(HALF // 2, 128).T
-        layers.append(jnp.concatenate([value[:64], value[64:]], axis=1))
-    value = jnp.concatenate(layers, axis=0)
-    side = lax.rem(lax.div(lax.broadcasted_iota(jnp.int32, (128, HALF), 1), 16), 2)
-    value = jnp.concatenate([value, jnp.where(side == zh, value, -value) * alternating((128, HALF))], axis=0)
-    both = pair(value)
+    side = lax.rem(lax.div(lax.broadcasted_iota(jnp.int32, (64, HALF), 1), 16), 2)
+    sign = jnp.where(side == zh, 1.0, -1.0) * alternating((64, HALF))
     step = 256
-    for k in range(NX // step):
-        here = slice(k * step, (k + 1) * step)
-        coef = table_right(both, mixed[0, :, here], mixed[1, :, here]) * rsp[:, here]
-        parts = [coef[SHARE * n : SHARE * (n + 1)] for n in range(8)]
-        cosine = (parts[0] + parts[1]) + (parts[2] + parts[3])
-        sine = (parts[4] + parts[5]) + (parts[6] + parts[7])
-        pst[:, here] = pair(jnp.concatenate([cosine, sine], axis=0))
-
-    def send_rows(member, depth, other):
+    for cross in range(2):
+        landed = sbuf.at[pl.ds(GROUP * cross, GROUP - 1 + cross)]
+        pltpu.make_async_copy(landed, landed, cr.at[cross]).wait()
+        value = sbuf[GROUP * cross : GROUP * (cross + 1)].reshape(HALF // 2, 128).T
+        value = jnp.concatenate([value[:64], value[64:]], axis=1)
+        both = pair(jnp.concatenate([value, value * sign], axis=0))
+        for k in range(NX // step):
+            here = slice(k * step, (k + 1) * step)
+            coef = table_right(both, mixed[0, :, here], mixed[1, :, here]) * rsp[cross, :, here]
+            parts = [coef[SHARE * n : SHARE * (n + 1)] for n in range(4)]
+            coef = jnp.concatenate([parts[0] + parts[1], parts[2] + parts[3]], axis=0)
+            if cross:
+                pst[:, here] = pair(coef + acc[:, here])
+            else:
+                acc[:, here] = coef
+
+    def send_rows(group, k, cross):
+        member = 1 - parity if cross else parity
         return pltpu.make_async_remote_copy(
-            src_ref=xsend.at[2 * other + member], dst_ref=cbuf.at[2 * q + parity], send_sem=xs, recv_sem=xr,
-            device_id=(depth, at_q(other)[1]), device_id_type=MESH,
+            src_ref=xsend.at[2 * (8 * group + turns[k]) + member], dst_ref=cbuf.at[2 * q + parity],
+            send_sem=xs, recv_sem=xr,
+            device_id=(mate if cross else d, 16 * group + places[k]), device_id_type=MESH,
         )
 
     lane = lax.broadcasted_iota(jnp.int32, (8, 128), 1)
@@ -331,25 +335,27 @@
                 ):
                     xsend[2 * spot + member] = jnp.where(early, one, two)[:4]
 
-        for k in range(16):
-            spot = lax.rem(q + k, 16)
-            upper = lax.div(spot, 8)
-            other = spot + 16 * (upper if part else 1 - upper)
-            send_rows(1 - parity, mate, other).start()
-            if k == 0:
-                pl.when(other != q)(send_rows(parity, d, other).start)
-            else:
-                send_rows(parity, d, other).start()
+        for k in range(8):
+            for group in (2 + part, 1 - part):
+                send_rows(group, k, 1).start()
+                if k:
+                    send_rows(group, k, 0).start()
+    for group in range(4):
+        pl.when(group != q_set)(send_rows(group, 0, 0).start)
 
     cbuf[2 * q + parity] = xsend[2 * q + parity]
     landed = cbuf.at[pl.ds(0, 2 * GROUP - 1)]
     pltpu.make_async_copy(landed, landed, xr).wait()
 
-    def send_field(other):
+    def send_field(far, depth):
+        row = 1 - zh if far else zh
         return pltpu.make_async_remote_copy(
-            src_ref=gsend.at[other], dst_ref=gbuf.at[z], send_sem=gs, recv_sem=gr,
-            device_id=at_z(other), device_id_type=MESH,
+            src_ref=gsend.at[DEPTH * row + depth], dst_ref=gbuf.at[z], send_sem=gs, recv_sem=gr,
+            device_id=(depth, p + 2 - 4 * zh if far else p), device_id_type=MESH,
         )
+
+    steps = [lax.rem(d + 2 + k, 4) for k in range(4)]
+    depths = ([2 + turn for turn in steps], [lax.rem(6 + turn, DEPTH) for turn in steps])
 
     for m in range(2 * NX // 128):
         parts = regroup([cbuf[4 * m + t] for t in range(4)])
@@ -370,13 +376,12 @@
                 lanes = slice(128 * n, 128 * (n + 1))
                 gsend[DEPTH * half + 4 + 2 * cut + n] = plus[rows, lanes]
                 gsend[DEPTH * half + 3 - 2 * cut - n] = minus[rows, lanes]
-        for k in range(8):
-            turn = lax.rem(4 * zh + lax.rem(d + 2, 4) + k, 8)
-            other = DEPTH * lax.div(turn, 4) + lax.rem(2 + 4 * cut + lax.rem(turn, 4), DEPTH)
-            if k == 0:
-                pl.when(other != z)(send_field(other).start)
-            else:
-                send_field(other).start()
+        for k in range(4):
+            send_field(True, depths[cut][k]).start()
+        for k in range(1, 4):
+            send_field(False, depths[cut][k]).start()
+    for cut in range(2):
+        pl.when(depths[cut][0] != d)(send_field(False, depths[cut][0]).start)
 
     gbuf[z] = gsend[z]
     pltpu.make_async_copy(gbuf.at[pl.ds(0, RING - 1)], gbuf.at[pl.ds(0, RING - 1)], gr).wait()
@@ -433,7 +438,8 @@
                 pltpu.VMEM((2, 16, 128), F32),
                 pltpu.VMEM((2 * GROUP, 8, 128), F32),
                 pltpu.VMEM((2 * GROUP, 8, 128), F32),
-                pltpu.VMEM((256, NX), F32),
+                pltpu.VMEM((2, 128, NX), F32),
+                pltpu.VMEM((64, NX), F32),
                 pltpu.VMEM((128, NX), BF16),
                 pltpu.VMEM((2 * GROUP, 4, 128), F32),
                 pltpu.VMEM((2 * GROUP, 4, 128), F32),
@@ -441,7 +447,7 @@
                 pltpu.VMEM((RING, 8, 128), F32),
                 pltpu.VMEM((RING, 8, 128), F32),
                 dma(()), dma(()), dma((2,)), dma((2,)), dma((2,)), dma((4,)), dma((4,)),
-                dma(()), dma(()), dma(()), dma(()), dma(()), dma(()),
+                dma(()), dma((2,)), dma(()), dma(()), dma(()), dma(()),
             ],
             compiler_params=pltpu.CompilerParams(
                 collective_id=0, has_side_effects=True, vmem_limit_bytes=63 * 1024 * 1024

time: 51.9 us -> 51.7 us (level)
  no operation moved by 1% of the time
where the time goes in v9:
time: 51.7 us; the launch traced here: 51.5 us
  Pallas kernels  50.2 us (97%)
  local copies, waits for them, and re-layouts  1.3 us (3%)
    pallas_call x1, Pallas kernels, step(): pl.pallas_call(kernel, out_shape=jax.ShapeDtypeStruct((ROWS, 128), F32),...  50.2 us
    unnamed x1, local copies, waits for them, and re-layouts  1.3 us

profile of v9, /device:TPU:1, one launch (start us, length us, event | category | flops | bytes accessed | tf_op | source)
XLA Modules:
  0.0 51.5 jit_solution(578090420015186811)
XLA Ops:
  0.0 50.2 %shard_map.55 = f32[16,128]{1,0:T(8,128)} custom-call(f32[2,16,1024]{2,1,0:T(8,128)} %ls_hbm.1, f32[2]{0:T(128)} %con_hbm.1, bf16[2,512,1024]{2,1,0:T(8,128)(2,1)} %constant.6.clone.wide_hbm, bf16[2,512,1024]{2,1,0:T(8,128)(2,1)} %constant.7.clone.mixed_hbm, bf16[2,1024,512]{2,1,0:T(8,128)(2,1)} %constant.8.clone.tall_hbm), custom_call_target="tpu_custom_call" | custom-call | tf_op jit(solution)/shard_map/pallas_call | solution.py:423
  50.2 1.3 %copy.7 = f32[16,128]{1,0:T(8,128)} copy(f32[16,128]{1,0:T(8,128)} %shard_map.55) | data formatting | bytes 16384

commit v10 on v9

--- a/solution.py
+++ b/solution.py
@@ -113,9 +113,16 @@
     z = zh * DEPTH + d
     lower = p < PLAN // 2
 
-    turns = [lax.rem(q + k, 8) for k in range(8)]
-    places = [lax.div(turn, 2) * 4 + lax.rem(turn, 2) + 2 * zh for turn in turns]
-    q_set = lax.div(q, 8)
+    x, y = lax.div(p, 16), lax.rem(lax.div(p, 4), 4)
+    kind_own, cut_own = lax.div(y, 2), lax.rem(x + y, 2)
+    set_own = 2 * kind_own + cut_own
+    coef_block = 8 * set_own + 2 * x + core
+    order = (2, 6, 4, 3, 7, 5, 1, 0)
+    turns = [lax.rem(2 * x + core + k, 8) for k in order]
+    places = [
+        [16 * lax.div(t, 2) + 4 * lax.rem(lax.div(t, 2) + cut, 2) + 2 * zh + lax.rem(t, 2) for t in turns]
+        for cut in range(2)
+    ]
 
     def at_z(other):
         return (lax.rem(other, DEPTH), p + 2 * (lax.div(other, DEPTH) - zh))
@@ -241,7 +248,7 @@
         return pltpu.make_async_remote_copy(
             src_ref=csend.at[2 * (8 * group + turns[k]) + member], dst_ref=sbuf.at[GROUP * cross + block],
             send_sem=cs, recv_sem=cr.at[cross],
-            device_id=(mate if cross else d, 16 * group + places[k]), device_id_type=MESH,
+            device_id=(mate if cross else d, 8 * (group // 2) + places[group % 2][k]), device_id_type=MESH,
         )
 
     both = pair(jnp.concatenate(even + odd, axis=0))
@@ -255,10 +262,11 @@
                 starts = [2 * ROWS * kind + ROWS * layer + 8 * half for half in range(2) for layer in range(2)]
                 for t, value in enumerate(regroup([coef[n : n + 8, lanes] for n in starts])):
                     csend[2 * start + 4 * m + t] = value
-            for k in range(1, 8):
-                send_coef(start // 8, k, 0).start()
+        for k in range(7):
+            for kind in range(2):
+                send_coef(2 * kind + cut, k, 0).start()
     for group in range(4):
-        pl.when(group != q_set)(send_coef(group, 0, 0).start)
+        pl.when(group != set_own)(send_coef(group, 7, 0).start)
     for k in range(8):
         for group in range(4):
             send_coef(group, k, 1).start()
@@ -266,8 +274,8 @@
     def respond(start, cross):
         row = lax.broadcasted_iota(jnp.int32, (128, 128), 0)
         col = lax.broadcasted_iota(jnp.int32, (128, 128), 1) + start
-        place = lax.rem(q, GROUP // 2) * COEF + parity * SHARE + lax.rem(row, SHARE)
-        v = jnp.where(q >= GROUP // 2, NX - place, place).astype(F32)
+        place = lax.rem(coef_block, GROUP // 2) * COEF + parity * SHARE + lax.rem(row, SHARE)
+        v = jnp.where(kind_own == 1, NX - place, place).astype(F32)
         scale = 2.0 * math.pi * grav_scale * thickness / (4.0 * NX * NX)
         weight = jnp.where(place == 0, scale, 2.0 * scale) * jnp.where(col == 0, 1.0, 2.0)
         layer = (2 * (mate if cross else d) + lax.rem(lax.div(row, SHARE), 2)).astype(F32)
@@ -279,7 +287,7 @@
         for k in range(NX // 128):
             rsp[cross, :, 128 * k : 128 * (k + 1)] = respond(128 * k, cross)
 
-    sbuf[block] = csend[2 * q + parity]
+    sbuf[block] = csend[2 * coef_block + parity]
     for copy in mixed_copies + tall_copies:
         copy.wait()
     side = lax.rem(lax.div(lax.broadcasted_iota(jnp.int32, (64, HALF), 1), 16), 2)
@@ -301,24 +309,34 @@
             else:
                 acc[:, here] = coef
 
-    def send_rows(group, k, cross):
+    low = 2 * lax.rem(y, 2) + core
+    x_turns = [lax.rem(x + k, 4) for k in range(4)]
+    low_turns = [lax.rem(low + k, 4) for k in range(4)]
+    low_places = [4 * lax.div(t, 2) + lax.rem(t, 2) + 2 * zh for t in low_turns]
+
+    def send_rows(part, r, k, cross):
+        upper = lax.div(x_turns[r], 2)
+        upper = upper if part else 1 - upper
         member = 1 - parity if cross else parity
         return pltpu.make_async_remote_copy(
-            src_ref=xsend.at[2 * (8 * group + turns[k]) + member], dst_ref=cbuf.at[2 * q + parity],
-            send_sem=xs, recv_sem=xr,
-            device_id=(mate if cross else d, 16 * group + places[k]), device_id_type=MESH,
+            src_ref=xsend.at[2 * (8 * x_turns[r] + 4 * upper + low_turns[k]) + member],
+            dst_ref=cbuf.at[2 * coef_block + parity], send_sem=xs, recv_sem=xr,
+            device_id=(mate if cross else d, 16 * x_turns[r] + 8 * upper + low_places[k]), device_id_type=MESH,
         )
 
     lane = lax.broadcasted_iota(jnp.int32, (8, 128), 1)
     early, even_lane = lane < 64, lax.rem(lane, 64) < 32
+    def columns(part):
+        cols = slice(128 * part, 128 * part + 128), slice(128 * part + 256, 128 * part + 384)
+        return [jnp.concatenate([tall[n, :, col] for col in cols], axis=1) for n in range(2)]
+
     for part in range(2):
-        cols = slice(256 * part, 256 * (part + 1))
-        value = table_right(pst[...], tall[0, :, cols], tall[1, :, cols])
+        value = table_right(pst[...], *columns(part))
         evens, odds = value[:SHARE], value[SHARE:] * alternating((SHARE, 256))
         plus, minus = evens + odds, evens - odds
         value = jnp.concatenate([plus, minus, plus, minus], axis=0).T
         for g in range(4):
-            chunk = 4 * part + g
+            chunk = 2 * part + 4 * (g // 2) + g % 2
             for member in range(2):
                 ups, downs = [], []
                 for n in range(4):
@@ -335,15 +353,16 @@
                 ):
                     xsend[2 * spot + member] = jnp.where(early, one, two)[:4]
 
-        for k in range(8):
-            for group in (2 + part, 1 - part):
-                send_rows(group, k, 1).start()
-                if k:
-                    send_rows(group, k, 0).start()
-    for group in range(4):
-        pl.when(group != q_set)(send_rows(group, 0, 0).start)
-
-    cbuf[2 * q + parity] = xsend[2 * q + parity]
+        for r in (1, 3, 2, 0):
+            for k in range(4):
+                send_rows(part, r, k, 1).start()
+                if r or k:
+                    send_rows(part, r, k, 0).start()
+    upper_own = lax.rem(lax.div(x, 2) + lax.div(y, 2), 2)
+    pl.when(upper_own == 0)(send_rows(0, 0, 0, 0).start)
+    pl.when(upper_own == 1)(send_rows(1, 0, 0, 0).start)
+
+    cbuf[2 * coef_block + parity] = xsend[2 * q + parity]
     landed = cbuf.at[pl.ds(0, 2 * GROUP - 1)]
     pltpu.make_async_copy(landed, landed, xr).wait()
 
@@ -354,8 +373,8 @@
             device_id=(depth, p + 2 - 4 * zh if far else p), device_id_type=MESH,
         )
 
-    steps = [lax.rem(d + 2 + k, 4) for k in range(4)]
-    depths = ([2 + turn for turn in steps], [lax.rem(6 + turn, DEPTH) for turn in steps])
+    steps = [lax.rem(lax.div(d, 2) + k, 4) for k in range(4)]
+    depths = ([2 * t + 1 - lax.div(t, 2) for t in steps], [2 * t + lax.div(t, 2) for t in steps])
 
     for m in range(2 * NX // 128):
         parts = regroup([cbuf[4 * m + t] for t in range(4)])
@@ -365,8 +384,7 @@
             coefs[start : start + 4, lanes] = parts[g]
     both = pair(coefs[...])
     for cut in range(2):
-        cols = slice(256 * cut, 256 * (cut + 1))
-        value = table_right(both, tall[0, :, cols], tall[1, :, cols])
+        value = table_right(both, *columns(cut))
         evens, odds = value[:ROWS], value[ROWS:] * alternating((ROWS, 256))
         plus = evens + odds
         minus = evens - odds
@@ -374,8 +392,8 @@
             rows = slice(8 * half, 8 * (half + 1))
             for n in range(2):
                 lanes = slice(128 * n, 128 * (n + 1))
-                gsend[DEPTH * half + 4 + 2 * cut + n] = plus[rows, lanes]
-                gsend[DEPTH * half + 3 - 2 * cut - n] = minus[rows, lanes]
+                gsend[DEPTH * half + 4 + cut + 2 * n] = plus[rows, lanes]
+                gsend[DEPTH * half + 3 - cut - 2 * n] = minus[rows, lanes]
         for k in range(4):
             send_field(True, depths[cut][k]).start()
         for k in range(1, 4):

time: 51.7 us -> 50.9 us (0.985)
  Pallas kernels: 50.2 us -> 49.4 us
    pallas_call x1, Pallas kernels: 50.2 us -> 49.4 us  [step(): pl.pallas_call(kernel, out_shape=jax.ShapeDtypeStruct((ROWS, 128), F32),...]
where the time goes in v10:
time: 50.9 us; the launch traced here: 50.7 us
  Pallas kernels  49.4 us (97%)
  local copies, waits for them, and re-layouts  1.3 us (3%)
    pallas_call x1, Pallas kernels, step(): pl.pallas_call(kernel, out_shape=jax.ShapeDtypeStruct((ROWS, 128), F32),...  49.4 us
    unnamed x1, local copies, waits for them, and re-layouts  1.3 us

profile of v10, /device:TPU:1, one launch (start us, length us, event | category | flops | bytes accessed | tf_op | source)
XLA Modules:
  0.0 50.7 jit_solution(12267953389722751579)
XLA Ops:
  0.0 49.4 %shard_map.55 = f32[16,128]{1,0:T(8,128)} custom-call(f32[2,16,1024]{2,1,0:T(8,128)} %ls_hbm.1, f32[2]{0:T(128)} %con_hbm.1, bf16[2,512,1024]{2,1,0:T(8,128)(2,1)} %constant.6.clone.wide_hbm, bf16[2,512,1024]{2,1,0:T(8,128)(2,1)} %constant.7.clone.mixed_hbm, bf16[2,1024,512]{2,1,0:T(8,128)(2,1)} %constant.8.clone.tall_hbm), custom_call_target="tpu_custom_call" | custom-call | tf_op jit(solution)/shard_map/pallas_call | solution.py:441
  49.4 1.3 %copy.7 = f32[16,128]{1,0:T(8,128)} copy(f32[16,128]{1,0:T(8,128)} %shard_map.55) | data formatting | bytes 16384

commit v11 on v10

--- a/solution.py
+++ b/solution.py
@@ -102,7 +102,7 @@
 
 def kernel(
     ls_hbm, con_hbm, wide_hbm, mixed_hbm, tall_hbm, out_ref,
-    ls_ref, con_ref, own, part_density, wide, mixed, tall, zhalo, rsend, rhalo, csend, sbuf, rsp, acc, pst, xsend, cbuf, coefs, gsend, gbuf,
+    ls_ref, con_ref, own, part_density, wide, mixed, tall, zhalo, rsend, rhalo, folded, folded_back, csend, sbuf, rsp, acc, pst, xsend, cbuf, coefs, gsend, gbuf,
     ls_sem, con_sem, wide_sem, mixed_sem, tall_sem, hs, hr, cs, cr, xs, xr, gs, gr,
 ):
     d = lax.axis_index("depth")
@@ -117,12 +117,9 @@
     kind_own, cut_own = lax.div(y, 2), lax.rem(x + y, 2)
     set_own = 2 * kind_own + cut_own
     coef_block = 8 * set_own + 2 * x + core
-    order = (2, 6, 4, 3, 7, 5, 1, 0)
-    turns = [lax.rem(2 * x + core + k, 8) for k in order]
-    places = [
-        [16 * lax.div(t, 2) + 4 * lax.rem(lax.div(t, 2) + cut, 2) + 2 * zh + lax.rem(t, 2) for t in turns]
-        for cut in range(2)
-    ]
+
+    def turn(k):
+        return lax.rem(2 * x + core + k, 8)
 
     def at_z(other):
         return (lax.rem(other, DEPTH), p + 2 * (lax.div(other, DEPTH) - zh))
@@ -151,12 +148,17 @@
         greet(at_z(lax.rem(z + k, RING)))
     greet((d, p + 1 - 2 * core))
     pl.when(has_outer)(lambda: greet((d, outer)))
-    for k in range(1, GROUP // 2):
+
+    @pl.loop(1, GROUP // 2)
+    def _(k):
         first = 4 * lax.rem(xy + k, GROUP // 2) + 2 * zh
         greet((d, first))
         greet((d, first + 1))
-    for k in range(2, RING - 1):
+
+    @pl.loop(2, RING - 1)
+    def _(k):
         greet(at_z(lax.rem(z + k, RING)))
+
 
     ls_copy.wait()
     con_copy.wait()
@@ -243,33 +245,46 @@
     for copy in wide_copies:
         copy.wait()
 
-    def send_coef(group, k, cross):
+    def send_coef(kind, cut, k, cross):
+        place = turn(k)
+        x_to = lax.div(place, 2)
+        target = 16 * x_to + 8 * kind + 4 * lax.rem(x_to + cut, 2) + 2 * zh + lax.rem(place, 2)
         member = 1 - parity if cross else parity
         return pltpu.make_async_remote_copy(
-            src_ref=csend.at[2 * (8 * group + turns[k]) + member], dst_ref=sbuf.at[GROUP * cross + block],
-            send_sem=cs, recv_sem=cr.at[cross],
-            device_id=(mate if cross else d, 8 * (group // 2) + places[group % 2][k]), device_id_type=MESH,
+            src_ref=csend.at[2 * (16 * kind + 8 * cut + place) + member], dst_ref=sbuf.at[GROUP * cross + block],
+            send_sem=cs, recv_sem=cr.at[cross], device_id=(mate if cross else d, target), device_id_type=MESH,
         )
 
-    both = pair(jnp.concatenate(even + odd, axis=0))
-    for cut in range(2):
-        cols = slice(HALF * cut, HALF * (cut + 1))
-        coef = table_right(both, wide[0, :, cols], wide[1, :, cols])
+    folded[...] = pair(jnp.concatenate(even + odd, axis=0))
+
+    @pl.loop(0, 2)
+    def _(cut):
+        cols = pl.ds(pl.multiple_of(HALF * cut, HALF), HALF)
+        coef = table_right(folded[...], wide[0, :, cols], wide[1, :, cols])
         for kind in range(2):
-            start = kind * 16 + 8 * cut
             for m in range(4):
                 lanes = slice(128 * m, 128 * (m + 1))
                 starts = [2 * ROWS * kind + ROWS * layer + 8 * half for half in range(2) for layer in range(2)]
                 for t, value in enumerate(regroup([coef[n : n + 8, lanes] for n in starts])):
-                    csend[2 * start + 4 * m + t] = value
-        for k in range(7):
+                    csend[16 * cut + 32 * kind + 4 * m + t] = value
+
+        @pl.loop(1, 8)
+        def _(k):
             for kind in range(2):
-                send_coef(2 * kind + cut, k, 0).start()
-    for group in range(4):
-        pl.when(group != set_own)(send_coef(group, 7, 0).start)
-    for k in range(8):
-        for group in range(4):
-            send_coef(group, k, 1).start()
+                send_coef(kind, cut, k, 0).start()
+
+    for kind in range(2):
+        for cut in range(2):
+            pl.when(2 * kind + cut != set_own)(send_coef(kind, cut, 0, 0).start)
+
+    @pl.loop(0, 8)
+    def _(k):
+        for kind in range(2):
+            for cut in range(2):
+                send_coef(kind, cut, k, 1).start()
+
+    home = pltpu.make_async_copy(csend.at[2 * coef_block + parity], sbuf.at[block], cr.at[0])
+    home.start()
 
     def respond(start, cross):
         row = lax.broadcasted_iota(jnp.int32, (128, 128), 0)
@@ -283,54 +298,58 @@
         u = jnp.where(row >= 64, NX - col, col).astype(F32)
         return jnp.exp(jnp.sqrt(u * u + v * v) * rate) * weight
 
-    for cross in range(2):
-        for k in range(NX // 128):
-            rsp[cross, :, 128 * k : 128 * (k + 1)] = respond(128 * k, cross)
-
-    sbuf[block] = csend[2 * coef_block + parity]
+    @pl.loop(0, NX // 128)
+    def _(k):
+        for cross in range(2):
+            rsp[cross, :, pl.ds(pl.multiple_of(128 * k, 128), 128)] = respond(128 * k, cross)
+
+
     for copy in mixed_copies + tall_copies:
         copy.wait()
     side = lax.rem(lax.div(lax.broadcasted_iota(jnp.int32, (64, HALF), 1), 16), 2)
     sign = jnp.where(side == zh, 1.0, -1.0) * alternating((64, HALF))
     step = 256
-    for cross in range(2):
-        landed = sbuf.at[pl.ds(GROUP * cross, GROUP - 1 + cross)]
+    acc[...] = jnp.zeros(acc.shape, F32)
+
+    @pl.loop(0, 2)
+    def _(cross):
+        here = pl.ds(GROUP * cross, GROUP)
+        landed = sbuf.at[here]
         pltpu.make_async_copy(landed, landed, cr.at[cross]).wait()
-        value = sbuf[GROUP * cross : GROUP * (cross + 1)].reshape(HALF // 2, 128).T
+        value = sbuf[here].reshape(HALF // 2, 128).T
         value = jnp.concatenate([value[:64], value[64:]], axis=1)
         both = pair(jnp.concatenate([value, value * sign], axis=0))
         for k in range(NX // step):
             here = slice(k * step, (k + 1) * step)
             coef = table_right(both, mixed[0, :, here], mixed[1, :, here]) * rsp[cross, :, here]
             parts = [coef[SHARE * n : SHARE * (n + 1)] for n in range(4)]
-            coef = jnp.concatenate([parts[0] + parts[1], parts[2] + parts[3]], axis=0)
-            if cross:
-                pst[:, here] = pair(coef + acc[:, here])
-            else:
-                acc[:, here] = coef
+            acc[:, here] += jnp.concatenate([parts[0] + parts[1], parts[2] + parts[3]], axis=0)
+
+    pst[...] = pair(acc[...])
 
     low = 2 * lax.rem(y, 2) + core
-    x_turns = [lax.rem(x + k, 4) for k in range(4)]
-    low_turns = [lax.rem(low + k, 4) for k in range(4)]
-    low_places = [4 * lax.div(t, 2) + lax.rem(t, 2) + 2 * zh for t in low_turns]
 
     def send_rows(part, r, k, cross):
-        upper = lax.div(x_turns[r], 2)
-        upper = upper if part else 1 - upper
+        x_to = lax.rem(x + r, 4)
+        low_to = lax.rem(low + k, 4)
+        upper = lax.rem(lax.div(x_to, 2) + 1 + part, 2)
         member = 1 - parity if cross else parity
+        target = 16 * x_to + 8 * upper + 4 * lax.div(low_to, 2) + lax.rem(low_to, 2) + 2 * zh
         return pltpu.make_async_remote_copy(
-            src_ref=xsend.at[2 * (8 * x_turns[r] + 4 * upper + low_turns[k]) + member],
+            src_ref=xsend.at[2 * (8 * x_to + 4 * upper + low_to) + member],
             dst_ref=cbuf.at[2 * coef_block + parity], send_sem=xs, recv_sem=xr,
-            device_id=(mate if cross else d, 16 * x_turns[r] + 8 * upper + low_places[k]), device_id_type=MESH,
+            device_id=(mate if cross else d, target), device_id_type=MESH,
         )
 
     lane = lax.broadcasted_iota(jnp.int32, (8, 128), 1)
     early, even_lane = lane < 64, lax.rem(lane, 64) < 32
+
     def columns(part):
-        cols = slice(128 * part, 128 * part + 128), slice(128 * part + 256, 128 * part + 384)
+        cols = [pl.ds(pl.multiple_of(128 * part + start, 128), 128) for start in (0, 256)]
         return [jnp.concatenate([tall[n, :, col] for col in cols], axis=1) for n in range(2)]
 
-    for part in range(2):
+    @pl.loop(0, 2)
+    def _(part):
         value = table_right(pst[...], *columns(part))
         evens, odds = value[:SHARE], value[SHARE:] * alternating((SHARE, 256))
         plus, minus = evens + odds, evens - odds
@@ -353,11 +372,13 @@
                 ):
                     xsend[2 * spot + member] = jnp.where(early, one, two)[:4]
 
-        for r in (1, 3, 2, 0):
-            for k in range(4):
-                send_rows(part, r, k, 1).start()
-                if r or k:
-                    send_rows(part, r, k, 0).start()
+        send_rows(part, 0, 0, 1).start()
+
+        @pl.loop(1, 16)
+        def _(n):
+            send_rows(part, lax.rem(n, 4), lax.div(n, 4), 1).start()
+            send_rows(part, lax.rem(n, 4), lax.div(n, 4), 0).start()
+
     upper_own = lax.rem(lax.div(x, 2) + lax.div(y, 2), 2)
     pl.when(upper_own == 0)(send_rows(0, 0, 0, 0).start)
     pl.when(upper_own == 1)(send_rows(1, 0, 0, 0).start)
@@ -373,8 +394,9 @@
             device_id=(depth, p + 2 - 4 * zh if far else p), device_id_type=MESH,
         )
 
-    steps = [lax.rem(lax.div(d, 2) + k, 4) for k in range(4)]
-    depths = ([2 * t + 1 - lax.div(t, 2) for t in steps], [2 * t + lax.div(t, 2) for t in steps])
+    def depth_of(cut, k):
+        t = lax.rem(lax.div(d, 2) + k, 4)
+        return 2 * t + lax.rem(lax.div(t, 2) + 1 + cut, 2)
 
     for m in range(2 * NX // 128):
         parts = regroup([cbuf[4 * m + t] for t in range(4)])
@@ -382,9 +404,11 @@
         for g in range(4):
             start = ROWS * (m // 8) + 4 * g
             coefs[start : start + 4, lanes] = parts[g]
-    both = pair(coefs[...])
-    for cut in range(2):
-        value = table_right(both, *columns(cut))
+    folded_back[...] = pair(coefs[...])
+
+    @pl.loop(0, 2)
+    def _(cut):
+        value = table_right(folded_back[...], *columns(cut))
         evens, odds = value[:ROWS], value[ROWS:] * alternating((ROWS, 256))
         plus = evens + odds
         minus = evens - odds
@@ -394,12 +418,15 @@
                 lanes = slice(128 * n, 128 * (n + 1))
                 gsend[DEPTH * half + 4 + cut + 2 * n] = plus[rows, lanes]
                 gsend[DEPTH * half + 3 - cut - 2 * n] = minus[rows, lanes]
-        for k in range(4):
-            send_field(True, depths[cut][k]).start()
-        for k in range(1, 4):
-            send_field(False, depths[cut][k]).start()
+        send_field(True, depth_of(cut, 0)).start()
+
+        @pl.loop(1, 4)
+        def _(k):
+            send_field(True, depth_of(cut, k)).start()
+            send_field(False, depth_of(cut, k)).start()
+
     for cut in range(2):
-        pl.when(depths[cut][0] != d)(send_field(False, depths[cut][0]).start)
+        pl.when(depth_of(cut, 0) != d)(send_field(False, depth_of(cut, 0)).start)
 
     gbuf[z] = gsend[z]
     pltpu.make_async_copy(gbuf.at[pl.ds(0, RING - 1)], gbuf.at[pl.ds(0, RING - 1)], gr).wait()
@@ -454,6 +481,8 @@
                 pltpu.VMEM((2, ROWS, NX), F32),
                 pltpu.VMEM((2, 16, 128), F32),
                 pltpu.VMEM((2, 16, 128), F32),
+                pltpu.VMEM((128, HALF), BF16),
+                pltpu.VMEM((64, NX), BF16),
                 pltpu.VMEM((2 * GROUP, 8, 128), F32),
                 pltpu.VMEM((2 * GROUP, 8, 128), F32),
                 pltpu.VMEM((2, 128, NX), F32),

time: 50.9 us -> 51 us (level)
  no operation moved by 1% of the time
where the time goes in v11:
time: 51 us; the launch traced here: 50.8 us
  Pallas kernels  49.5 us (97%)
  local copies, waits for them, and re-layouts  1.3 us (3%)
    pallas_call x1, Pallas kernels, step(): pl.pallas_call(kernel, out_shape=jax.ShapeDtypeStruct((ROWS, 128), F32),...  49.5 us
    unnamed x1, local copies, waits for them, and re-layouts  1.3 us

profile of v11, /device:TPU:1, one launch (start us, length us, event | category | flops | bytes accessed | tf_op | source)
XLA Modules:
  0.0 50.8 jit_solution(18150321316073651367)
XLA Ops:
  0.0 49.5 %shard_map.55 = f32[16,128]{1,0:T(8,128)} custom-call(f32[2,16,1024]{2,1,0:T(8,128)} %ls_hbm.1, f32[2]{0:T(128)} %con_hbm.1, bf16[2,512,1024]{2,1,0:T(8,128)(2,1)} %constant.6.clone.wide_hbm, bf16[2,512,1024]{2,1,0:T(8,128)(2,1)} %constant.7.clone.mixed_hbm, bf16[2,1024,512]{2,1,0:T(8,128)(2,1)} %constant.8.clone.tall_hbm), custom_call_target="tpu_custom_call" | custom-call | tf_op jit(solution)/shard_map/pallas_call | solution.py:468
  49.5 1.3 %copy.7 = f32[16,128]{1,0:T(8,128)} copy(f32[16,128]{1,0:T(8,128)} %shard_map.55) | data formatting | bytes 16384

commit v12 on v10

--- a/solution.py
+++ b/solution.py
@@ -103,7 +103,7 @@
 def kernel(
     ls_hbm, con_hbm, wide_hbm, mixed_hbm, tall_hbm, out_ref,
     ls_ref, con_ref, own, part_density, wide, mixed, tall, zhalo, rsend, rhalo, csend, sbuf, rsp, acc, pst, xsend, cbuf, coefs, gsend, gbuf,
-    ls_sem, con_sem, wide_sem, mixed_sem, tall_sem, hs, hr, cs, cr, xs, xr, gs, gr,
+    ls_sem, con_sem, wide_sem, mixed_sem, tall_sem, hs, hr, cs, cr, xs, xr, gs, gr, news,
 ):
     d = lax.axis_index("depth")
     p = lax.axis_index("plan")
@@ -144,19 +144,27 @@
 
     has = (d < DEPTH - 1, d > 0, p < PLAN - 1, p > 0)
     gets = (d > 0, d < DEPTH - 1, p > 0, p < PLAN - 1)
-    xy = lax.div(p, 4)
     outer = jnp.where(core == 0, p - 1, p + 1)
     has_outer = (outer >= 0) & (outer < PLAN)
-    for k in (1, RING - 1):
-        greet(at_z(lax.rem(z + k, RING)))
-    greet((d, p + 1 - 2 * core))
+    x_line = [(d, p + 16 * (lax.rem(x + k, 4) - x)) for k in (1, 3, 2)]
+    y_line = [(d, p + 4 * (lax.rem(y + k, 4) - y)) for k in (1, 3, 2)]
+    buddy = (d, p + 1 - 2 * core)
+
+    def z_pair(k):
+        return [at_z(lax.rem(z + away, RING)) for away in (k, RING - k)]
+
+    for target in z_pair(1) + [buddy]:
+        greet(target)
     pl.when(has_outer)(lambda: greet((d, outer)))
-    for k in range(1, GROUP // 2):
-        first = 4 * lax.rem(xy + k, GROUP // 2) + 2 * zh
-        greet((d, first))
-        greet((d, first + 1))
-    for k in range(2, RING - 1):
-        greet(at_z(lax.rem(z + k, RING)))
+    for target in x_line + y_line:
+        greet(target)
+
+    def tell(number, targets):
+        for target in targets:
+            pl.semaphore_signal(news.at[number], inc=1, device_id=target, device_id_type=MESH)
+
+    def hear(number, count):
+        pl.semaphore_wait(news.at[number], count)
 
     ls_copy.wait()
     con_copy.wait()
@@ -175,7 +183,7 @@
             rsend[0, spot : spot + 1, :] = jnp.where(lower, bottom, top)
             rsend[1, spot : spot + 1, :] = jnp.where(lower, top, bottom)
 
-    pl.semaphore_wait(barrier, GROUP + RING - 2 + has_outer.astype(jnp.int32))
+    pl.semaphore_wait(barrier, 9 + has_outer.astype(jnp.int32))
 
     def halo(source, target, number, device):
         return pltpu.make_async_remote_copy(
@@ -191,6 +199,8 @@
     copies = (z_up, z_down, r_up, r_down)
     for copy, there in zip(copies, has):
         pl.when(there)(copy.start)
+    tell(0, y_line)
+    tell(1, z_pair(1))
     for copy in mixed_copies + tall_copies:
         copy.start()
     for land, comes in zip(lands, gets):
@@ -220,6 +230,9 @@
         bend = bend + jnp.concatenate(across, axis=1)
         part_density[layer] = con_ref[layer] * (0.5 * (1.0 + jnp.tanh(centre))) + bend_weight * bend
 
+    hear(0, 3)
+    tell(2, [buddy])
+
     for copy, comes in zip(copies, gets):
         pl.when(comes)(copy.wait_recv)
     even, odd = [], []
@@ -240,6 +253,9 @@
     block = jnp.where(lower, PLAN // 2 - 1 - p, p - PLAN // 2)
     parity = lax.rem(d, 2)
     mate = d + 1 - 2 * parity
+    hear(2, 1)
+    hear(1, 2)
+    tell(3, [(mate, p)])
     for copy in wide_copies:
         copy.wait()
 
@@ -267,6 +283,8 @@
                 send_coef(2 * kind + cut, k, 0).start()
     for group in range(4):
         pl.when(group != set_own)(send_coef(group, 7, 0).start)
+    hear(3, 1)
+    tell(4, z_pair(2))
     for k in range(8):
         for group in range(4):
             send_coef(group, k, 1).start()
@@ -287,6 +305,8 @@
         for k in range(NX // 128):
             rsp[cross, :, 128 * k : 128 * (k + 1)] = respond(128 * k, cross)
 
+    hear(4, 2)
+    tell(5, z_pair(4))
     sbuf[block] = csend[2 * coef_block + parity]
     for copy in mixed_copies + tall_copies:
         copy.wait()
@@ -362,6 +382,7 @@
     pl.when(upper_own == 0)(send_rows(0, 0, 0, 0).start)
     pl.when(upper_own == 1)(send_rows(1, 0, 0, 0).start)
 
+    hear(5, 2)
     cbuf[2 * coef_block + parity] = xsend[2 * q + parity]
     landed = cbuf.at[pl.ds(0, 2 * GROUP - 1)]
     pltpu.make_async_copy(landed, landed, xr).wait()
@@ -465,7 +486,7 @@
                 pltpu.VMEM((RING, 8, 128), F32),
                 pltpu.VMEM((RING, 8, 128), F32),
                 dma(()), dma(()), dma((2,)), dma((2,)), dma((2,)), dma((4,)), dma((4,)),
-                dma(()), dma((2,)), dma(()), dma(()), dma(()), dma(()),
+                dma(()), dma((2,)), dma(()), dma(()), dma(()), dma(()), pltpu.SemaphoreType.REGULAR((6,)),
             ],
             compiler_params=pltpu.CompilerParams(
                 collective_id=0, has_side_effects=True, vmem_limit_bytes=63 * 1024 * 1024

time: 50.9 us -> 50.6 us (level)
  no operation moved by 1% of the time
where the time goes in v12:
time: 50.6 us; the launch traced here: 50.4 us
  Pallas kernels  49.1 us (97%)
  local copies, waits for them, and re-layouts  1.3 us (3%)
    pallas_call x1, Pallas kernels, step(): pl.pallas_call(kernel, out_shape=jax.ShapeDtypeStruct((ROWS, 128), F32),...  49.1 us
    unnamed x1, local copies, waits for them, and re-layouts  1.3 us

profile of v12, /device:TPU:1, one launch (start us, length us, event | category | flops | bytes accessed | tf_op | source)
XLA Modules:
  0.0 50.4 jit_solution(13511413679139615967)
XLA Ops:
  0.0 49.1 %shard_map.55 = f32[16,128]{1,0:T(8,128)} custom-call(f32[2,16,1024]{2,1,0:T(8,128)} %ls_hbm.1, f32[2]{0:T(128)} %con_hbm.1, bf16[2,512,1024]{2,1,0:T(8,128)(2,1)} %constant.6.clone.wide_hbm, bf16[2,512,1024]{2,1,0:T(8,128)(2,1)} %constant.7.clone.mixed_hbm, bf16[2,1024,512]{2,1,0:T(8,128)(2,1)} %constant.8.clone.tall_hbm), custom_call_target="tpu_custom_call" | custom-call | tf_op jit(solution)/shard_map/pallas_call | solution.py:462
  49.1 1.3 %copy.7 = f32[16,128]{1,0:T(8,128)} copy(f32[16,128]{1,0:T(8,128)} %shard_map.55) | data formatting | bytes 16384

commit v13 on v12

--- a/solution.py
+++ b/solution.py
@@ -117,6 +117,8 @@
     kind_own, cut_own = lax.div(y, 2), lax.rem(x + y, 2)
     set_own = 2 * kind_own + cut_own
     coef_block = 8 * set_own + 2 * x + core
+    parity = lax.rem(d, 2)
+    mate = d + 1 - 2 * parity
     order = (2, 6, 4, 3, 7, 5, 1, 0)
     turns = [lax.rem(2 * x + core + k, 8) for k in order]
     places = [
@@ -233,6 +235,22 @@
     hear(0, 3)
     tell(2, [buddy])
 
+    def respond(start, cross):
+        row = lax.broadcasted_iota(jnp.int32, (128, 128), 0)
+        col = lax.broadcasted_iota(jnp.int32, (128, 128), 1) + start
+        place = lax.rem(coef_block, GROUP // 2) * COEF + parity * SHARE + lax.rem(row, SHARE)
+        v = jnp.where(kind_own == 1, NX - place, place).astype(F32)
+        scale = 2.0 * math.pi * grav_scale * thickness / (4.0 * NX * NX)
+        weight = jnp.where(place == 0, scale, 2.0 * scale) * jnp.where(col == 0, 1.0, 2.0)
+        layer = (2 * (mate if cross else d) + lax.rem(lax.div(row, SHARE), 2)).astype(F32)
+        rate = (top_depth + (layer + 0.5) * thickness) * (-2.0 * math.pi / (2 * NX))
+        u = jnp.where(row >= 64, NX - col, col).astype(F32)
+        return jnp.exp(jnp.sqrt(u * u + v * v) * rate) * weight
+
+    for cross in range(2):
+        for k in range(NX // 128):
+            rsp[cross, :, 128 * k : 128 * (k + 1)] = respond(128 * k, cross)
+
     for copy, comes in zip(copies, gets):
         pl.when(comes)(copy.wait_recv)
     even, odd = [], []
@@ -251,8 +269,6 @@
         odd.append((density[:, :HALF] - density[:, HALF:]) * alternating((ROWS, HALF)))
 
     block = jnp.where(lower, PLAN // 2 - 1 - p, p - PLAN // 2)
-    parity = lax.rem(d, 2)
-    mate = d + 1 - 2 * parity
     hear(2, 1)
     hear(1, 2)
     tell(3, [(mate, p)])
@@ -288,22 +304,6 @@
     for k in range(8):
         for group in range(4):
             send_coef(group, k, 1).start()
-
-    def respond(start, cross):
-        row = lax.broadcasted_iota(jnp.int32, (128, 128), 0)
-        col = lax.broadcasted_iota(jnp.int32, (128, 128), 1) + start
-        place = lax.rem(coef_block, GROUP // 2) * COEF + parity * SHARE + lax.rem(row, SHARE)
-        v = jnp.where(kind_own == 1, NX - place, place).astype(F32)
-        scale = 2.0 * math.pi * grav_scale * thickness / (4.0 * NX * NX)
-        weight = jnp.where(place == 0, scale, 2.0 * scale) * jnp.where(col == 0, 1.0, 2.0)
-        layer = (2 * (mate if cross else d) + lax.rem(lax.div(row, SHARE), 2)).astype(F32)
-        rate = (top_depth + (layer + 0.5) * thickness) * (-2.0 * math.pi / (2 * NX))
-        u = jnp.where(row >= 64, NX - col, col).astype(F32)
-        return jnp.exp(jnp.sqrt(u * u + v * v) * rate) * weight
-
-    for cross in range(2):
-        for k in range(NX // 128):
-            rsp[cross, :, 128 * k : 128 * (k + 1)] = respond(128 * k, cross)
 
     hear(4, 2)
     tell(5, z_pair(4))
@@ -489,7 +489,7 @@
                 dma(()), dma((2,)), dma(()), dma(()), dma(()), dma(()), pltpu.SemaphoreType.REGULAR((6,)),
             ],
             compiler_params=pltpu.CompilerParams(
-                collective_id=0, has_side_effects=True, vmem_limit_bytes=63 * 1024 * 1024
+                collective_id=0, has_side_effects=True, vmem_limit_bytes=55176 * 1024
             ),
         )(level_set, contrast, jnp.asarray(wide), jnp.asarray(mixed), jnp.asarray(tall))
 

time: 50.6 us -> 50.2 us (level)
    unnamed x1 -> x3, local copies, waits for them, and re-layouts: 1.3 us -> 1.26 us
where the time goes in v13:
time: 50.2 us; the launch traced here: 50 us
  Pallas kernels  48.8 us (97%)
  local copies, waits for them, and re-layouts  1.26 us (3%)
    pallas_call x1, Pallas kernels, step(): pl.pallas_call(kernel, out_shape=jax.ShapeDtypeStruct((ROWS, 128), F32),...  48.8 us
    unnamed x3, local copies, waits for them, and re-layouts  1.26 us

profile of v13, /device:TPU:1, one launch (start us, length us, event | category | flops | bytes accessed | tf_op | source)
XLA Modules:
  0.0 50.0 jit_solution(960171436045973564)
XLA Ops:
  0.0 0.0 copy-start
  0.0 0.7 %copy-done = f32[2]{0:T(128)S(1)} copy-done((f32[2]{0:T(128)S(1)}, f32[2]{0:T(128)}, u32[]{:S(2)}) %copy-start) | copy-done | bytes 32
  0.7 48.8 %shard_map.55 = f32[16,128]{1,0:T(8,128)S(1)} custom-call(f32[2,16,1024]{2,1,0:T(8,128)} %ls_hbm.1, f32[2]{0:T(128)S(1)} %copy-done, bf16[2,512,1024]{2,1,0:T(8,128)(2,1)} %constant.6.clone.wide_hbm, bf16[2,512,1024]{2,1,0:T(8,128)(2,1)} %constant.7.clone.mixed_hbm, bf16[2,1024,512]{2,1,0:T(8,128)(2,1)} %constant.8.clone.tall_hbm), custom_call_target="tpu_custom_call" | custom-call | tf_op jit(solution)/shard_map/pallas_call | solution.py:462
  49.4 0.6 %copy.7 = f32[16,128]{1,0:T(8,128)} copy(f32[16,128]{1,0:T(8,128)S(1)} %shard_map.55) | data formatting | bytes 16384
Async XLA Ops:
  0.0 0.7 %copy-start = (f32[2]{0:T(128)S(1)}, f32[2]{0:T(128)}, u32[]{:S(2)}) copy-start(f32[2]{0:T(128)} %con_hbm.1) | copy-start | bytes 28

commit v14 on v13

--- a/solution.py
+++ b/solution.py
@@ -102,7 +102,7 @@
 
 def kernel(
     ls_hbm, con_hbm, wide_hbm, mixed_hbm, tall_hbm, out_ref,
-    ls_ref, con_ref, own, part_density, wide, mixed, tall, zhalo, rsend, rhalo, csend, sbuf, rsp, acc, pst, xsend, cbuf, coefs, gsend, gbuf,
+    ls_ref, con_ref, part_density, wide, mixed, tall, zhalo, rsend, rhalo, csend, sbuf, rsp, acc, pst, xsend, cbuf, coefs, gsend, gbuf,
     ls_sem, con_sem, wide_sem, mixed_sem, tall_sem, hs, hr, cs, cr, xs, xr, gs, gr, news,
 ):
     d = lax.axis_index("depth")
@@ -168,23 +168,6 @@
     def hear(number, count):
         pl.semaphore_wait(news.at[number], count)
 
-    ls_copy.wait()
-    con_copy.wait()
-
-    for layer in range(2):
-        value = ls_ref[layer]
-        value = jnp.where(lower, flip(value, 0, ROWS), value)
-        own[layer, :, :HALF] = value[:, HALF:]
-        own[layer, :, HALF:] = flip_lanes(value[:, :HALF])
-
-    for layer in range(2):
-        for k in range(8):
-            spot = layer * 8 + k
-            top = own[layer, 0:1, 128 * k : 128 * (k + 1)]
-            bottom = own[layer, ROWS - 1 : ROWS, 128 * k : 128 * (k + 1)]
-            rsend[0, spot : spot + 1, :] = jnp.where(lower, bottom, top)
-            rsend[1, spot : spot + 1, :] = jnp.where(lower, top, bottom)
-
     pl.semaphore_wait(barrier, 9 + has_outer.astype(jnp.int32))
 
     def halo(source, target, number, device):
@@ -193,18 +176,28 @@
             device_id=device, device_id_type=MESH,
         )
 
-    z_up = halo(own.at[1], zhalo.at[0], 0, (d + 1, p))
-    z_down = halo(own.at[0], zhalo.at[1], 1, (d - 1, p))
+    z_up = halo(ls_hbm.at[1], zhalo.at[0], 0, (d + 1, p))
+    z_down = halo(ls_hbm.at[0], zhalo.at[1], 1, (d - 1, p))
     r_up = halo(rsend.at[1], rhalo.at[0], 2, (d, p + 1))
     r_down = halo(rsend.at[0], rhalo.at[1], 3, (d, p - 1))
     lands = (zhalo.at[0], zhalo.at[1], rhalo.at[0], rhalo.at[1])
     copies = (z_up, z_down, r_up, r_down)
-    for copy, there in zip(copies, has):
+    for copy, there in zip(copies[:2], has[:2]):
         pl.when(there)(copy.start)
     tell(0, y_line)
     tell(1, z_pair(1))
+    ls_copy.wait()
+    for layer in range(2):
+        for k in range(8):
+            spot = layer * 8 + k
+            lanes = slice(128 * k, 128 * (k + 1))
+            rsend[0, spot : spot + 1, :] = ls_ref[layer, 0:1, lanes]
+            rsend[1, spot : spot + 1, :] = ls_ref[layer, ROWS - 1 : ROWS, lanes]
+    for copy, there in zip(copies[2:], has[2:]):
+        pl.when(there)(copy.start)
     for copy in mixed_copies + tall_copies:
         copy.start()
+    con_copy.wait()
     for land, comes in zip(lands, gets):
 
         @pl.when(jnp.logical_not(comes))
@@ -212,24 +205,17 @@
             land[...] = jnp.zeros(land.shape, F32)
 
     row_id = lax.broadcasted_iota(jnp.int32, (ROWS, NX), 0)
-    lane_id = lax.broadcasted_iota(jnp.int32, (ROWS, HALF), 1)
-    field = [own[0], own[1]]
+    col_id = lax.broadcasted_iota(jnp.int32, (ROWS, NX), 1)
+    field = [ls_ref[0], ls_ref[1]]
     middle = flux(field[1] - field[0])
     for layer in range(2):
         centre = field[layer]
         bend = -middle if layer else middle
-        inner_flux = flux(pltpu.roll(centre, 1, 0) - centre)
-        bend = bend + jnp.where(row_id == 0, 0.0, inner_flux)
-        bend = bend - jnp.where(row_id == ROWS - 1, 0.0, pltpu.roll(inner_flux, ROWS - 1, 0))
-        sides = centre[:, :HALF], centre[:, HALF:]
-        across = []
-        for side in range(2):
-            here = sides[side]
-            inside = jnp.where(lane_id == 0, sides[1 - side], pltpu.roll(here, 1, 1))
-            inner_flux = flux(inside - here)
-            outside = jnp.where(lane_id == HALF - 1, flux(here), pltpu.roll(inner_flux, HALF - 1, 1))
-            across.append(inner_flux - outside)
-        bend = bend + jnp.concatenate(across, axis=1)
+        row_flux = flux(pltpu.roll(centre, 1, 0) - centre)
+        bend = bend + jnp.where(row_id == 0, 0.0, row_flux)
+        bend = bend - jnp.where(row_id == ROWS - 1, 0.0, pltpu.roll(row_flux, ROWS - 1, 0))
+        col_flux = flux(jnp.where(col_id == 0, 0.0, pltpu.roll(centre, 1, 1)) - centre)
+        bend = bend + col_flux - jnp.where(col_id == NX - 1, flux(centre), pltpu.roll(col_flux, NX - 1, 1))
         part_density[layer] = con_ref[layer] * (0.5 * (1.0 + jnp.tanh(centre))) + bend_weight * bend
 
     hear(0, 3)
@@ -255,18 +241,19 @@
         pl.when(comes)(copy.wait_recv)
     even, odd = [], []
     for layer in range(2):
-        centre = own[layer]
+        centre = ls_ref[layer]
         here = slice(layer * 8, layer * 8 + 8)
-        top = jnp.where(lower, rhalo[1, here, :], rhalo[0, here, :])
-        bottom = jnp.where(lower, rhalo[0, here, :], rhalo[1, here, :])
+        top, bottom = rhalo[0, here, :], rhalo[1, here, :]
         tops = [jnp.broadcast_to(top[k : k + 1], (ROWS, 128)) for k in range(8)]
         bottoms = [jnp.broadcast_to(bottom[k : k + 1], (ROWS, 128)) for k in range(8)]
         beside = jnp.where(row_id == 0, jnp.concatenate(tops, axis=1), jnp.concatenate(bottoms, axis=1))
         outer_rows = (row_id == 0) | (row_id == ROWS - 1)
         bend = flux(zhalo[layer] - centre) + jnp.where(outer_rows, flux(beside - centre), 0.0)
         density = part_density[layer] + bend_weight * bend
-        even.append(density[:, :HALF] + density[:, HALF:])
-        odd.append((density[:, :HALF] - density[:, HALF:]) * alternating((ROWS, HALF)))
+        density = jnp.where(lower, flip(density, 0, ROWS), density)
+        left, right = flip_lanes(density[:, :HALF]), density[:, HALF:]
+        even.append(right + left)
+        odd.append((right - left) * alternating((ROWS, HALF)))
 
     block = jnp.where(lower, PLAN // 2 - 1 - p, p - PLAN // 2)
     hear(2, 1)
@@ -468,7 +455,6 @@
                 pltpu.VMEM((2, ROWS, NX), F32),
                 pltpu.SMEM((2,), F32),
                 pltpu.VMEM((2, ROWS, NX), F32),
-                pltpu.VMEM((2, ROWS, NX), F32),
                 pltpu.VMEM((2, HALF, NX), BF16),
                 pltpu.VMEM((2, HALF, NX), BF16),
                 pltpu.VMEM((2, NX, HALF), BF16),

time: 50.2 us -> 50.8 us (1.012)
  Pallas kernels: 48.8 us -> 49.4 us
    pallas_call x1, Pallas kernels: 48.8 us -> 49.4 us  [step(): pl.pallas_call(kernel, out_shape=jax.ShapeDtypeStruct((ROWS, 128), F32),...]
where the time goes in v14:
time: 50.8 us; the launch traced here: 50.7 us
  Pallas kernels  49.4 us (97%)
  local copies, waits for them, and re-layouts  1.26 us (2%)
    pallas_call x1, Pallas kernels, step(): pl.pallas_call(kernel, out_shape=jax.ShapeDtypeStruct((ROWS, 128), F32),...  49.4 us
    unnamed x3, local copies, waits for them, and re-layouts  1.26 us

profile of v14, /device:TPU:1, one launch (start us, length us, event | category | flops | bytes accessed | tf_op | source)
XLA Modules:
  0.0 50.7 jit_solution(5450753785012226601)
XLA Ops:
  0.0 0.0 copy-start
  0.0 0.7 %copy-done = f32[2]{0:T(128)S(1)} copy-done((f32[2]{0:T(128)S(1)}, f32[2]{0:T(128)}, u32[]{:S(2)}) %copy-start) | copy-done | bytes 32
  0.7 49.4 %shard_map.55 = f32[16,128]{1,0:T(8,128)S(1)} custom-call(f32[2,16,1024]{2,1,0:T(8,128)} %ls_hbm.1, f32[2]{0:T(128)S(1)} %copy-done, bf16[2,512,1024]{2,1,0:T(8,128)(2,1)} %constant.6.clone.wide_hbm, bf16[2,512,1024]{2,1,0:T(8,128)(2,1)} %constant.7.clone.mixed_hbm, bf16[2,1024,512]{2,1,0:T(8,128)(2,1)} %constant.8.clone.tall_hbm), custom_call_target="tpu_custom_call" | custom-call | tf_op jit(solution)/shard_map/pallas_call | solution.py:449
  50.1 0.6 %copy.7 = f32[16,128]{1,0:T(8,128)} copy(f32[16,128]{1,0:T(8,128)S(1)} %shard_map.55) | data formatting | bytes 16384
Async XLA Ops:
  0.0 0.7 %copy-start = (f32[2]{0:T(128)S(1)}, f32[2]{0:T(128)}, u32[]{:S(2)}) copy-start(f32[2]{0:T(128)} %con_hbm.1) | copy-start | bytes 28

commit v15 on v12

--- a/solution.py
+++ b/solution.py
@@ -117,6 +117,8 @@
     kind_own, cut_own = lax.div(y, 2), lax.rem(x + y, 2)
     set_own = 2 * kind_own + cut_own
     coef_block = 8 * set_own + 2 * x + core
+    parity = lax.rem(d, 2)
+    mate = d + 1 - 2 * parity
     order = (2, 6, 4, 3, 7, 5, 1, 0)
     turns = [lax.rem(2 * x + core + k, 8) for k in order]
     places = [
@@ -127,6 +129,23 @@
     def at_z(other):
         return (lax.rem(other, DEPTH), p + 2 * (lax.div(other, DEPTH) - zh))
 
+    barrier = pltpu.get_barrier_semaphore()
+
+    def greet(target):
+        pl.semaphore_signal(barrier, inc=1, device_id=target, device_id_type=MESH)
+
+    has = (d < DEPTH - 1, d > 0, p < PLAN - 1, p > 0)
+    gets = (d > 0, d < DEPTH - 1, p > 0, p < PLAN - 1)
+    outer = jnp.where(core == 0, p - 1, p + 1)
+    has_outer = (outer >= 0) & (outer < PLAN)
+    x_line = [(d, p + 16 * (lax.rem(x + k, 4) - x)) for k in (1, 3, 2)]
+    y_line = [(d, p + 4 * (lax.rem(y + k, 4) - y)) for k in (1, 3, 2)]
+    buddy = (d, p + 1 - 2 * core)
+
+    def z_pair(k):
+        return [at_z(lax.rem(z + away, RING)) for away in (k, RING - k)]
+
+    pl.when(has_outer)(lambda: greet((d, outer)))
     ls_copy = pltpu.make_async_copy(ls_hbm, ls_ref, ls_sem)
     con_copy = pltpu.make_async_copy(con_hbm, con_ref, con_sem)
     ls_copy.start()
@@ -136,27 +155,7 @@
     tall_copies = [pltpu.make_async_copy(tall_hbm.at[n], tall.at[n], tall_sem.at[n]) for n in range(2)]
     for copy in wide_copies:
         copy.start()
-
-    barrier = pltpu.get_barrier_semaphore()
-
-    def greet(target):
-        pl.semaphore_signal(barrier, inc=1, device_id=target, device_id_type=MESH)
-
-    has = (d < DEPTH - 1, d > 0, p < PLAN - 1, p > 0)
-    gets = (d > 0, d < DEPTH - 1, p > 0, p < PLAN - 1)
-    outer = jnp.where(core == 0, p - 1, p + 1)
-    has_outer = (outer >= 0) & (outer < PLAN)
-    x_line = [(d, p + 16 * (lax.rem(x + k, 4) - x)) for k in (1, 3, 2)]
-    y_line = [(d, p + 4 * (lax.rem(y + k, 4) - y)) for k in (1, 3, 2)]
-    buddy = (d, p + 1 - 2 * core)
-
-    def z_pair(k):
-        return [at_z(lax.rem(z + away, RING)) for away in (k, RING - k)]
-
-    for target in z_pair(1) + [buddy]:
-        greet(target)
-    pl.when(has_outer)(lambda: greet((d, outer)))
-    for target in x_line + y_line:
+    for target in z_pair(1) + [buddy] + x_line + y_line:
         greet(target)
 
     def tell(number, targets):
@@ -165,23 +164,6 @@
 
     def hear(number, count):
         pl.semaphore_wait(news.at[number], count)
-
-    ls_copy.wait()
-    con_copy.wait()
-
-    for layer in range(2):
-        value = ls_ref[layer]
-        value = jnp.where(lower, flip(value, 0, ROWS), value)
-        own[layer, :, :HALF] = value[:, HALF:]
-        own[layer, :, HALF:] = flip_lanes(value[:, :HALF])
-
-    for layer in range(2):
-        for k in range(8):
-            spot = layer * 8 + k
-            top = own[layer, 0:1, 128 * k : 128 * (k + 1)]
-            bottom = own[layer, ROWS - 1 : ROWS, 128 * k : 128 * (k + 1)]
-            rsend[0, spot : spot + 1, :] = jnp.where(lower, bottom, top)
-            rsend[1, spot : spot + 1, :] = jnp.where(lower, top, bottom)
 
     pl.semaphore_wait(barrier, 9 + has_outer.astype(jnp.int32))
 
@@ -191,18 +173,42 @@
             device_id=device, device_id_type=MESH,
         )
 
-    z_up = halo(own.at[1], zhalo.at[0], 0, (d + 1, p))
-    z_down = halo(own.at[0], zhalo.at[1], 1, (d - 1, p))
+    z_up = halo(ls_hbm.at[1], zhalo.at[0], 0, (d + 1, p))
+    z_down = halo(ls_hbm.at[0], zhalo.at[1], 1, (d - 1, p))
     r_up = halo(rsend.at[1], rhalo.at[0], 2, (d, p + 1))
     r_down = halo(rsend.at[0], rhalo.at[1], 3, (d, p - 1))
     lands = (zhalo.at[0], zhalo.at[1], rhalo.at[0], rhalo.at[1])
     copies = (z_up, z_down, r_up, r_down)
-    for copy, there in zip(copies, has):
+    for copy, there in zip(copies[:2], has[:2]):
+        pl.when(there)(copy.start)
+    ls_copy.wait()
+
+    for layer in range(2):
+        for k in range(8):
+            spot = layer * 8 + k
+            block = 4 + k if k < 4 else 7 - k
+            lanes = slice(128 * block, 128 * (block + 1))
+            rsend[0, spot : spot + 1, :] = ls_ref[layer, 0:1, lanes]
+            rsend[1, spot : spot + 1, :] = ls_ref[layer, ROWS - 1 : ROWS, lanes]
+    turned = lax.rem(lax.broadcasted_iota(jnp.int32, (16, 128), 0), 8) >= 4
+    for side in range(2):
+        rsend[side] = jnp.where(turned, flip(rsend[side], 1, 128), rsend[side])
+
+    for copy, there in zip(copies[2:], has[2:]):
         pl.when(there)(copy.start)
     tell(0, y_line)
     tell(1, z_pair(1))
     for copy in mixed_copies + tall_copies:
         copy.start()
+
+    def fold(value):
+        value = jnp.where(lower, flip(value, 0, ROWS), value)
+        return jnp.concatenate([value[:, HALF:], flip_lanes(value[:, :HALF])], axis=1)
+
+    for layer in range(2):
+        own[layer] = fold(ls_ref[layer])
+    con_copy.wait()
+
     for land, comes in zip(lands, gets):
 
         @pl.when(jnp.logical_not(comes))
@@ -233,8 +239,11 @@
     hear(0, 3)
     tell(2, [buddy])
 
-    for copy, comes in zip(copies, gets):
-        pl.when(comes)(copy.wait_recv)
+    for layer in range(2):
+        pl.when(gets[layer])(copies[layer].wait_recv)
+        part_density[layer] += bend_weight * flux(fold(zhalo[layer]) - own[layer])
+    for number in (2, 3):
+        pl.when(gets[number])(copies[number].wait_recv)
     even, odd = [], []
     for layer in range(2):
         centre = own[layer]
@@ -245,14 +254,11 @@
         bottoms = [jnp.broadcast_to(bottom[k : k + 1], (ROWS, 128)) for k in range(8)]
         beside = jnp.where(row_id == 0, jnp.concatenate(tops, axis=1), jnp.concatenate(bottoms, axis=1))
         outer_rows = (row_id == 0) | (row_id == ROWS - 1)
-        bend = flux(zhalo[layer] - centre) + jnp.where(outer_rows, flux(beside - centre), 0.0)
-        density = part_density[layer] + bend_weight * bend
+        density = part_density[layer] + jnp.where(outer_rows, bend_weight * flux(beside - centre), 0.0)
         even.append(density[:, :HALF] + density[:, HALF:])
         odd.append((density[:, :HALF] - density[:, HALF:]) * alternating((ROWS, HALF)))
 
     block = jnp.where(lower, PLAN // 2 - 1 - p, p - PLAN // 2)
-    parity = lax.rem(d, 2)
-    mate = d + 1 - 2 * parity
     hear(2, 1)
     hear(1, 2)
     tell(3, [(mate, p)])
@@ -489,7 +495,7 @@
                 dma(()), dma((2,)), dma(()), dma(()), dma(()), dma(()), pltpu.SemaphoreType.REGULAR((6,)),
             ],
             compiler_params=pltpu.CompilerParams(
-                collective_id=0, has_side_effects=True, vmem_limit_bytes=63 * 1024 * 1024
+                collective_id=0, has_side_effects=True, vmem_limit_bytes=55176 * 1024
             ),
         )(level_set, contrast, jnp.asarray(wide), jnp.asarray(mixed), jnp.asarray(tall))
 

time: 50.6 us -> 50.5 us (level)
    unnamed x1 -> x3, local copies, waits for them, and re-layouts: 1.3 us -> 1.26 us
where the time goes in v15:
time: 50.5 us; the launch traced here: 50.4 us
  Pallas kernels  49.2 us (97%)
  local copies, waits for them, and re-layouts  1.26 us (2%)
    pallas_call x1, Pallas kernels, step(): pl.pallas_call(kernel, out_shape=jax.ShapeDtypeStruct((ROWS, 128), F32),...  49.2 us
    unnamed x3, local copies, waits for them, and re-layouts  1.26 us

profile of v15, /device:TPU:1, one launch (start us, length us, event | category | flops | bytes accessed | tf_op | source)
XLA Modules:
  0.0 50.4 jit_solution(9724633261352873064)
XLA Ops:
  0.0 0.0 copy-start
  0.0 0.7 %copy-done = f32[2]{0:T(128)S(1)} copy-done((f32[2]{0:T(128)S(1)}, f32[2]{0:T(128)}, u32[]{:S(2)}) %copy-start) | copy-done | bytes 32
  0.7 49.2 %shard_map.55 = f32[16,128]{1,0:T(8,128)S(1)} custom-call(f32[2,16,1024]{2,1,0:T(8,128)} %ls_hbm.1, f32[2]{0:T(128)S(1)} %copy-done, bf16[2,512,1024]{2,1,0:T(8,128)(2,1)} %constant.6.clone.wide_hbm, bf16[2,512,1024]{2,1,0:T(8,128)(2,1)} %constant.7.clone.mixed_hbm, bf16[2,1024,512]{2,1,0:T(8,128)(2,1)} %constant.8.clone.tall_hbm), custom_call_target="tpu_custom_call" | custom-call | tf_op jit(solution)/shard_map/pallas_call | solution.py:468
  49.8 0.6 %copy.7 = f32[16,128]{1,0:T(8,128)} copy(f32[16,128]{1,0:T(8,128)S(1)} %shard_map.55) | data formatting | bytes 16384
Async XLA Ops:
  0.0 0.7 %copy-start = (f32[2]{0:T(128)S(1)}, f32[2]{0:T(128)}, u32[]{:S(2)}) copy-start(f32[2]{0:T(128)} %con_hbm.1) | copy-start | bytes 28

commit v16 on v13

--- a/solution.py
+++ b/solution.py
@@ -235,24 +235,32 @@
     hear(0, 3)
     tell(2, [buddy])
 
-    def respond(start, cross):
-        row = lax.broadcasted_iota(jnp.int32, (128, 128), 0)
-        col = lax.broadcasted_iota(jnp.int32, (128, 128), 1) + start
+    def respond(start):
+        row = lax.broadcasted_iota(jnp.int32, (64, 128), 0)
+        col = lax.broadcasted_iota(jnp.int32, (64, 128), 1) + start
         place = lax.rem(coef_block, GROUP // 2) * COEF + parity * SHARE + lax.rem(row, SHARE)
         v = jnp.where(kind_own == 1, NX - place, place).astype(F32)
+        u = jnp.where(row >= SHARE, NX - col, col).astype(F32)
         scale = 2.0 * math.pi * grav_scale * thickness / (4.0 * NX * NX)
         weight = jnp.where(place == 0, scale, 2.0 * scale) * jnp.where(col == 0, 1.0, 2.0)
-        layer = (2 * (mate if cross else d) + lax.rem(lax.div(row, SHARE), 2)).astype(F32)
-        rate = (top_depth + (layer + 0.5) * thickness) * (-2.0 * math.pi / (2 * NX))
-        u = jnp.where(row >= 64, NX - col, col).astype(F32)
-        return jnp.exp(jnp.sqrt(u * u + v * v) * rate) * weight
-
-    for cross in range(2):
-        for k in range(NX // 128):
-            rsp[cross, :, 128 * k : 128 * (k + 1)] = respond(128 * k, cross)
-
-    for copy, comes in zip(copies, gets):
-        pl.when(comes)(copy.wait_recv)
+        kappa = jnp.sqrt(u * u + v * v) * (2.0 * math.pi / (2 * NX))
+        next_layer = jnp.exp(-thickness * kappa)
+        for cross, depth in enumerate((d, mate)):
+            top = top_depth + (2.0 * depth.astype(F32) + 0.5) * thickness
+            first = jnp.exp(-top * kappa) * weight
+            second = first * next_layer
+            for n, value in enumerate((first[:SHARE], second[:SHARE], first[SHARE:], second[SHARE:])):
+                rsp[cross, SHARE * n : SHARE * (n + 1), start : start + 128] = value
+
+    for k in range(NX // 128):
+        respond(128 * k)
+
+    for layer in range(2):
+        pl.when(gets[layer])(copies[layer].wait_recv)
+    for layer in range(2):
+        part_density[layer] += bend_weight * flux(zhalo[layer] - own[layer])
+    for number in (2, 3):
+        pl.when(gets[number])(copies[number].wait_recv)
     even, odd = [], []
     for layer in range(2):
         centre = own[layer]
@@ -263,8 +271,7 @@
         bottoms = [jnp.broadcast_to(bottom[k : k + 1], (ROWS, 128)) for k in range(8)]
         beside = jnp.where(row_id == 0, jnp.concatenate(tops, axis=1), jnp.concatenate(bottoms, axis=1))
         outer_rows = (row_id == 0) | (row_id == ROWS - 1)
-        bend = flux(zhalo[layer] - centre) + jnp.where(outer_rows, flux(beside - centre), 0.0)
-        density = part_density[layer] + bend_weight * bend
+        density = part_density[layer] + jnp.where(outer_rows, bend_weight * flux(beside - centre), 0.0)
         even.append(density[:, :HALF] + density[:, HALF:])
         odd.append((density[:, :HALF] - density[:, HALF:]) * alternating((ROWS, HALF)))
 

time: 50.2 us -> 50.1 us (level)
  no operation moved by 1% of the time
where the time goes in v16:
time: 50.1 us; the launch traced here: 50 us
  Pallas kernels  48.7 us (97%)
  local copies, waits for them, and re-layouts  1.26 us (3%)
    pallas_call x1, Pallas kernels, step(): pl.pallas_call(kernel, out_shape=jax.ShapeDtypeStruct((ROWS, 128), F32),...  48.7 us
    unnamed x3, local copies, waits for them, and re-layouts  1.26 us

profile of v16, /device:TPU:1, one launch (start us, length us, event | category | flops | bytes accessed | tf_op | source)
XLA Modules:
  0.0 50.0 jit_solution(12536120292224027819)
XLA Ops:
  0.0 0.0 copy-start
  0.0 0.7 %copy-done = f32[2]{0:T(128)S(1)} copy-done((f32[2]{0:T(128)S(1)}, f32[2]{0:T(128)}, u32[]{:S(2)}) %copy-start) | copy-done | bytes 32
  0.7 48.7 %shard_map.55 = f32[16,128]{1,0:T(8,128)S(1)} custom-call(f32[2,16,1024]{2,1,0:T(8,128)} %ls_hbm.1, f32[2]{0:T(128)S(1)} %copy-done, bf16[2,512,1024]{2,1,0:T(8,128)(2,1)} %constant.6.clone.wide_hbm, bf16[2,512,1024]{2,1,0:T(8,128)(2,1)} %constant.7.clone.mixed_hbm, bf16[2,1024,512]{2,1,0:T(8,128)(2,1)} %constant.8.clone.tall_hbm), custom_call_target="tpu_custom_call" | custom-call | tf_op jit(solution)/shard_map/pallas_call | solution.py:469
  49.4 0.6 %copy.7 = f32[16,128]{1,0:T(8,128)} copy(f32[16,128]{1,0:T(8,128)S(1)} %shard_map.55) | data formatting | bytes 16384
Async XLA Ops:
  0.0 0.7 %copy-start = (f32[2]{0:T(128)S(1)}, f32[2]{0:T(128)}, u32[]{:S(2)}) copy-start(f32[2]{0:T(128)} %con_hbm.1) | copy-start | bytes 28

commit v17 on v16

--- a/solution.py
+++ b/solution.py
@@ -255,6 +255,9 @@
     for k in range(NX // 128):
         respond(128 * k)
 
+    hear(2, 1)
+    hear(1, 2)
+    tell(3, [(mate, p)])
     for layer in range(2):
         pl.when(gets[layer])(copies[layer].wait_recv)
     for layer in range(2):
@@ -276,9 +279,8 @@
         odd.append((density[:, :HALF] - density[:, HALF:]) * alternating((ROWS, HALF)))
 
     block = jnp.where(lower, PLAN // 2 - 1 - p, p - PLAN // 2)
-    hear(2, 1)
-    hear(1, 2)
-    tell(3, [(mate, p)])
+    hear(3, 1)
+    tell(4, z_pair(2))
     for copy in wide_copies:
         copy.wait()
 
@@ -306,8 +308,6 @@
                 send_coef(2 * kind + cut, k, 0).start()
     for group in range(4):
         pl.when(group != set_own)(send_coef(group, 7, 0).start)
-    hear(3, 1)
-    tell(4, z_pair(2))
     for k in range(8):
         for group in range(4):
             send_coef(group, k, 1).start()

time: 50.1 us -> 50.2 us (level)
  no operation moved by 1% of the time
where the time goes in v17:
time: 50.2 us; the launch traced here: 50 us
  Pallas kernels  48.8 us (97%)
  local copies, waits for them, and re-layouts  1.26 us (3%)
    pallas_call x1, Pallas kernels, step(): pl.pallas_call(kernel, out_shape=jax.ShapeDtypeStruct((ROWS, 128), F32),...  48.8 us
    unnamed x3, local copies, waits for them, and re-layouts  1.26 us

profile of v17, /device:TPU:1, one launch (start us, length us, event | category | flops | bytes accessed | tf_op | source)
XLA Modules:
  0.0 50.0 jit_solution(12826747110348607038)
XLA Ops:
  0.0 0.0 copy-start
  0.0 0.7 %copy-done = f32[2]{0:T(128)S(1)} copy-done((f32[2]{0:T(128)S(1)}, f32[2]{0:T(128)}, u32[]{:S(2)}) %copy-start) | copy-done | bytes 32
  0.7 48.8 %shard_map.55 = f32[16,128]{1,0:T(8,128)S(1)} custom-call(f32[2,16,1024]{2,1,0:T(8,128)} %ls_hbm.1, f32[2]{0:T(128)S(1)} %copy-done, bf16[2,512,1024]{2,1,0:T(8,128)(2,1)} %constant.6.clone.wide_hbm, bf16[2,512,1024]{2,1,0:T(8,128)(2,1)} %constant.7.clone.mixed_hbm, bf16[2,1024,512]{2,1,0:T(8,128)(2,1)} %constant.8.clone.tall_hbm), custom_call_target="tpu_custom_call" | custom-call | tf_op jit(solution)/shard_map/pallas_call | solution.py:469
  49.4 0.6 %copy.7 = f32[16,128]{1,0:T(8,128)} copy(f32[16,128]{1,0:T(8,128)S(1)} %shard_map.55) | data formatting | bytes 16384
Async XLA Ops:
  0.0 0.7 %copy-start = (f32[2]{0:T(128)S(1)}, f32[2]{0:T(128)}, u32[]{:S(2)}) copy-start(f32[2]{0:T(128)} %con_hbm.1) | copy-start | bytes 28

commit v18 on v16

--- a/solution.py
+++ b/solution.py
@@ -102,7 +102,7 @@
 
 def kernel(
     ls_hbm, con_hbm, wide_hbm, mixed_hbm, tall_hbm, out_ref,
-    ls_ref, con_ref, own, part_density, wide, mixed, tall, zhalo, rsend, rhalo, csend, sbuf, rsp, acc, pst, xsend, cbuf, coefs, gsend, gbuf,
+    ls_ref, con_ref, own, part_density, wide, mixed, tall, zhalo, rsend, rhalo, csend, sbuf, rsp, pst, xsend, cbuf, coefs, gsend, gbuf,
     ls_sem, con_sem, wide_sem, mixed_sem, tall_sem, hs, hr, cs, cr, xs, xr, gs, gr, news,
 ):
     d = lax.axis_index("depth")
@@ -320,21 +320,22 @@
     side = lax.rem(lax.div(lax.broadcasted_iota(jnp.int32, (64, HALF), 1), 16), 2)
     sign = jnp.where(side == zh, 1.0, -1.0) * alternating((64, HALF))
     step = 256
+    values = []
     for cross in range(2):
         landed = sbuf.at[pl.ds(GROUP * cross, GROUP - 1 + cross)]
         pltpu.make_async_copy(landed, landed, cr.at[cross]).wait()
         value = sbuf[GROUP * cross : GROUP * (cross + 1)].reshape(HALF // 2, 128).T
         value = jnp.concatenate([value[:64], value[64:]], axis=1)
-        both = pair(jnp.concatenate([value, value * sign], axis=0))
-        for k in range(NX // step):
-            here = slice(k * step, (k + 1) * step)
-            coef = table_right(both, mixed[0, :, here], mixed[1, :, here]) * rsp[cross, :, here]
-            parts = [coef[SHARE * n : SHARE * (n + 1)] for n in range(4)]
-            coef = jnp.concatenate([parts[0] + parts[1], parts[2] + parts[3]], axis=0)
-            if cross:
-                pst[:, here] = pair(coef + acc[:, here])
-            else:
-                acc[:, here] = coef
+        values += [value, value * sign]
+    both = pair(jnp.concatenate(values, axis=0))
+    for k in range(NX // step):
+        here = slice(k * step, (k + 1) * step)
+        coef = table_right(both, mixed[0, :, here], mixed[1, :, here])
+        coef = coef * jnp.concatenate([rsp[0, :, here], rsp[1, :, here]], axis=0)
+        parts = [coef[SHARE * n : SHARE * (n + 1)] for n in range(8)]
+        cosine = (parts[0] + parts[1]) + (parts[4] + parts[5])
+        sine = (parts[2] + parts[3]) + (parts[6] + parts[7])
+        pst[:, here] = pair(jnp.concatenate([cosine, sine], axis=0))
 
     low = 2 * lax.rem(y, 2) + core
     x_turns = [lax.rem(x + k, 4) for k in range(4)]
@@ -485,7 +486,6 @@
                 pltpu.VMEM((2 * GROUP, 8, 128), F32),
                 pltpu.VMEM((2 * GROUP, 8, 128), F32),
                 pltpu.VMEM((2, 128, NX), F32),
-                pltpu.VMEM((64, NX), F32),
                 pltpu.VMEM((128, NX), BF16),
                 pltpu.VMEM((2 * GROUP, 4, 128), F32),
                 pltpu.VMEM((2 * GROUP, 4, 128), F32),

time: 50.1 us -> 50.5 us (level)
  no operation moved by 1% of the time
where the time goes in v18:
time: 50.5 us; the launch traced here: 50.4 us
  Pallas kernels  49.1 us (97%)
  local copies, waits for them, and re-layouts  1.26 us (2%)
    pallas_call x1, Pallas kernels, step(): pl.pallas_call(kernel, out_shape=jax.ShapeDtypeStruct((ROWS, 128), F32),...  49.1 us
    unnamed x3, local copies, waits for them, and re-layouts  1.26 us

profile of v18, /device:TPU:1, one launch (start us, length us, event | category | flops | bytes accessed | tf_op | source)
XLA Modules:
  0.0 50.4 jit_solution(1865583204917080554)
XLA Ops:
  0.0 0.0 copy-start
  0.0 0.7 %copy-done = f32[2]{0:T(128)S(1)} copy-done((f32[2]{0:T(128)S(1)}, f32[2]{0:T(128)}, u32[]{:S(2)}) %copy-start) | copy-done | bytes 32
  0.7 49.1 %shard_map.55 = f32[16,128]{1,0:T(8,128)S(1)} custom-call(f32[2,16,1024]{2,1,0:T(8,128)} %ls_hbm.1, f32[2]{0:T(128)S(1)} %copy-done, bf16[2,512,1024]{2,1,0:T(8,128)(2,1)} %constant.6.clone.wide_hbm, bf16[2,512,1024]{2,1,0:T(8,128)(2,1)} %constant.7.clone.mixed_hbm, bf16[2,1024,512]{2,1,0:T(8,128)(2,1)} %constant.8.clone.tall_hbm), custom_call_target="tpu_custom_call" | custom-call | tf_op jit(solution)/shard_map/pallas_call | solution.py:470
  49.8 0.6 %copy.7 = f32[16,128]{1,0:T(8,128)} copy(f32[16,128]{1,0:T(8,128)S(1)} %shard_map.55) | data formatting | bytes 16384
Async XLA Ops:
  0.0 0.7 %copy-start = (f32[2]{0:T(128)S(1)}, f32[2]{0:T(128)}, u32[]{:S(2)}) copy-start(f32[2]{0:T(128)} %con_hbm.1) | copy-start | bytes 28

commit v19 on v17

--- a/solution.py
+++ b/solution.py
@@ -306,11 +306,11 @@
         for k in range(7):
             for kind in range(2):
                 send_coef(2 * kind + cut, k, 0).start()
+        for k in range(8):
+            for kind in range(2):
+                send_coef(2 * kind + cut, k, 1).start()
     for group in range(4):
         pl.when(group != set_own)(send_coef(group, 7, 0).start)
-    for k in range(8):
-        for group in range(4):
-            send_coef(group, k, 1).start()
 
     hear(4, 2)
     tell(5, z_pair(4))

time: 50.2 us -> 50.2 us (level)
  no operation moved by 1% of the time
where the time goes in v19:
time: 50.2 us; the launch traced here: 50.1 us
  Pallas kernels  48.8 us (97%)
  local copies, waits for them, and re-layouts  1.26 us (3%)
    pallas_call x1, Pallas kernels, step(): pl.pallas_call(kernel, out_shape=jax.ShapeDtypeStruct((ROWS, 128), F32),...  48.8 us
    unnamed x3, local copies, waits for them, and re-layouts  1.26 us

profile of v19, /device:TPU:1, one launch (start us, length us, event | category | flops | bytes accessed | tf_op | source)
XLA Modules:
  0.0 50.1 jit_solution(12595349994939964300)
XLA Ops:
  0.0 0.0 copy-start
  0.0 0.7 %copy-done = f32[2]{0:T(128)S(1)} copy-done((f32[2]{0:T(128)S(1)}, f32[2]{0:T(128)}, u32[]{:S(2)}) %copy-start) | copy-done | bytes 32
  0.7 48.8 %shard_map.55 = f32[16,128]{1,0:T(8,128)S(1)} custom-call(f32[2,16,1024]{2,1,0:T(8,128)} %ls_hbm.1, f32[2]{0:T(128)S(1)} %copy-done, bf16[2,512,1024]{2,1,0:T(8,128)(2,1)} %constant.6.clone.wide_hbm, bf16[2,512,1024]{2,1,0:T(8,128)(2,1)} %constant.7.clone.mixed_hbm, bf16[2,1024,512]{2,1,0:T(8,128)(2,1)} %constant.8.clone.tall_hbm), custom_call_target="tpu_custom_call" | custom-call | tf_op jit(solution)/shard_map/pallas_call | solution.py:469
  49.5 0.6 %copy.7 = f32[16,128]{1,0:T(8,128)} copy(f32[16,128]{1,0:T(8,128)S(1)} %shard_map.55) | data formatting | bytes 16384
Async XLA Ops:
  0.0 0.7 %copy-start = (f32[2]{0:T(128)S(1)}, f32[2]{0:T(128)}, u32[]{:S(2)}) copy-start(f32[2]{0:T(128)} %con_hbm.1) | copy-start | bytes 28
